TPU v7x, 32 devices: a whole 2x2x4 slice. The times are simulated.
32 devices in a mesh: dp: 4 (over z), expert: 8 (over y, x, core).
Axes of the slice: x: 2, y: 2, z: 4, core: 2. Of those that a mesh axis runs over, the one named last changes fastest.
Arguments:
- tokens: bfloat16 [2, 8, 1024, 1536], P(None, 'expert', 'dp'), may hold values from -6 to 6
- cotangent: bfloat16 [2, 8, 1024, 1536], P(None, 'expert', 'dp'), may hold values from -6 to 6
- parents: int32 [2, 8, 8], P(None, 'expert'), may hold values from 0 to 6, as said below
- valid_mask: int32 [2, 8, 1024], P(None, 'expert'), may hold values 0 or 1
- routes: int32 [2, 8, 1024, 8], P(None, 'expert', 'dp'), may hold values from 0 to 15, all different within a row; in each aligned block of 256 rows (0 to 255, 256 to 511, ..., all dimensions but the last counted through in order) at most 192 rows name the same one
- route_gates: float32 [2, 8, 1024, 8], P(None, 'expert', 'dp'), may hold values from 0.06 to 0.19
- norm_gains: bfloat16 [2, 1536], P(None, ('dp', 'expert')), may hold values from 0.5 to 1.5
- w_qkv: bfloat16 [1536, 2560], P(('dp', 'expert')), may hold values from -0.15625 to 0.15625
- w_out: bfloat16 [1536, 1536], P(None, ('dp', 'expert')), may hold values from -1.25 to 1.25
- w_gate_up: bfloat16 [16, 1536, 1024], P('expert', 'dp'), may hold values from -0.15625 to 0.15625
- w_down: bfloat16 [16, 512, 1536], P('expert', 'dp'), may hold values from -1 to 1
Outputs:
- layer_out: bfloat16 [2, 8, 1024, 1536], P(None, 'expert', 'dp')
- grad_tokens: bfloat16 [2, 8, 1024, 1536], P(None, 'expert', 'dp')
- grad_norm_gains: float32 [2, 1536], P(None, ('dp', 'expert'))
- grad_w_qkv: float32 [1536, 2560], P(('dp', 'expert'))
- grad_w_out: float32 [1536, 1536], P(None, ('dp', 'expert'))
- grad_w_gate_up: float32 [16, 1536, 1024], P('expert', 'dp')
- grad_w_down: float32 [16, 512, 1536], P('expert', 'dp')
Inputs may be any that keep to these rules, and one draw needn't show every extreme that they name: `parents`: segments 1 to 2 form a chain (each segment's parent is the one before it) and segment 0 is its own parent; every later segment b has a parent from 2 to b - 1, so every segment's path reaches segment 0. `routes`: in each aligned block of 256 rows (the tokens of one tree on one device in one micro-batch) no expert is named by more than 192 rows, a bound that some block reaches.
All inputs are finite; a program needn't handle non-finite values. No bound on the sum of `valid_mask` on one device may be relied on, other than what follows from the above.
Results may differ from a plain program's by a relative error of at most 0.015.
Values may be sent and summed in bfloat16 or wider, within the bound.
No kernel may reach another device: no remote copies, remote signals or barrier semaphores. Data moves between devices by JAX's collectives and lax.ppermute only.
A program may use at most 384 MiB of HBM per device.

v0:
```python
import jax
import jax.numpy as jnp
from jax import lax
from jax.sharding import PartitionSpec as P

H = 24
KV = 8
HD = 64
FFE = 512
BLOCK = 128


EPSILON = 1e-06
NEGATIVE = -1e30


def rms_norm(values_in, gain):
    return (
        values_in
        * lax.rsqrt(jnp.mean(values_in * values_in, axis=-1, keepdims=True) + EPSILON)
        * gain
    )


def ancestry(parents_in):
    count = parents_in.shape[-1]
    labels = jnp.arange(count, dtype=jnp.int32)
    start = jnp.broadcast_to(labels, parents_in.shape)
    reach_first = (start[..., :, None] == labels).astype(jnp.int32)

    def extend(step_num, carry):
        current, reach = carry
        current = jnp.take_along_axis(parents_in, current, axis=-1)
        reach = jnp.maximum(reach, (current[..., :, None] == labels).astype(jnp.int32))
        return (current, reach)

    return lax.fori_loop(0, count, extend, (start, reach_first))[1]


def allowed_pairs(block_rows, valid_in, first_row):
    token_table = jnp.repeat(jnp.repeat(block_rows, BLOCK, axis=1), BLOCK, axis=2)
    query_pos = first_row + jnp.arange(token_table.shape[1], dtype=jnp.int32)
    key_pos = jnp.arange(token_table.shape[2], dtype=jnp.int32)
    causal = key_pos[None, :] <= query_pos[:, None]
    itself = key_pos[None, :] == query_pos[:, None]
    return (token_table > 0) & causal[None] & ((valid_in[:, None, :] > 0) | itself[None])


def slot_positions(routes_flat, expert_count):
    labels = jnp.arange(expert_count, dtype=jnp.int32)
    hits = (routes_flat[..., None] == labels).astype(jnp.int32)
    before = jnp.cumsum(hits, axis=-2) - hits
    return jnp.sum(before * hits, axis=-1)


def attention_scores(queries, keys_all, allowed, score_scale):
    scores = (
        jnp.einsum("mqkgd,mtkd->mkgqt", queries, keys_all, preferred_element_type=jnp.float32)
        * score_scale
    )
    return jnp.where(allowed[:, None, None], scores, NEGATIVE)


def body(
    tokens,
    cotangent,
    parents,
    valid_mask,
    routes,
    route_gates,
    norm_gains,
    w_qkv,
    w_out,
    w_gate_up,
    w_down,
):
    micro_count, _, row_count, model_width = tokens.shape
    top_count = routes.shape[-1]
    group_size = H // KV
    query_width = H * HD
    kv_width = KV * HD
    score_scale = HD ** (-0.5)
    gains, qkv_weight, out_weight = (
        lax.all_gather(norm_gains, ("dp", "expert"), axis=1, tiled=True),
        lax.all_gather(w_qkv, ("dp", "expert"), axis=0, tiled=True),
        lax.all_gather(w_out, ("dp", "expert"), axis=1, tiled=True),
    )
    gate_up_weight, down_weight = (
        lax.all_gather(w_gate_up, "dp", axis=1, tiled=True),
        lax.all_gather(w_down, "dp", axis=1, tiled=True),
    )
    x_in = tokens.reshape(micro_count, row_count, model_width).astype(jnp.float32)
    gain_in = gains[0].astype(jnp.float32)
    gain_mid = gains[1].astype(jnp.float32)
    h_in = rms_norm(x_in, gain_in).astype(jnp.bfloat16)
    h_flat = h_in.reshape(micro_count * row_count, model_width)
    qkv = jnp.dot(h_flat, qkv_weight, preferred_element_type=jnp.float32).astype(jnp.bfloat16)
    qkv = qkv.reshape(micro_count, row_count, -1)
    queries = qkv[..., :query_width].reshape(micro_count, row_count, KV, group_size, HD)
    keys_local = qkv[..., query_width : query_width + kv_width].reshape(
        micro_count, row_count, KV, HD
    )
    values_local = qkv[..., query_width + kv_width :].reshape(micro_count, row_count, KV, HD)
    keys_all, values_all = (
        lax.all_gather(keys_local, "dp", axis=1, tiled=True),
        lax.all_gather(values_local, "dp", axis=1, tiled=True),
    )
    dp_index = lax.axis_index("dp")
    ancestors = ancestry(parents.reshape(micro_count, -1))
    blocks_dev = row_count // BLOCK
    local_blocks = lax.dynamic_slice_in_dim(ancestors, dp_index * blocks_dev, blocks_dev, 1)
    allowed = allowed_pairs(local_blocks, valid_mask.reshape(micro_count, -1), dp_index * row_count)
    scores = attention_scores(queries, keys_all, allowed, score_scale)
    score_peak = jnp.max(scores, axis=-1, keepdims=True)
    score_exp = jnp.exp(scores - score_peak)
    score_total = jnp.sum(score_exp, axis=-1, keepdims=True)
    attn_probs = score_exp / score_total
    log_total = score_peak + jnp.log(score_total)
    attn_mixed = jnp.einsum(
        "mkgqt,mtkd->mqkgd",
        attn_probs.astype(jnp.bfloat16),
        values_all,
        preferred_element_type=jnp.float32,
    ).astype(jnp.bfloat16)
    attn_mixed = attn_mixed.reshape(micro_count * row_count, query_width)
    branch = jnp.dot(attn_mixed, out_weight, preferred_element_type=jnp.float32)
    x_mid = x_in + branch.reshape(micro_count, row_count, model_width)
    h_mid = rms_norm(x_mid, gain_mid).astype(jnp.bfloat16)
    local_experts = gate_up_weight.shape[0]
    experts_all = local_experts * lax.axis_size("expert")
    capacity = max(4, row_count * top_count * 3 // (2 * experts_all))
    flat_routes = routes.reshape(micro_count, row_count * top_count)
    position = slot_positions(flat_routes, experts_all)
    target = (
        flat_routes * (micro_count * capacity)
        + jnp.arange(micro_count, dtype=jnp.int32)[:, None] * capacity
        + position
    ).reshape(-1)
    spread = jnp.repeat(h_mid, top_count, axis=1).reshape(-1, model_width)
    send_rows = (
        jnp.zeros((experts_all * micro_count * capacity, model_width), jnp.bfloat16)
        .at[target]
        .set(spread)
    )
    send_three = send_rows.reshape(experts_all, micro_count * capacity, model_width)
    arrived = lax.all_to_all(send_three, "expert", split_axis=0, concat_axis=1, tiled=True)
    gate_up = jnp.einsum(
        "erd,edf->erf", arrived, gate_up_weight, preferred_element_type=jnp.float32
    )
    gate_part = gate_up[..., :FFE]
    up_part = gate_up[..., FFE:]
    gate_sigmoid = jax.nn.sigmoid(gate_part)
    activation = (gate_part * gate_sigmoid * up_part).astype(jnp.bfloat16)
    expert_out = jnp.einsum(
        "erf,efd->erd", activation, down_weight, preferred_element_type=jnp.float32
    ).astype(jnp.bfloat16)
    returned = lax.all_to_all(
        expert_out, "expert", split_axis=1, concat_axis=0, tiled=True
    ).reshape(-1, model_width)
    picked = returned[target].reshape(micro_count, row_count, top_count, model_width)
    gate_table = route_gates.reshape(micro_count, row_count, top_count)
    x_out = x_mid + jnp.sum(gate_table[..., None] * picked.astype(jnp.float32), axis=2)
    gains_back, qkv_back, out_back = (
        lax.all_gather(norm_gains, ("dp", "expert"), axis=1, tiled=True),
        lax.all_gather(w_qkv, ("dp", "expert"), axis=0, tiled=True),
        lax.all_gather(w_out, ("dp", "expert"), axis=1, tiled=True),
    )
    gate_up_back, down_back = (
        lax.all_gather(w_gate_up, "dp", axis=1, tiled=True),
        lax.all_gather(w_down, "dp", axis=1, tiled=True),
    )
    grad_out = cotangent.reshape(micro_count, row_count, model_width).astype(jnp.float32)
    slot_grad = (
        (gate_table[..., None] * grad_out[:, :, None, :])
        .astype(jnp.bfloat16)
        .reshape(-1, model_width)
    )
    grad_rows = (
        jnp.zeros((experts_all * micro_count * capacity, model_width), jnp.bfloat16)
        .at[target]
        .set(slot_grad)
    )
    grad_rows = grad_rows.reshape(experts_all, micro_count * capacity, model_width)
    grad_arrived = lax.all_to_all(grad_rows, "expert", split_axis=0, concat_axis=1, tiled=True)
    grad_act = jnp.einsum(
        "erd,efd->erf", grad_arrived, down_back, preferred_element_type=jnp.float32
    )
    grad_down = jnp.einsum(
        "erf,erd->efd", activation, grad_arrived, preferred_element_type=jnp.float32
    )
    grad_gate = grad_act * up_part * gate_sigmoid * (1.0 + gate_part * (1.0 - gate_sigmoid))
    grad_up = grad_act * gate_part * gate_sigmoid
    grad_gu = jnp.concatenate([grad_gate, grad_up], axis=-1).astype(jnp.bfloat16)
    grad_gate_up = jnp.einsum("erd,erf->edf", arrived, grad_gu, preferred_element_type=jnp.float32)
    grad_slots = jnp.einsum(
        "erf,edf->erd", grad_gu, gate_up_back, preferred_element_type=jnp.float32
    ).astype(jnp.bfloat16)
    grad_returned = lax.all_to_all(
        grad_slots, "expert", split_axis=1, concat_axis=0, tiled=True
    ).reshape(-1, model_width)
    grad_h_mid = jnp.sum(
        grad_returned[target]
        .reshape(micro_count, row_count, top_count, model_width)
        .astype(jnp.float32),
        axis=2,
    )
    _, norm_pull_mid = jax.vjp(rms_norm, x_mid, gain_mid)
    grad_x_part_mid, grad_gain_mid = norm_pull_mid(grad_h_mid)
    grad_x_mid = grad_out + grad_x_part_mid
    grad_branch = grad_x_mid.reshape(micro_count * row_count, model_width).astype(jnp.bfloat16)
    grad_wout = jnp.dot(attn_mixed.T, grad_branch, preferred_element_type=jnp.float32)
    grad_mixed = jnp.dot(grad_branch, out_back.T, preferred_element_type=jnp.float32).astype(
        jnp.bfloat16
    )
    grad_mixed = grad_mixed.reshape(micro_count, row_count, KV, group_size, HD)
    scores_again = attention_scores(queries, keys_all, allowed, score_scale)
    probs_again = jnp.exp(scores_again - log_total)
    grad_probs = jnp.einsum(
        "mqkgd,mtkd->mkgqt", grad_mixed, values_all, preferred_element_type=jnp.float32
    )
    grad_values_all = jnp.einsum(
        "mkgqt,mqkgd->mtkd",
        probs_again.astype(jnp.bfloat16),
        grad_mixed,
        preferred_element_type=jnp.float32,
    )
    grad_scores = (
        probs_again * (grad_probs - jnp.sum(probs_again * grad_probs, axis=-1, keepdims=True))
    ).astype(jnp.bfloat16)
    grad_queries = (
        jnp.einsum("mkgqt,mtkd->mqkgd", grad_scores, keys_all, preferred_element_type=jnp.float32)
        * score_scale
    )
    grad_keys_all = (
        jnp.einsum("mkgqt,mqkgd->mtkd", grad_scores, queries, preferred_element_type=jnp.float32)
        * score_scale
    )
    grad_keys, grad_values = (
        lax.psum_scatter(
            grad_keys_all.astype(jnp.bfloat16), "dp", scatter_dimension=1, tiled=True
        ).astype(jnp.float32),
        lax.psum_scatter(
            grad_values_all.astype(jnp.bfloat16), "dp", scatter_dimension=1, tiled=True
        ).astype(jnp.float32),
    )
    grad_qkv = jnp.concatenate(
        [
            grad_queries.reshape(micro_count, row_count, query_width),
            grad_keys.reshape(micro_count, row_count, kv_width),
            grad_values.reshape(micro_count, row_count, kv_width),
        ],
        axis=-1,
    )
    grad_qkv = grad_qkv.astype(jnp.bfloat16).reshape(micro_count * row_count, -1)
    grad_wqkv = jnp.dot(h_flat.T, grad_qkv, preferred_element_type=jnp.float32)
    grad_h_in = jnp.dot(grad_qkv, qkv_back.T, preferred_element_type=jnp.float32)
    grad_h_in = grad_h_in.reshape(micro_count, row_count, model_width)
    _, norm_pull_in = jax.vjp(rms_norm, x_in, gain_in)
    grad_x_part_in, grad_gain_in = norm_pull_in(grad_h_in)
    grad_x = grad_x_mid + grad_x_part_in
    gain_grads = jnp.stack([grad_gain_in, grad_gain_mid])
    grad_gains_s, grad_wqkv_s, grad_wout_s = (
        lax.psum_scatter(gain_grads, ("dp", "expert"), scatter_dimension=1, tiled=True),
        lax.psum_scatter(grad_wqkv, ("dp", "expert"), scatter_dimension=0, tiled=True),
        lax.psum_scatter(grad_wout, ("dp", "expert"), scatter_dimension=1, tiled=True),
    )
    grad_gu_s, grad_down_s = (
        lax.psum_scatter(
            grad_gate_up.astype(jnp.bfloat16), "dp", scatter_dimension=1, tiled=True
        ).astype(jnp.float32),
        lax.psum_scatter(
            grad_down.astype(jnp.bfloat16), "dp", scatter_dimension=1, tiled=True
        ).astype(jnp.float32),
    )
    out_shape = (micro_count, 1, row_count, model_width)
    return (
        x_out.astype(jnp.bfloat16).reshape(out_shape),
        grad_x.astype(jnp.bfloat16).reshape(out_shape),
        grad_gains_s,
        grad_wqkv_s,
        grad_wout_s,
        grad_gu_s,
        grad_down_s,
    )


def solution(mesh):
    placed = (
        P(None, "expert", "dp", None),
        P(None, "expert", "dp", None),
        P(None, "expert", None),
        P(None, "expert", None),
        P(None, "expert", "dp", None),
        P(None, "expert", "dp", None),
        P(None, ("dp", "expert")),
        P(("dp", "expert"), None),
        P(None, ("dp", "expert")),
        P("expert", "dp", None),
        P("expert", "dp", None),
    )
    return jax.shard_map(
        body,
        mesh=mesh,
        in_specs=placed,
        out_specs=(
            P(None, "expert", "dp", None),
            P(None, "expert", "dp", None),
            P(None, ("dp", "expert")),
            P(("dp", "expert"), None),
            P(None, ("dp", "expert")),
            P("expert", "dp", None),
            P("expert", "dp", None),
        ),
        check_vma=False,
    )
```

profile of v0, /device:TPU:0, one launch (start us, length us, event | category | flops | bytes accessed | tf_op | source)
XLA Modules:
  0.0 1859.7 jit_solution(15481003950590722893)
XLA Ops:
  10.3 43.3 %all-gather = bf16[32,48,2]{1,2,0:T(2,128)(2,1)S(1)} all-gather(bf16[1,48,2]{1,2,0:T(2,128)(2,1)} %bitcast.315), channel_id=1, replica_groups=mesh['dp'=4,'expert'=8] {'dp','expert'}, dimensions={0}, use_global_device_ids=true | all-gather | bytes 6336 | tf_op jit(solution)/shard_map/all_gather | solution.py:84
  56.8 32.3 %all-gather.8.cloned.1.call-done = bf16[1536,2560]{1,0:T(8,128)(2,1)} async-done(((bf16[48,2560]{1,0:T(8,128)(2,1)}), bf16[1536,2560]{1,0:T(8,128)(2,1)}) %all-gather.8.cloned.1.call-update) | async-done | bytes 7864336 | tf_op jit(solution)/shard_map/all_gather | solution.py:85
  89.1 7.6 convolution_convert_fusion.2
  101.8 9.1 reduce-window.6
  112.9 6.0 fusion.10
  119.0 42.1 %scatter_custom_fusion.1 = bf16[6144,1536]{1,0:T(8,128)(2,1)} fusion(s32[4096]{0:T(1024)S(1)} %bitcast.306, bf16[4096,1536]{1,0:T(8,128)(2,1)} %fusion.10, bf16[]{:T(256)} %constant.64.clone.1), kind=kCustom, calls=%fused_computation.39 | custom fusion | bytes 18874880 | tf_op jit(solution)/shard_map/scatter | solution.py:181
  161.1 5.9 all-to-all-start.2
  167.7 7.7 while.13
  179.5 20.9 %fusion.13 = (f32[2,8,3,256]{3,2,1,0:T(4,128)S(1)}, f32[2,8,1024,256,3]{3,2,4,1,0:T(8,128)}) fusion(pred[2,256,1024]{1,2,0:T(8,128)(4,1)S(1)} %fusion.48, bf16[2,256,8,3,64]{1,4,3,2,0:T(8,128)(2,1)S(1)} %bitcast.282, bf16[2,1024,8,64]{1,3,2,0:T(8,128)(2,1)} %all-gather.12.cloned.1.call-done), kind=kOutput, calls=%fused_computation.30 | convolution fusion | flops 1648349184 | bytes 54575104 | tf_op jit(solution)/shard_map/mqkgd,mtkd->mkgqt/dot_general | solution.py:58
  200.4 21.0 %fusion.5 = f32[2,8,3,256]{3,2,1,0:T(4,128)S(1)} fusion(f32[2,8,3,256]{3,2,1,0:T(4,128)S(1)} %get-tuple-element.91, f32[2,8,1024,256,3]{3,2,4,1,0:T(8,128)} %get-tuple-element.92, pred[2,256,1024]{1,2,0:T(8,128)(4,1)S(1)} %fusion.48), kind=kLoop, calls=%fused_computation.20 | loop fusion | flops 50319360 | bytes 50954240 | tf_op jit(solution)/shard_map/reduce_sum | solution.py:116
  221.5 22.3 %fusion.49 = bf16[2,8,64,3,256]{4,2,3,1,0:T(8,128)(2,1)} fusion(f32[2,8,3,256]{3,2,1,0:T(4,128)S(1)} %fusion.5, f32[2,8,3,256]{3,2,1,0:T(4,128)S(1)} %get-tuple-element.91, f32[2,8,1024,256,3]{3,2,4,1,0:T(8,128)} %get-tuple-element.92, pred[2,256,1024]{1,2,0:T(8,128)(4,1)S(1)} %fusion.48, bf16[2,1024,8,64]{1,3,2,0:T(8,128)(2,1)} %all-gather.10.cloned.1.call-done), kind=kOutput, calls=%fused_computation.90 | convolution fusion | flops 1674313728 | bytes 54624256 | tf_op jit(solution)/shard_map/mkgqt,mtkd->mqkgd/dot_general | solution.py:119
  243.8 72.4 %all-gather.14.cloned.1.call-done = bf16[1536,1536]{0,1:T(8,128)(2,1)} async-done(((bf16[1536,48]{0,1:T(8,128)(2,1)}), bf16[1536,1536]{0,1:T(8,128)(2,1)}) %all-gather.14.cloned.1.call-update) | async-done | bytes 4718608 | tf_op jit(solution)/shard_map/all_gather | solution.py:86
  321.8 6.2 broadcast_in_dim.35
  328.0 30.8 %scatter_custom_fusion = bf16[6144,1536]{1,0:T(8,128)(2,1)} fusion(s32[4096]{0:T(1024)S(1)} %bitcast.307, bf16[4096,1536]{1,0:T(8,128)(2,1)} %bitcast.288, bf16[]{:T(256)} %constant.64.clone.1), kind=kCustom, calls=%fused_computation.41 | custom fusion | bytes 18874880 | tf_op jit(solution)/shard_map/scatter | solution.py:143
  358.8 28.4 %all-to-all-done.2 = bf16[16,384,1536]{2,1,0:T(8,128)(2,1)} async-done(((bf16[16,384,1536]{2,1,0:T(8,128)(2,1)}), bf16[16,384,1536]{2,1,0:T(8,128)(2,1)}, u32[]{:S(2)}, u32[]{:S(2)}) %all-to-all-start.2) | async-done | bytes 18874400 | tf_op jit(solution)/shard_map/all_to_all | solution.py:184
  387.2 11.9 all-to-all-start
  401.3 17.2 copy.99
  418.5 188.6 %all-to-all-done = bf16[16,384,1536]{2,1,0:T(8,128)(2,1)} async-done(((bf16[16,384,1536]{2,1,0:T(8,128)(2,1)}), bf16[16,384,1536]{2,1,0:T(8,128)(2,1)}, u32[]{:S(2)}, u32[]{:S(2)}) %all-to-all-start) | async-done | bytes 18874400 | tf_op jit(solution)/shard_map/all_to_all | solution.py:146
  607.1 16.9 copy.92
  624.0 27.2 %fusion.85 = f32[2,3072,1024]{1,2,0:T(8,128)} fusion(bf16[2,3072,1536]{2,1,0:T(8,128)(2,1)} %bitcast.284, bf16[2,1536,1024]{1,2,0:T(8,128)(2,1)} %all-gather.16.cloned.1.call-done), kind=kOutput, calls=%fused_computation.146 | convolution fusion | flops 19327352832 | bytes 50331648 | tf_op jit(solution)/shard_map/erd,edf->erf/dot_general | solution.py:147
  651.3 26.0 %multiply_convert_fusion.1 = (bf16[2,3072,512]{1,2,0:T(8,128)(2,1)}, bf16[2,3072,512]{1,2,0:T(8,128)(2,1)}, bf16[2,3072,512]{1,2,0:T(8,128)(2,1)}) fusion(f32[2,3072,1024]{1,2,0:T(8,128)} %fusion.85, bf16[2,3072,1536]{2,1,0:T(8,128)(2,1)} %bitcast.286, bf16[2,512,1536]{2,1,0:T(8,128)(2,1)} %all-gather.18.cloned.1.call-done), kind=kOutput, calls=%fused_computation.36 | convolution fusion | flops 9714008064 | bytes 66060288 | tf_op jit(solution)/shard_map/erd,efd->erf/dot_general | solution.py:185
  677.2 27.2 %convolution_convert_fusion = bf16[2,3072,1536]{2,1,0:T(8,128)(2,1)} fusion(bf16[2,1536,1024]{1,2,0:T(8,128)(2,1)} %all-gather.16.cloned.1.call-done, bf16[2,3072,512]{1,2,0:T(8,128)(2,1)} %get-tuple-element.81, bf16[2,3072,512]{1,2,0:T(8,128)(2,1)} %get-tuple-element.80), kind=kOutput, calls=%fused_computation.31 | convolution fusion | flops 19361955840 | bytes 37748736 | tf_op jit(solution)/shard_map/erf,edf->erd/dot_general | solution.py:195
  704.4 34.8 %copy.102 = bf16[2,3072,1536]{2,0,1:T(2,128)(2,1)} copy(bf16[2,3072,1536]{2,1,0:T(8,128)(2,1)} %convolution_convert_fusion) | data formatting | bytes 37748736 | tf_op jit(solution)/shard_map/convert_element_type | solution.py:197
  739.2 6.0 all-to-all-start.3
  745.4 206.3 %all-to-all-done.3 = bf16[2,3072,1536]{2,0,1:T(2,128)(2,1)} async-done(((bf16[2,3072,1536]{2,0,1:T(2,128)(2,1)}), bf16[2,3072,1536]{2,0,1:T(2,128)(2,1)}, u32[]{:S(2)}, u32[]{:S(2)}) %all-to-all-start.3) | async-done | bytes 18874400 | tf_op jit(solution)/shard_map/all_to_all | solution.py:198
  951.6 19.1 %copy.103 = bf16[2,8,384,1536]{3,2,0,1:T(8,128)(2,1)} copy(bf16[2,8,384,1536]{3,0,2,1:T(2,128)(2,1)} %bitcast.43) | data formatting | bytes 37748736 | tf_op jit(solution)/shard_map/all_to_all | solution.py:198
  970.7 34.1 %gather_fusion.2 = bf16[4096,1536]{1,0:T(8,128)(2,1)} fusion(bf16[6144,1536]{1,0:T(8,128)(2,1)} %bitcast.279, s32[4096]{0:T(1024)S(1)} %broadcast_clamp_fusion), kind=kCustom, calls=%fused_computation.2 | custom fusion | bytes 25182208 | tf_op jit(solution)/shard_map/gather | solution.py:202
  1004.8 10.8 convert_reduce_fusion
  1027.6 22.7 %fusion.53 = bf16[2,1024,8,64]{1,3,2,0:T(8,128)(2,1)} fusion(f32[2,8,3,256]{3,2,1,0:T(4,128)S(1)} %log_add_fusion, f32[2,8,1024,256,3]{3,2,4,1,0:T(8,128)} %get-tuple-element.92, pred[2,256,1024]{1,2,0:T(8,128)(4,1)S(1)} %copy-done.7, bf16[2,256,8,3,64]{1,0,4,3,2:T(2,128)(2,1)} %reshape.324), kind=kOutput, calls=%fused_computation.92 | convolution fusion | flops 1661992960 | bytes 54575104 | tf_op jit(solution)/shard_map/mkgqt,mqkgd->mtkd/dot_general | solution.py:221
  1050.4 37.6 %fusion.2 = (f32[2,8,3,256]{3,2,1,0:T(4,128)S(1)}, f32[2,8,1024,256,3]{3,2,4,1,0:T(8,128)}) fusion(f32[2,8,3,256]{3,2,1,0:T(4,128)S(1)} %log_add_fusion, f32[2,8,1024,256,3]{3,2,4,1,0:T(8,128)} %get-tuple-element.92, pred[2,256,1024]{1,2,0:T(8,128)(4,1)S(1)} %copy-done.7, bf16[2,256,8,3,64]{1,0,4,3,2:T(2,128)(2,1)S(1)} %copy-done.16, ...), kind=kOutput, calls=%fused_computation.13 | convolution fusion | flops 1673515008 | bytes 104955904 | tf_op jit(solution)/shard_map/mqkgd,mtkd->mkgqt/dot_general | solution.py:218
  1088.0 41.2 %fusion.4 = bf16[2,8,3,256,1024]{3,4,2,1,0:T(8,128)(2,1)} fusion(f32[2,8,1024,256,3]{3,2,4,1,0:T(8,128)} %get-tuple-element.96, f32[2,8,3,256]{3,2,1,0:T(4,128)S(1)} %get-tuple-element.95, f32[2,8,3,256]{3,2,1,0:T(4,128)S(1)} %log_add_fusion, f32[2,8,1024,256,3]{3,2,4,1,0:T(8,128)} %get-tuple-element.92, pred[2,256,1024]{1,2,0:T(8,128)(4,1)S(1)} %copy-done.7), kind=kLoop, calls=%fused_computation.15 | loop fusion | flops 75497472 | bytes 126451712 | tf_op jit(solution)/shard_map/convert_element_type | solution.py:229
  1129.2 13.3 fusion.52
  1142.7 17.3 convolution_convert_fusion.3
  1160.1 30.7 %fusion.21 = bf16[2,1536,1024]{2,1,0:T(8,128)(2,1)} fusion(bf16[2,3072,1536]{2,1,0:T(8,128)(2,1)} %bitcast.285, bf16[2,3072,512]{1,2,0:T(8,128)(2,1)} %get-tuple-element.81, bf16[2,3072,512]{1,2,0:T(8,128)(2,1)} %get-tuple-element.80), kind=kOutput, calls=%fused_computation.46 | convolution fusion | flops 19355664384 | bytes 37748736 | tf_op jit(solution)/shard_map/erd,erf->edf/dot_general | solution.py:194
  1196.0 13.6 multiply_convert_fusion.3
  1216.5 10.3 fusion.35
  1228.1 6.5 fusion.86
  1236.1 9.1 convolution_bitcast_fusion
  1245.2 16.7 convolution_convert_fusion.1
  1261.8 34.8 %copy.95 = bf16[2,3072,1536]{2,0,1:T(2,128)(2,1)} copy(bf16[2,3072,1536]{2,1,0:T(8,128)(2,1)} %convolution_convert_fusion.1) | data formatting | bytes 37748736 | tf_op jit(solution)/shard_map/convert_element_type | solution.py:156
  1296.7 6.2 all-to-all-start.1
  1305.5 54.2 %reduce-scatter.18.cloned.1.call-done = bf16[2,384,1024]{2,1,0:T(8,128)(2,1)} async-done(((bf16[2,1536,1024]{2,1,0:T(8,128)(2,1)}), bf16[2,384,1024]{2,1,0:T(8,128)(2,1)}) %reduce-scatter.18.cloned.1.call-update) | async-done | bytes 1572880 | tf_op jit(solution)/shard_map/reduce_scatter | solution.py:268
  1363.2 148.0 %all-to-all-done.1 = bf16[2,3072,1536]{2,0,1:T(2,128)(2,1)} async-done(((bf16[2,3072,1536]{2,0,1:T(2,128)(2,1)}), bf16[2,3072,1536]{2,0,1:T(2,128)(2,1)}, u32[]{:S(2)}, u32[]{:S(2)}) %all-to-all-start.1) | async-done | bytes 18874400 | tf_op jit(solution)/shard_map/all_to_all | solution.py:157
  1511.2 18.8 %copy.96 = bf16[2,8,384,1536]{3,2,0,1:T(8,128)(2,1)} copy(bf16[2,8,384,1536]{3,0,2,1:T(2,128)(2,1)} %bitcast.29) | data formatting | bytes 37748736 | tf_op jit(solution)/shard_map/all_to_all | solution.py:157
  1530.0 34.2 %gather_fusion.1 = bf16[4096,1536]{1,0:T(8,128)(2,1)} fusion(bf16[6144,1536]{1,0:T(8,128)(2,1)} %bitcast.278, s32[4096]{0:T(1024)S(1)} %copy-done.32), kind=kCustom, calls=%fused_computation.1 | custom fusion | bytes 25182208 | tf_op jit(solution)/shard_map/gather | solution.py:160
  1564.2 30.2 %fusion.9 = f32[2,256,1536]{2,1,0:T(8,128)S(1)} fusion(f32[2,256,8]{2,1,0:T(8,128)S(1)} %copy.88, bf16[4096,1536]{1,0:T(8,128)(2,1)} %gather_fusion.1), kind=kLoop, calls=%fused_computation.25 | loop fusion | flops 18087936 | bytes 15745024 | tf_op jit(solution)/shard_map/reduce_sum | solution.py:162
  1599.4 76.4 %reduce-scatter.16.cloned.1.call-done = f32[1536,48]{0,1:T(8,128)} async-done(((f32[1536,1536]{0,1:T(8,128)}), f32[1536,48]{0,1:T(8,128)}) %reduce-scatter.16.cloned.1.call-update) | async-done | bytes 294928 | tf_op jit(solution)/shard_map/reduce_scatter | solution.py:265
  1675.8 177.3 %reduce-scatter.14.cloned.1.call-done = f32[48,2560]{1,0:T(8,128)} async-done(((f32[1536,2560]{1,0:T(8,128)}), f32[48,2560]{1,0:T(8,128)}) %reduce-scatter.14.cloned.1.call-update) | async-done | bytes 491536 | tf_op jit(solution)/shard_map/reduce_scatter | solution.py:264
  (259 shorter events, 71.1 us)
Async XLA Ops:
  7.2 82.0 %all-gather.8.cloned.1.call-start = ((), (), s32[]{:S(2)}) async-start(), calls=%async_computation.11 | async-start | bytes 8110080 | tf_op jit(solution)/shard_map/all_gather | solution.py:85
  7.9 171.6 %all-gather.12.cloned.1.call-start = ((), (), s32[]{:S(2)}) async-start(), calls=%async_computation.13 | async-start | bytes 2621440 | tf_op jit(solution)/shard_map/all_gather | solution.py:105
  9.7 43.9 %copy-start.46 = (f32[2,256]{1,0:T(2,128)}, f32[2,256]{1,0:T(2,128)S(1)}, u32[]{:S(2)}) copy-start(f32[2,256]{1,0:T(2,128)S(1)} %fusion.37) | copy-start | bytes 6148
  96.8 15.4 copy-start.35
  96.8 15.7 copy-start.10
  99.4 122.1 %all-gather.10.cloned.1.call-start = ((), (), s32[]{:S(2)}) async-start(), calls=%async_computation.12 | async-start | bytes 2621440 | tf_op jit(solution)/shard_map/all_gather | solution.py:106
  119.0 209.0 %copy-start.38 = (s32[4096,1]{0,1:T(1,128)}, s32[4096,1]{0,1:T(1,128)S(1)}, u32[]{:S(2)}) copy-start(s32[4096,1]{0,1:T(1,128)S(1)} %compare_select_fusion.1) | copy-start | bytes 49156
  161.1 14.3 copy-start.51
  161.1 226.1 %all-to-all-start.2 = ((bf16[16,384,1536]{2,1,0:T(8,128)(2,1)}), bf16[16,384,1536]{2,1,0:T(8,128)(2,1)}, u32[]{:S(2)}, u32[]{:S(2)}) async-start(bf16[16,384,1536]{2,1,0:T(8,128)(2,1)} %bitcast.280), calls=%async_computation.2 | async-start | bytes 37748736 | tf_op jit(solution)/shard_map/all_to_all | solution.py:184
  167.1 9.4 copy-start.19
  167.1 149.1 %all-gather.14.cloned.1.call-start = ((), (), s32[]{:S(2)}) async-start(), calls=%async_computation.14 | async-start | bytes 4866048 | tf_op jit(solution)/shard_map/all_gather | solution.py:86
  176.5 45.0 %copy-start.6 = (pred[2,256,1024]{1,2,0:T(8,128)(4,1)}, pred[2,256,1024]{1,2,0:T(8,128)(4,1)S(1)}, u32[]{:S(2)}) copy-start(pred[2,256,1024]{1,2,0:T(8,128)(4,1)S(1)} %fusion.48) | copy-start | bytes 1572868
  179.5 20.9 %copy-start.8 = (bf16[2,256,1536]{1,2,0:T(8,128)(2,1)}, bf16[2,256,1536]{1,2,0:T(8,128)(2,1)S(1)}, u32[]{:S(2)}) copy-start(bf16[2,256,1536]{1,2,0:T(8,128)(2,1)S(1)} %copy.85) | copy-start | bytes 4718596
  200.4 21.1 %copy-start.24 = (f32[2,8,3,256]{3,2,1,0:T(4,128)}, f32[2,8,3,256]{3,2,1,0:T(4,128)S(1)}, u32[]{:S(2)}) copy-start(f32[2,8,3,256]{3,2,1,0:T(4,128)S(1)} %get-tuple-element.91) | copy-start | bytes 147460
  221.4 22.3 %copy-start.26 = (f32[2,8,3,256]{3,2,1,0:T(4,128)}, f32[2,8,3,256]{3,2,1,0:T(4,128)S(1)}, u32[]{:S(2)}) copy-start(f32[2,8,3,256]{3,2,1,0:T(4,128)S(1)} %fusion.5) | copy-start | bytes 147460
  221.5 94.8 %copy-start.13 = (bf16[2,1,256,1536]{3,2,1,0:T(8,128)(2,1)S(1)}, bf16[2,1,256,1536]{3,2,1,0:T(8,128)(2,1)}, u32[]{:S(2)}) copy-start(bf16[2,1,256,1536]{3,2,1,0:T(8,128)(2,1)} %param.13) | copy-start | bytes 4718596
  387.2 11.9 copy-start.22
  387.2 219.9 %all-to-all-start = ((bf16[16,384,1536]{2,1,0:T(8,128)(2,1)}), bf16[16,384,1536]{2,1,0:T(8,128)(2,1)}, u32[]{:S(2)}, u32[]{:S(2)}) async-start(bf16[16,384,1536]{2,1,0:T(8,128)(2,1)} %bitcast.281), calls=%async_computation | async-start | bytes 37748736 | tf_op jit(solution)/shard_map/all_to_all | solution.py:146
  399.1 225.0 %all-gather.16.cloned.1.call-start = ((), (), s32[]{:S(2)}) async-start(), calls=%async_computation.15 | async-start | bytes 7864320 | tf_op jit(solution)/shard_map/all_gather | solution.py:89
  400.7 250.5 %all-gather.18.cloned.1.call-start = ((), (), s32[]{:S(2)}) async-start(), calls=%async_computation.16 | async-start | bytes 3932160 | tf_op jit(solution)/shard_map/all_gather | solution.py:90
  739.2 212.5 %all-to-all-start.3 = ((bf16[2,3072,1536]{2,0,1:T(2,128)(2,1)}), bf16[2,3072,1536]{2,0,1:T(2,128)(2,1)}, u32[]{:S(2)}, u32[]{:S(2)}) async-start(bf16[2,3072,1536]{2,0,1:T(2,128)(2,1)} %copy.102), calls=%async_computation.3 | async-start | bytes 37748736 | tf_op jit(solution)/shard_map/all_to_all | solution.py:198
  745.2 467.1 %reduce-scatter.12.cloned.1.call-start = ((), (), s32[]{:S(2)}) async-start(), calls=%async_computation.18 | async-start | bytes 2621440 | tf_op jit(solution)/shard_map/reduce_scatter | solution.py:242
  745.3 225.4 %copy-start.31 = (s32[4096]{0:T(1024)}, s32[4096]{0:T(1024)S(1)}, u32[]{:S(2)}) copy-start(s32[4096]{0:T(1024)S(1)} %broadcast_clamp_fusion) | copy-start | bytes 49156
  1004.8 10.8 copy-start.2
  1004.8 10.8 copy-start.29
  1004.8 10.9 copy-start.41
  1027.6 22.8 %copy-start.16 = (bf16[2,256,8,3,64]{1,0,4,3,2:T(2,128)(2,1)S(1)}, bf16[2,256,8,3,64]{1,0,4,3,2:T(2,128)(2,1)}, u32[]{:S(2)}) copy-start(bf16[2,256,8,3,64]{1,0,4,3,2:T(2,128)(2,1)} %reshape.324) | copy-start | bytes 4718596
  1050.3 164.1 %reduce-scatter.10.cloned.1.call-start = ((), (), s32[]{:S(2)}) async-start(), calls=%async_computation.17 | async-start | bytes 2621440 | tf_op jit(solution)/shard_map/reduce_scatter | solution.py:239
  1088.0 41.3 %copy-start.9 = (bf16[2,256,1536]{1,2,0:T(8,128)(2,1)S(1)}, bf16[2,256,1536]{1,2,0:T(8,128)(2,1)}, u32[]{:S(2)}) copy-start(bf16[2,256,1536]{1,2,0:T(8,128)(2,1)} %copy-done.8) | copy-start | bytes 4718596
  1142.6 160.4 %reduce-scatter.20.cloned.1.call-start = ((), (), s32[]{:S(2)}) async-start(), calls=%async_computation.22 | async-start | bytes 3932160 | tf_op jit(solution)/shard_map/reduce_scatter | solution.py:271
  1160.0 199.7 %reduce-scatter.18.cloned.1.call-start = ((), (), s32[]{:S(2)}) async-start(), calls=%async_computation.21 | async-start | bytes 7864320 | tf_op jit(solution)/shard_map/reduce_scatter | solution.py:268
  1190.8 407.2 %reduce-scatter.22.cloned.1.call-start = ((), (), s32[]{:S(2)}) async-start(), calls=%async_computation.23 | async-start | bytes 811008
  1209.7 6.8 copy-start.14
  1209.7 6.8 copy-start.34
  1209.7 6.8 copy-start.48
  1216.5 11.7 copy-start.21
  1228.1 447.7 %reduce-scatter.16.cloned.1.call-start = ((), (), s32[]{:S(2)}) async-start(), calls=%async_computation.20 | async-start | bytes 9732096 | tf_op jit(solution)/shard_map/reduce_scatter | solution.py:265
  1234.7 618.3 %reduce-scatter.14.cloned.1.call-start = ((), (), s32[]{:S(2)}) async-start(), calls=%async_computation.19 | async-start | bytes 16220160 | tf_op jit(solution)/shard_map/reduce_scatter | solution.py:264
  1296.7 214.5 %all-to-all-start.1 = ((bf16[2,3072,1536]{2,0,1:T(2,128)(2,1)}), bf16[2,3072,1536]{2,0,1:T(2,128)(2,1)}, u32[]{:S(2)}, u32[]{:S(2)}) async-start(bf16[2,3072,1536]{2,0,1:T(2,128)(2,1)} %copy.95), calls=%async_computation.1 | async-start | bytes 37748736 | tf_op jit(solution)/shard_map/all_to_all | solution.py:157
  1511.2 18.8 %copy-start.32 = (s32[4096]{0:T(1024)S(1)}, s32[4096]{0:T(1024)}, u32[]{:S(2)}) copy-start(s32[4096]{0:T(1024)} %copy-done.31) | copy-start | bytes 49156
  1564.2 30.3 %copy-start.47 = (f32[2,256]{1,0:T(2,128)S(1)}, f32[2,256]{1,0:T(2,128)}, u32[]{:S(2)}) copy-start(f32[2,256]{1,0:T(2,128)} %copy-done.46) | copy-start | bytes 6148
  1564.2 30.3 %copy-start.3 = (f32[2,256,1536]{2,1,0:T(8,128)S(1)}, f32[2,256,1536]{2,1,0:T(8,128)}, u32[]{:S(2)}) copy-start(f32[2,256,1536]{2,1,0:T(8,128)} %copy-done.1) | copy-start | bytes 9437188
  1564.2 30.3 %copy-start.5 = (f32[2,256,1536]{2,1,0:T(8,128)S(1)}, f32[2,256,1536]{2,1,0:T(8,128)}, u32[]{:S(2)}) copy-start(f32[2,256,1536]{2,1,0:T(8,128)} %copy-done.4) | copy-start | bytes 9437188
  1564.2 30.3 %copy-start.12 = (bf16[2,1,256,1536]{3,2,1,0:T(8,128)(2,1)S(1)}, bf16[2,1,256,1536]{3,2,1,0:T(8,128)(2,1)}, u32[]{:S(2)}) copy-start(bf16[2,1,256,1536]{3,2,1,0:T(8,128)(2,1)} %param.14) | copy-start | bytes 4718596
  1564.2 30.3 %copy-start.17 = (f32[2,256,1536]{2,1,0:T(8,128)S(1)}, f32[2,256,1536]{2,1,0:T(8,128)}, u32[]{:S(2)}) copy-start(f32[2,256,1536]{2,1,0:T(8,128)} %get-tuple-element.97) | copy-start | bytes 9437188
  1564.2 30.3 %copy-start.30 = (f32[1536]{0:T(1024)S(1)}, f32[1536]{0:T(1024)}, u32[]{:S(2)}) copy-start(f32[1536]{0:T(1024)} %get-tuple-element.70) | copy-start | bytes 18436
  1564.2 30.3 %copy-start.42 = (f32[2,256]{1,0:T(2,128)S(1)}, f32[2,256]{1,0:T(2,128)}, u32[]{:S(2)}) copy-start(f32[2,256]{1,0:T(2,128)} %copy-done.40) | copy-start | bytes 6148
  1564.2 30.3 %copy-start.45 = (f32[2,256]{1,0:T(2,128)S(1)}, f32[2,256]{1,0:T(2,128)}, u32[]{:S(2)}) copy-start(f32[2,256]{1,0:T(2,128)} %copy-done.44) | copy-start | bytes 6148
  (23 other events, 92.5 us)
Sparse Core Ops, SparseCore 0:
  10.9 78.1 all-gather.7
  99.5 44.7 all-gather.11
  145.9 44.4 all-gather.9
  193.2 122.9 all-gather.13
  401.8 117.1 all-gather.15
  520.4 61.6 all-gather.17
  1050.4 41.6 reduce-scatter.11
  1142.7 41.4 reduce-scatter.9
  1187.1 59.5 reduce-scatter.19
  1248.9 110.7 reduce-scatter.17
  1364.8 170.0 reduce-scatter.21
  1541.2 134.5 reduce-scatter.15
  1683.4 169.6 reduce-scatter.13
where the time goes:
time: 1860 us
  waiting for transfers between devices  986 us (53%)
  local copies, waits for them, and re-layouts  328 us (18%)
  matrix products  318 us (17%)
  other arithmetic  138 us (7%)
  blocking collectives  43.3 us (2%)
  starting transfers between devices  31.6 us (2%)
    all_to_all x1, waiting for transfers between devices, body(): lax.all_to_all(grad_slots, 'expert', split_axis=1, concat_axis=0, tiled=T...  206 us
    all_to_all x1, waiting for transfers between devices, body(): lax.all_to_all(send_three, 'expert', split_axis=0, concat_axis=1, tiled=T...  189 us
    reduce_scatter x1, waiting for transfers between devices, body(): lax.psum_scatter(grad_wqkv, ('dp', 'expert'), scatter_dimension=0, tiled=...  177 us
    all_to_all x1, waiting for transfers between devices, body(): lax.all_to_all(expert_out, 'expert', split_axis=1, concat_axis=0, tiled=T...  148 us
    reduce_scatter x1, waiting for transfers between devices, body(): lax.psum_scatter(grad_wout, ('dp', 'expert'), scatter_dimension=1, tiled=...  76.4 us
    all_gather x1, waiting for transfers between devices, body(): lax.all_gather(w_out, ('dp', 'expert'), axis=1, tiled=True)  72.4 us
    reduce_scatter x1, waiting for transfers between devices, body(): lax.psum_scatter(grad_gate_up.astype(jnp.bfloat16), 'dp', scatter_dimensi...  54.2 us
    all_gather x1, blocking collectives, body(): lax.all_gather(norm_gains, ('dp', 'expert'), axis=1, tiled=True)  43.3 us
  transfers between devices with their start and end apart: 17, of which 9 were waited for; matrix products, arithmetic and copies ran while one was open for 31% of the time, Pallas kernels for 0%

commit v1 on v0

v1 whole, which is shorter than its diff:
```python
import functools

import jax
import jax.numpy as jnp
from jax import lax
from jax.experimental import pallas as pl
from jax.experimental.pallas import tpu as pltpu
from jax.sharding import PartitionSpec as P

H = 24
KV = 8
HD = 64
FFE = 512
BLOCK = 128
PAIRS = KV // 2
GROUP = H // KV
PAIR_Q = 2 * GROUP * HD
PAIR_K = 2 * HD

EPSILON = 1e-06
NEGATIVE = -1e30
F32 = jnp.float32
BF16 = jnp.bfloat16


def mm(a, b):
    return jnp.dot(a, b, preferred_element_type=F32)


def mm_nt(a, b):
    return lax.dot_general(a, b, (((1,), (1,)), ((), ())), preferred_element_type=F32)


def mm_tn(a, b):
    return lax.dot_general(a, b, (((0,), (0,)), ((), ())), preferred_element_type=F32)


def rms_norm(values_in, gain):
    return (
        values_in
        * lax.rsqrt(jnp.mean(values_in * values_in, axis=-1, keepdims=True) + EPSILON)
        * gain
    )


def rms_back(values, gain, grad):
    inv = lax.rsqrt(jnp.mean(values * values, axis=-1, keepdims=True) + EPSILON)
    unit = values * inv
    scaled = grad * gain
    grad_values = inv * (scaled - unit * jnp.mean(scaled * unit, axis=-1, keepdims=True))
    return grad_values, jnp.sum(grad * unit, axis=0)


def padded_rows(rows, half):
    blank = jnp.zeros_like(rows)
    return jnp.concatenate([rows, blank] if half == 0 else [blank, rows], axis=0)


def attend_kernel(chunks, q_ref, *refs):
    k_refs, v_refs = refs[:chunks], refs[chunks : 2 * chunks]
    bias_ref, o_ref, lse_ref, s_scr, p_scr = refs[2 * chunks :]
    rows = q_ref.shape[0]
    keys = k_refs[0].shape[0]
    q_t = q_ref[...].T * jnp.asarray(HD**-0.5, BF16)
    v_t = [v[...].T for v in v_refs]
    outs, totals = [], []
    for head in range(2 * GROUP):
        half = head // GROUP
        slot = head % 2
        q_pad = padded_rows(q_t[head * HD : (head + 1) * HD], half)
        peak = None
        for c in range(chunks):
            part = slice(c * keys, (c + 1) * keys)
            scores = mm(k_refs[c][...], q_pad) + bias_ref[part, :]
            s_scr[slot, part, :] = scores
            top = jnp.max(scores, axis=0, keepdims=True)
            peak = top if peak is None else jnp.maximum(peak, top)
        total = jnp.zeros((1, rows), F32)
        mixed = jnp.zeros((HD, rows), F32)
        for c in range(chunks):
            part = slice(c * keys, (c + 1) * keys)
            prob = jnp.exp(s_scr[slot, part, :] - peak)
            total = total + jnp.sum(prob, axis=0, keepdims=True)
            p_scr[slot, part, :] = prob.astype(BF16)
        for c in range(chunks):
            part = slice(c * keys, (c + 1) * keys)
            mixed = mixed + mm(v_t[c][half * HD : (half + 1) * HD], p_scr[slot, part, :])
        outs.append(mixed / total)
        totals.append(peak + jnp.log(total))
    o_ref[...] = jnp.concatenate(outs, axis=0).T.astype(BF16)
    blank = jnp.zeros((8 - 2 * GROUP, rows), F32)
    lse_ref[0] = jnp.concatenate(totals + [blank], axis=0)


def kv_specs(chunks, keys):
    k_spec = pl.BlockSpec((keys, PAIR_K), lambda j: (0, j))
    v_spec = pl.BlockSpec((keys, PAIR_K), lambda j: (0, PAIRS + j))
    return [k_spec] * chunks + [v_spec] * chunks


def attend(queries, kv_chunks, bias):
    rows, width = queries.shape
    chunks, keys = len(kv_chunks), kv_chunks[0].shape[0]
    work = 4 * H * rows * chunks * keys * HD
    q_spec = pl.BlockSpec((rows, PAIR_Q), lambda j: (0, j))
    return pl.pallas_call(
        functools.partial(attend_kernel, chunks),
        grid=(PAIRS,),
        in_specs=[q_spec]
        + kv_specs(chunks, keys)
        + [pl.BlockSpec((chunks * keys, rows), lambda j: (0, 0))],
        out_specs=[q_spec, pl.BlockSpec((1, 8, rows), lambda j: (j, 0, 0))],
        out_shape=[
            jax.ShapeDtypeStruct(queries.shape, BF16),
            jax.ShapeDtypeStruct((PAIRS, 8, rows), F32),
        ],
        scratch_shapes=[
            pltpu.VMEM((2, chunks * keys, rows), F32),
            pltpu.VMEM((2, chunks * keys, rows), BF16),
        ],
        compiler_params=pltpu.CompilerParams(vmem_limit_bytes=32 * 1024 * 1024),
        cost_estimate=pl.CostEstimate(
            flops=8 * work, bytes_accessed=4 * 1024 * 1024, transcendentals=work // (4 * HD)
        ),
        name="path_attention",
    )(queries, *kv_chunks, *kv_chunks, bias)


def attend_back_kernel(chunks, q_ref, g_ref, *refs):
    k_refs, v_refs = refs[:chunks], refs[chunks : 2 * chunks]
    bias_ref, lse_ref, dq_ref = refs[2 * chunks : 2 * chunks + 3]
    out_refs = refs[2 * chunks + 3 : 3 * chunks + 3]
    p_scr, gp_scr, ps_scr, ds_scr = refs[3 * chunks + 3 :]
    rows = q_ref.shape[0]
    keys = k_refs[0].shape[0]
    q_t = q_ref[...].T * jnp.asarray(HD**-0.5, BF16)
    g_t = g_ref[...].T
    k_t = [k[...].T for k in k_refs]
    dqs, q_pads, g_pads = [], [], []
    for head in range(2 * GROUP):
        half = head // GROUP
        slot = head % 2
        here = slice(head * rows, (head + 1) * rows)
        q_pad = padded_rows(q_t[head * HD : (head + 1) * HD], half)
        g_pad = padded_rows(g_t[head * HD : (head + 1) * HD], half)
        q_pads.append(q_pad)
        g_pads.append(g_pad)
        lse = lse_ref[0, head : head + 1, :]
        delta = jnp.zeros((1, rows), F32)
        for c in range(chunks):
            part = slice(c * keys, (c + 1) * keys)
            prob = jnp.exp(mm(k_refs[c][...], q_pad) + bias_ref[part, :] - lse)
            grad_prob = mm(v_refs[c][...], g_pad)
            delta = delta + jnp.sum(prob * grad_prob, axis=0, keepdims=True)
            p_scr[slot, part, :] = prob
            gp_scr[slot, part, :] = grad_prob
            ps_scr[part, here] = prob.astype(BF16)
        dq = jnp.zeros((HD, rows), F32)
        for c in range(chunks):
            part = slice(c * keys, (c + 1) * keys)
            ds = (p_scr[slot, part, :] * (gp_scr[slot, part, :] - delta)).astype(BF16)
            ds_scr[part, here] = ds
            dq = dq + mm(k_t[c][half * HD : (half + 1) * HD], ds)
        dqs.append(dq * HD**-0.5)
    dq_ref[...] = jnp.concatenate(dqs, axis=0).T.astype(BF16)
    q_all = jnp.concatenate(q_pads, axis=1)
    g_all = jnp.concatenate(g_pads, axis=1)
    for c in range(chunks):
        part = slice(c * keys, (c + 1) * keys)
        out_refs[c][0] = mm_nt(ds_scr[part, :], q_all).astype(BF16)
        out_refs[c][1] = mm_nt(ps_scr[part, :], g_all).astype(BF16)


def attend_back(queries, grad_mixed, kv_chunks, bias, lse):
    rows, width = queries.shape
    chunks, keys = len(kv_chunks), kv_chunks[0].shape[0]
    work = 10 * H * rows * chunks * keys * HD
    q_spec = pl.BlockSpec((rows, PAIR_Q), lambda j: (0, j))
    return pl.pallas_call(
        functools.partial(attend_back_kernel, chunks),
        grid=(PAIRS,),
        in_specs=[q_spec, q_spec]
        + kv_specs(chunks, keys)
        + [
            pl.BlockSpec((chunks * keys, rows), lambda j: (0, 0)),
            pl.BlockSpec((1, 8, rows), lambda j: (j, 0, 0)),
        ],
        out_specs=[q_spec] + [pl.BlockSpec((2, keys, PAIR_K), lambda j: (0, 0, j))] * chunks,
        out_shape=[jax.ShapeDtypeStruct(queries.shape, BF16)]
        + [jax.ShapeDtypeStruct((2, keys, KV * HD), BF16)] * chunks,
        scratch_shapes=[
            pltpu.VMEM((2, chunks * keys, rows), F32),
            pltpu.VMEM((2, chunks * keys, rows), F32),
            pltpu.VMEM((chunks * keys, 2 * GROUP * rows), BF16),
            pltpu.VMEM((chunks * keys, 2 * GROUP * rows), BF16),
        ],
        compiler_params=pltpu.CompilerParams(vmem_limit_bytes=40 * 1024 * 1024),
        cost_estimate=pl.CostEstimate(
            flops=6 * work, bytes_accessed=8 * 1024 * 1024, transcendentals=work // (10 * HD)
        ),
        name="path_attention_back",
    )(queries, grad_mixed, *kv_chunks, *kv_chunks, bias, lse)


def ancestry(parents_in):
    count = parents_in.shape[-1]
    labels = jnp.arange(count, dtype=jnp.int32)
    reach = (parents_in[..., :, None] == labels) | (labels[:, None] == labels)
    steps = 1
    while steps < count:
        reach = jnp.any(reach[..., :, :, None] & reach[..., None, :, :], axis=-2)
        steps *= 2
    return reach


def mask_bias(parents, valid, dp_index, n_dp, rows):
    micro = parents.shape[0]
    per = rows // BLOCK
    reach = lax.dynamic_slice_in_dim(ancestry(parents), dp_index * per, per, 1)
    early = (n_dp - 1) * per
    reach = jnp.pad(reach, ((0, 0), (0, 0), (early, 0)))
    reach = lax.dynamic_slice_in_dim(reach, dp_index * per, n_dp * per, 2)
    ok = jnp.pad(valid > 0, ((0, 0), (early * BLOCK, 0)))
    ok = lax.dynamic_slice_in_dim(ok, dp_index * rows, n_dp * rows, 1)
    by_key = jnp.repeat(jnp.swapaxes(reach, 1, 2), BLOCK, axis=1)
    shape = (micro, n_dp * rows, rows)
    key = lax.broadcasted_iota(jnp.int32, shape, 1) - (n_dp - 1) * rows
    query = lax.broadcasted_iota(jnp.int32, shape, 2)
    onpath = jnp.zeros(shape, bool)
    for i in range(per):
        onpath = onpath | ((query // BLOCK == i) & by_key[:, :, i : i + 1])
    allowed = onpath & (key <= query) & (ok[:, :, None] | (key == query))
    return jnp.where(allowed, 0.0, NEGATIVE).astype(F32)


def expert_kernel(block, has_prev, has_acc, last, *refs):
    refs = list(refs)

    def take(n):
        out = refs[:n]
        del refs[:n]
        return out

    h_refs, c_refs = take(4), take(4)
    gate_ref, wgu_ref, wd_ref = take(3)
    prev = take(4) if has_prev else None
    acc_in = take(2) if has_acc else None
    y_sib, y_own, gh_sib, gh_own, dwgu_ref, dwd_ref = take(6)
    hb, cb, yb, gb, acc_gu, acc_d, sem_in, sem_out, sem_acc = take(9)
    if has_prev:
        yp, gp, sem_prev = take(3)
    lead = h_refs[0].shape[0]
    half = (lead + h_refs[1].shape[0]) // block
    steps = 2 * half

    def fetch_tokens(refs, buffer, sem, at, slot):
        head, tail = refs

        @pl.when(at == 0)
        def _():
            rest = block - lead
            pltpu.make_async_copy(head, buffer.at[slot, pl.ds(0, lead)], sem).start()
            pltpu.make_async_copy(
                tail.at[pl.ds(0, rest)], buffer.at[slot, pl.ds(lead, rest)], sem
            ).start()

        @pl.when(at > 0)
        def _():
            rows = pl.ds(pl.multiple_of(at * block - lead, lead), block)
            pltpu.make_async_copy(tail.at[rows], buffer.at[slot], sem).start()

    def fetch_side(side, at, slot):
        fetch_tokens(h_refs[2 * side : 2 * side + 2], hb, sem_in.at[0, slot], at, slot)
        fetch_tokens(c_refs[2 * side : 2 * side + 2], cb, sem_in.at[1, slot], at, slot)
        if has_prev:
            rows = pl.ds(pl.multiple_of(at * block, block), block)
            for n, buffer in enumerate((yp, gp)):
                pltpu.make_async_copy(
                    prev[2 * n + side].at[rows], buffer.at[slot], sem_prev.at[n, slot]
                ).start()

    def fetch(i, slot):
        @pl.when(i < half)
        def _():
            fetch_side(0, i, slot)

        @pl.when(i >= half)
        def _():
            fetch_side(1, i - half, slot)

    def fetched(slot):
        for n, buffer in enumerate((hb, cb)):
            pltpu.make_async_copy(buffer.at[slot], buffer.at[slot], sem_in.at[n, slot]).wait()
        if has_prev:
            for n, buffer in enumerate((yp, gp)):
                pltpu.make_async_copy(
                    buffer.at[slot], buffer.at[slot], sem_prev.at[n, slot]
                ).wait()

    def copies_out(y_ref, g_ref, at, slot):
        rows = pl.ds(pl.multiple_of(at * block, block), block)
        return (
            pltpu.make_async_copy(yb.at[slot], y_ref.at[rows], sem_out.at[0, slot]),
            pltpu.make_async_copy(gb.at[slot], g_ref.at[rows], sem_out.at[1, slot]),
        )

    def stored(slot):
        for copy in copies_out(y_own, gh_own, 0, slot):
            copy.wait()

    fetch(0, 0)
    if has_acc:
        acc_copies = [
            pltpu.make_async_copy(acc_in[0], acc_gu, sem_acc.at[0]),
            pltpu.make_async_copy(acc_in[1], acc_d, sem_acc.at[1]),
        ]
        for copy in acc_copies:
            copy.start()
    else:
        acc_gu[...] = jnp.zeros_like(acc_gu)
        acc_d[...] = jnp.zeros_like(acc_d)

    def step(i, carry):
        slot = lax.rem(i, 2)

        @pl.when(i + 1 < steps)
        def _():
            fetch(i + 1, 1 - slot)

        fetched(slot)

        @pl.when(i >= 2)
        def _():
            stored(slot)

        tokens = hb[slot]
        grads = cb[slot]
        scale = gate_ref[pl.ds(pl.multiple_of(i * block, block), block), :]
        gate_up = mm(tokens, wgu_ref[...])
        grad_act = mm_nt(grads, wd_ref[...]) * scale
        gate, up = gate_up[:, :FFE], gate_up[:, FFE:]
        sig = jax.nn.sigmoid(gate)
        silu = gate * sig
        act = (silu * up * scale).astype(BF16)
        grad_gate = grad_act * up * (sig + silu * (1.0 - sig))
        grad_gu = jnp.concatenate([grad_gate, grad_act * silu], axis=1).astype(BF16)
        y = mm(act, wd_ref[...])
        gh = mm_nt(grad_gu, wgu_ref[...])
        if has_prev:
            y = y + yp[slot].astype(F32)
            gh = gh + gp[slot].astype(F32)
        yb[slot] = y.astype(BF16)
        gb[slot] = gh.astype(BF16)

        @pl.when(i < half)
        def _():
            for copy in copies_out(y_sib, gh_sib, i, slot):
                copy.start()

        @pl.when(i >= half)
        def _():
            for copy in copies_out(y_own, gh_own, i - half, slot):
                copy.start()

        if has_acc:

            @pl.when(i == 0)
            def _():
                for copy in acc_copies:
                    copy.wait()

        acc_d[...] += mm_tn(act, grads)
        acc_gu[...] += mm_tn(tokens, grad_gu)
        return carry

    lax.fori_loop(0, steps, step, 0)
    stored(steps % 2)
    stored((steps - 1) % 2)
    if last:
        dwgu_ref[...] = acc_gu[...].astype(BF16)
        dwd_ref[...] = acc_d[...].astype(BF16)
    else:
        out = [
            pltpu.make_async_copy(acc_gu, dwgu_ref, sem_acc.at[0]),
            pltpu.make_async_copy(acc_d, dwd_ref, sem_acc.at[1]),
        ]
        for copy in out:
            copy.start()
        for copy in out:
            copy.wait()


def expert_pass(h_all, c_all, gates, wgu, wd, previous, totals, last, block=512):
    rows = h_all[0].shape[0] + h_all[1].shape[0]
    width = h_all[0].shape[1]
    hidden = wd.shape[0]
    far = pl.BlockSpec(memory_space=pl.ANY)
    near = pl.BlockSpec(memory_space=pltpu.VMEM)
    token_out = jax.ShapeDtypeStruct((rows, width), BF16)
    token_buffer = pltpu.VMEM((2, block, width), BF16)
    grad_type = BF16 if last else F32
    scratch = [token_buffer] * 4 + [
        pltpu.VMEM((width, 2 * hidden), F32),
        pltpu.VMEM((hidden, width), F32),
        pltpu.SemaphoreType.DMA((2, 2)),
        pltpu.SemaphoreType.DMA((2, 2)),
        pltpu.SemaphoreType.DMA((2,)),
    ]
    extra, aliases = [], {}
    if previous is not None:
        scratch += [token_buffer] * 2 + [pltpu.SemaphoreType.DMA((2, 2))]
        aliases = {11 + n: n for n in range(4)}
        extra += list(previous)
    if totals is not None:
        extra += list(totals)
    return pl.pallas_call(
        functools.partial(
            expert_kernel, block, previous is not None, totals is not None, last
        ),
        in_specs=[far] * 8 + [near] * 3 + [far] * len(extra),
        out_specs=[far] * 4 + [near if last else far] * 2,
        out_shape=[token_out] * 4
        + [
            jax.ShapeDtypeStruct((width, 2 * hidden), grad_type),
            jax.ShapeDtypeStruct((hidden, width), grad_type),
        ],
        scratch_shapes=scratch,
        input_output_aliases=aliases,
        compiler_params=pltpu.CompilerParams(vmem_limit_bytes=60 * 1024 * 1024),
        cost_estimate=pl.CostEstimate(
            flops=18 * 2 * rows * width * hidden,
            bytes_accessed=2 * 12 * rows * width,
            transcendentals=2 * rows * hidden,
        ),
        name="expert_pass",
    )(*h_all, *c_all, gates, wgu, wd, *extra)


def join(*items):
    return lax.optimization_barrier(items)


class Plane:
    def __init__(self, count):
        self.count = count
        self.chips = count // 2

    def swap(self, x):
        return lax.ppermute(x, "expert", [(i, i ^ 1) for i in range(self.count)])

    def cross(self, x, k):
        return lax.ppermute(x, "expert", [(i, i ^ (2 * k)) for i in range(self.count)])

    def crosses(self, x, ks=None):
        return [self.cross(x, k) for k in (ks or range(1, self.chips))]

    def sums(self, own, arrived):
        rows = own.shape[0] // self.chips
        parts = []
        for k in range(self.chips):
            here = slice(k * rows, (k + 1) * rows)
            parts.append(own[here].astype(F32) + arrived[here].astype(F32))
        return [parts[0]] + [p.astype(BF16) for p in parts[1:]]

    def send(self, parts, ks=None):
        return [self.cross(parts[k], k) for k in (ks or range(1, self.chips))]


def added(first, others):
    for x in others:
        first = first + x.astype(F32)
    return first


def dp_cross(x, k, n_dp):
    return lax.ppermute(x, "dp", [(i, i ^ k) for i in range(n_dp)])


def dp_along(x, by, n_dp):
    pairs = [(i, i + by) for i in range(n_dp) if 0 <= i + by < n_dp]
    return lax.ppermute(x, "dp", pairs)


def over_dp(x, n_dp, dp_index):
    below, above = [x], [x]
    for _ in range(n_dp - 1):
        below.append(dp_along(below[-1], 1, n_dp))
        above.append(dp_along(above[-1], -1, n_dp))
    rows = x.shape[0]
    whole = jnp.zeros((n_dp * rows,) + x.shape[1:], x.dtype)
    for d in range(n_dp):
        piece = x if d == 0 else jnp.where(dp_index >= d, below[d], above[n_dp - d])
        at = lax.rem(dp_index - d + n_dp, n_dp) * rows
        whole = lax.dynamic_update_slice_in_dim(whole, piece, at, 0)
    return whole


def all_rows(plane, x, n_dp):
    me = lax.axis_index("expert")
    core, chip, dp_index = me % 2, me // 2, lax.axis_index("dp")
    line = jnp.zeros((n_dp,) + x.shape, x.dtype)
    for k in range(n_dp):
        piece = x if k == 0 else dp_cross(x, k, n_dp)
        line = lax.dynamic_update_index_in_dim(line, piece, dp_index ^ k, 0)
    blocks = [line] + plane.crosses(line)
    whole = jnp.zeros((n_dp, plane.chips, 2) + x.shape, x.dtype)
    for c, held in enumerate((blocks, plane.swap(jnp.stack(blocks)))):
        for k in range(plane.chips):
            at = (0, chip ^ k, core ^ c, 0, 0)
            whole = lax.dynamic_update_slice(whole, held[k][:, None, None], at)
    return whole.reshape((-1,) + x.shape[1:])


def sum_of_all(plane, grads, n_dp):
    rows, width = grads.shape
    chunk = rows // (n_dp * plane.count)
    split = grads.reshape(n_dp, plane.chips, 2, chunk, width)
    me = lax.axis_index("expert")
    core, chip, dp_index = me % 2, me // 2, lax.axis_index("dp")
    own = lax.dynamic_index_in_dim(split, core, 2, keepdims=False)
    other = lax.dynamic_index_in_dim(split, 1 - core, 2, keepdims=False)
    both = (own.astype(F32) + plane.swap(other).astype(F32)).astype(BF16)

    def of_chip(k):
        return lax.dynamic_index_in_dim(both, chip ^ k, 1, keepdims=False)

    parts = [of_chip(k) for k in range(plane.chips)]
    total = added(parts[0].astype(F32), plane.send(parts))
    small = total.astype(BF16)
    out = lax.dynamic_index_in_dim(total, dp_index, 0, keepdims=False)
    for k in range(1, n_dp):
        piece = lax.dynamic_index_in_dim(small, dp_index ^ k, 0, keepdims=False)
        out = out + dp_cross(piece, k, n_dp).astype(F32)
    return out


def body(
    n_dp,
    n_expert,
    tokens,
    cotangent,
    parents,
    valid_mask,
    routes,
    route_gates,
    norm_gains,
    w_qkv,
    w_out,
    w_gate_up,
    w_down,
):
    both = ("dp", "expert")
    micro, _, rows, width = tokens.shape
    micros = range(micro)
    count = micro * rows
    top = routes.shape[-1]
    query_width = H * HD
    kv_width = KV * HD
    local_experts = w_gate_up.shape[0]
    experts = local_experts * n_expert
    plane = Plane(n_expert)
    dp_index = lax.axis_index("dp")

    gains_t = jnp.pad(norm_gains.T, ((0, 0), (0, 126)))
    first = lax.all_gather(
        jnp.concatenate([w_qkv, gains_t], axis=1), both, axis=0, tiled=True
    )
    gate_up_w = [over_dp(w_gate_up[0], n_dp, dp_index)]
    down_w = [over_dp(w_down[0], n_dp, dp_index)]
    for e in range(1, local_experts):
        gate_up_w.append(lax.all_gather(w_gate_up[e], "dp", axis=0, tiled=True))
        down_w.append(lax.all_gather(w_down[e], "dp", axis=0, tiled=True))
    w_out_t = all_rows(plane, w_out.T, n_dp)

    chosen = routes.reshape(count, top)[:, :, None] == jnp.arange(experts, dtype=jnp.int32)
    table = jnp.sum(jnp.where(chosen, route_gates.reshape(count, top)[:, :, None], 0.0), axis=1)
    table = table.T.reshape(n_expert, local_experts, micro, rows)
    table = lax.all_to_all(table, "expert", split_axis=0, concat_axis=0, tiled=True)
    order = [2 * k + 1 for k in range(plane.chips)] + [2 * k for k in range(plane.chips)]
    table = jnp.take(table, lax.axis_index("expert") ^ jnp.array(order, jnp.int32), axis=0)
    gates = [[table[:, e, m].reshape(-1, 1) for m in micros] for e in range(local_experts)]
    bias = mask_bias(
        parents.reshape(micro, -1), valid_mask.reshape(micro, -1), dp_index, n_dp, rows
    )
    x_in = [tokens[m, 0].astype(F32) for m in micros]
    grad_out = [cotangent[m, 0] for m in micros]
    first, gate_up_w[0], down_w[0], w_out_t, gates, bias = join(
        first, gate_up_w[0], down_w[0], w_out_t, gates, bias
    )

    qkv_width = w_qkv.shape[1]
    w_q, w_kv = first[:, :query_width], first[:, query_width:qkv_width]
    gain_in = first[:, qkv_width].astype(F32)
    gain_mid = first[:, qkv_width + 1].astype(F32)
    h_in = [rms_norm(x, gain_in).astype(BF16) for x in x_in]
    kv = [mm(h, w_kv).astype(BF16) for h in h_in]
    queries = [mm(h, w_q).astype(BF16) for h in h_in]
    lags = range(1, n_dp)
    middle = n_dp // 2

    def lagged(x, ds):
        return {d: dp_along(x, d, n_dp) for d in ds}

    def in_order(x, held):
        return [held[d] for d in reversed(lags)] + [x]

    def attention(m):
        mixed, total = attend(queries[m], kv_chunks[m], bias[m])
        middle_x = x_in[m] + mm_nt(mixed, w_out_t)
        return mixed, total, middle_x, rms_norm(middle_x, gain_mid).astype(BF16)

    near, far = list(range(1, plane.chips - 1)), [plane.chips - 1]
    held_0, kv[1], queries, c_cross_0 = join(
        lagged(kv[0], lags), kv[1], queries, plane.crosses(grad_out[0])
    )
    kv_chunks = [in_order(kv[0], held_0)]
    held_1 = lagged(kv[1], [middle])
    c_others = [jnp.concatenate(c_cross_0, axis=0)]
    c_swapped = [[plane.swap(grad_out[0]), plane.swap(c_others[0])]]
    state_0, held_1, c_swapped = join(attention(0), held_1, c_swapped)
    h_mid = [state_0[3]]
    held_1.update(lagged(kv[1], [d for d in lags if d != middle]))
    held_1, h_far, h_swap = join(
        held_1, plane.crosses(h_mid[0], far), plane.swap(h_mid[0])
    )
    kv_chunks.append(in_order(kv[1], held_1))
    state_1, h_near = join(attention(1), plane.crosses(h_mid[0], near))
    h_mid.append(state_1[3])
    attn, lse, x_mid, _ = zip(state_0, state_1)

    def run(e, m, gate):
        *out, d_gu, d_d = expert_pass(
            h_all[m],
            c_all[m],
            gate,
            gate_up_w[e],
            down_w[e],
            carried[m],
            totals[e],
            m + 1 == micro,
        )
        return out, (d_gu, d_d)

    totals, carried = [None] * local_experts, [None] * micro
    h_others = jnp.concatenate(h_near + h_far, axis=0)
    h_all = [[h_swap, plane.swap(h_others), h_mid[0], h_others], None]
    c_all = [c_swapped[0] + [grad_out[0], c_others[0]], None]
    (carried[0], totals[0]), h_cross, h_swap, c_swap = join(
        run(0, 0, gates[0][0]),
        plane.crosses(h_mid[1]),
        plane.swap(h_mid[1]),
        plane.swap(grad_out[1]),
    )
    h_others = jnp.concatenate(h_cross, axis=0)
    gate, h_others, c_sent = join(gates[1][0], h_others, grad_out[1])
    (carried[0], totals[1]), h_others_swap, c_cross = join(
        run(1, 0, gate), plane.swap(h_others), plane.crosses(c_sent)
    )
    h_all[1] = [h_swap, h_others_swap, h_mid[1], h_others]
    c_others = jnp.concatenate(c_cross, axis=0)
    y_sib_0, y_own_0, gh_sib_0, gh_own_0 = carried[0]
    arrived, c_others_swap, c_others = join(plane.swap(gh_sib_0), plane.swap(c_others), c_others)
    c_all[1] = [c_swap, c_others_swap, grad_out[1], c_others]
    gh_parts_0 = plane.sums(gh_own_0, arrived)
    gate, gh_parts_0 = join(gates[0][1], gh_parts_0)
    (carried[1], totals[0]), gh_sent_0, arrived = join(
        run(0, 1, gate), plane.send(gh_parts_0), plane.swap(y_sib_0)
    )
    y_parts_0 = plane.sums(y_own_0, arrived)
    gate, y_parts_0 = join(gates[1][1], y_parts_0)
    (carried[1], totals[1]), y_sent_0 = join(run(1, 1, gate), plane.send(y_parts_0))
    y_sib_1, y_own_1, gh_sib_1, gh_own_1 = carried[1]

    def middle_back(m, grad_h_mid):
        part, gain_part = rms_back(x_mid[m], gain_mid, grad_h_mid)
        grad_x_mid = grad_out[m].astype(F32) + part
        branch = grad_x_mid.astype(BF16)
        return grad_x_mid, gain_part, branch, mm(branch, w_out_t).astype(BF16)

    def attention_back(m, grad_mixed):
        dq, *dkv = attend_back(queries[m], grad_mixed, kv_chunks[m], bias[m], lse[m])
        return dq, dkv

    def returned(dkv, ds):
        return {d: dp_along(dkv[n_dp - 1 - d], -d, n_dp) for d in ds}

    def kv_total(dkv, held):
        return added(dkv[-1].astype(F32), [held[d] for d in lags]).astype(BF16)

    back_0, arrived, y_sib_1 = join(
        middle_back(0, added(gh_parts_0[0], gh_sent_0)), plane.swap(gh_sib_1), y_sib_1
    )
    gh_parts_1 = plane.sums(gh_own_1, arrived)
    grad_mixed, gh_parts_1 = join(back_0[3], gh_parts_1)
    (grad_q_0, dkv_0), gh_far, arrived = join(
        attention_back(0, grad_mixed), plane.send(gh_parts_1, far), plane.swap(y_sib_1)
    )
    held_0 = returned(dkv_0, [middle])
    y_parts_1 = plane.sums(y_own_1, arrived)
    held_0, gh_near, y_parts_1 = join(held_0, plane.send(gh_parts_1, near), y_parts_1)
    held_0.update(returned(dkv_0, [d for d in lags if d != middle]))

    def last_back():
        back = middle_back(1, added(gh_parts_1[0], gh_near + gh_far))
        return back, attention_back(1, back[3])

    (back_1, (grad_q_1, dkv_1)), held_0, y_sent_1 = join(
        last_back(), held_0, plane.send(y_parts_1)
    )
    grad_kv = [kv_total(dkv_0, held_0)]
    x_out = [
        x_mid[0] + added(y_parts_0[0], y_sent_0),
        x_mid[1] + added(y_parts_1[0], y_sent_1),
    ]
    grad_x_mid, grad_gain_mid, grad_branch, _ = zip(back_0, back_1)
    grad_q = [grad_q_0, grad_q_1]

    def weight_grad(left, right):
        total = sum(mm_tn(a, b) for a, b in zip(left, right))
        return total.astype(BF16)

    held_1, grad_wout_s, grad_wq_s = join(
        returned(dkv_1, lags),
        sum_of_all(plane, weight_grad(grad_branch, attn), n_dp),
        sum_of_all(plane, weight_grad(h_in, grad_q), n_dp),
    )
    grad_kv.append(kv_total(dkv_1, held_1))
    grad_wkv = jnp.concatenate(
        [weight_grad(h_in, [g[n] for g in grad_kv]) for n in range(2)], axis=1
    )
    grad_wkv_s = sum_of_all(plane, grad_wkv, n_dp)
    grad_x, grad_gain_in = [], 0.0
    for m in micros:
        grad_h_in = (
            mm_nt(grad_q[m], w_q)
            + mm_nt(grad_kv[m][0], w_kv[:, :kv_width])
            + mm_nt(grad_kv[m][1], w_kv[:, kv_width:])
        )
        part, gain_part = rms_back(x_in[m], gain_in, grad_h_in)
        grad_x.append((grad_x_mid[m] + part).astype(BF16))
        grad_gain_in = grad_gain_in + gain_part
    world = n_dp * n_expert
    gain_grads = jnp.stack([grad_gain_in, sum(grad_gain_mid)]).reshape(2, world, width // world)
    gain_grads = jnp.swapaxes(gain_grads, 0, 1)
    gain_grads = lax.all_to_all(gain_grads, both, split_axis=0, concat_axis=0, tiled=True)
    reduced = [
        [lax.psum_scatter(t, "dp", scatter_dimension=0, tiled=True) for t in pair]
        for pair in totals
    ]
    reduced, gain_grads = join(reduced, gain_grads)
    grad_gu_s, grad_down_s = (
        jnp.stack([pair[n].astype(F32) for pair in reduced]) for n in range(2)
    )
    return (
        jnp.stack([x.astype(BF16) for x in x_out])[:, None],
        jnp.stack(grad_x)[:, None],
        jnp.sum(gain_grads, axis=0),
        jnp.concatenate([grad_wq_s, grad_wkv_s], axis=1),
        grad_wout_s.T,
        grad_gu_s,
        grad_down_s,
    )


def solution(mesh):
    tokens_spec = P(None, "expert", "dp", None)
    experts_spec = P("expert", "dp", None)
    rows_spec = P(("dp", "expert"), None)
    columns_spec = P(None, ("dp", "expert"))
    return jax.shard_map(
        functools.partial(body, mesh.shape["dp"], mesh.shape["expert"]),
        mesh=mesh,
        in_specs=(
            tokens_spec,
            tokens_spec,
            P(None, "expert", None),
            P(None, "expert", None),
            tokens_spec,
            tokens_spec,
            columns_spec,
            rows_spec,
            columns_spec,
            experts_spec,
            experts_spec,
        ),
        out_specs=(
            tokens_spec,
            tokens_spec,
            columns_spec,
            rows_spec,
            columns_spec,
            experts_spec,
            experts_spec,
        ),
        check_vma=False,
    )
```

time: 1860 us -> 906 us (0.49)
  waiting for transfers between devices: 986 us -> 295 us
  local copies, waits for them, and re-layouts: 328 us -> 61.7 us
  matrix products: 318 us -> 51.9 us
  Pallas kernels: 0 us -> 242 us
  starting transfers between devices: 31.6 us -> 157 us
  other arithmetic: 138 us -> 70.4 us
  blocking collectives: 43.3 us -> 0 us
    all_to_all x4 -> x2, waiting for transfers between devices: 571 us -> 0.01 us  [the longest x1 0.01 us: body(): lax.all_to_all(table, 'expert', split_axis=0, concat_axis=0, tiled=True)]
    reduce_scatter x6 -> x4, waiting for transfers between devices: 308 us -> 0.01 us  [body(): lax.psum_scatter(t, 'dp', scatter_dimension=0, tiled=True)]
    ppermute x0 -> x88, waiting for transfers between devices: none -> 285 us  [the longest x24 157 us: dp_along(): return lax.ppermute(x, 'dp', pairs)]
    dot_general x18 -> x22, matrix products: 318 us -> 51.9 us  [the longest x8 25.8 us: mm_nt(): lax.dot_general(a, b, (((1,), (1,)), ((), ())), preferred_element_type=F32)]
    pallas_call x0 -> x8, Pallas kernels: none -> 242 us  [the longest x4 163 us: expert_pass(): pl.pallas_call(functools.partial(expert_kernel, block, previous is not No...]
    ppermute x0 -> x88, starting transfers between devices: none -> 145 us  [the longest x24 74.9 us: dp_along(): return lax.ppermute(x, 'dp', pairs)]
    all_gather x6 -> x3, waiting for transfers between devices: 105 us -> 9.29 us  [the longest x1 9.29 us: body(): gate_up_w.append(lax.all_gather(w_gate_up[e], 'dp', axis=0, tiled=True))]
    convert_element_type x4 -> x0, local copies, waits for them, and re-layouts: 74.8 us -> none  [the longest x1 34.8 us: body(): expert_out = jnp.einsum('erf,efd->erd', activation, down_weight, preferre...]
  transfers between devices with their start and end apart: 17 -> 97, of which waited for: 9 -> 25; matrix products, arithmetic and copies ran while one was open for 31% -> 19% of each run, Pallas kernels for 0% -> 27%
where the time goes in v1:
time: 906 us; the launch traced here: 897 us
  waiting for transfers between devices  295 us (33%)
  Pallas kernels  242 us (27%)
  starting transfers between devices  157 us (17%)
  other arithmetic  70.4 us (8%)
  local copies, waits for them, and re-layouts  61.7 us (7%)
  matrix products  51.9 us (6%)
  between operations  18.2 us (2%)
    pallas_call x4, Pallas kernels, expert_pass(): pl.pallas_call(functools.partial(expert_kernel, block, previous is not No...  163 us
    ppermute x24, waiting for transfers between devices, dp_along(): return lax.ppermute(x, 'dp', pairs)  157 us
    ppermute x36, waiting for transfers between devices, cross(): lax.ppermute(x, 'expert', [(i, i ^ 2 * k) for i in range(self.count)])  76.6 us
    ppermute x24, starting transfers between devices, dp_along(): return lax.ppermute(x, 'dp', pairs)  74.9 us
    pallas_call x2, Pallas kernels, attend_back(): pl.pallas_call(functools.partial(attend_back_kernel, chunks), grid=(PAIRS...  48.6 us
    ppermute x36, starting transfers between devices, cross(): lax.ppermute(x, 'expert', [(i, i ^ 2 * k) for i in range(self.count)])  45.6 us
    ppermute x12, waiting for transfers between devices, dp_cross(): return lax.ppermute(x, 'dp', [(i, i ^ k) for i in range(n_dp)])  44 us
    pallas_call x2, Pallas kernels, attend(): pl.pallas_call(functools.partial(attend_kernel, chunks), grid=(PAIRS,), i...  30.2 us
  transfers between devices with their start and end apart: 97, of which 25 were waited for; matrix products, arithmetic and copies ran while one was open for 19% of the time, Pallas kernels for 27%

profile of v1, /device:TPU:0, one launch (start us, length us, event | category | flops | bytes accessed | tf_op | source)
XLA Modules:
  0.0 896.6 jit_solution(1582438430730458914)
XLA Ops:
  19.7 5.3 collective-permute-start.6
  25.7 3.9 all-to-all-start
  50.0 4.6 collective-permute-start
  54.6 9.8 %collective-permute-done.15 = bf16[4,48,1536]{2,1,0:T(8,128)(2,1)S(1)} collective-permute-done((bf16[4,48,1536]{2,1,0:T(8,128)(2,1)S(1)}, bf16[4,48,1536]{2,1,0:T(8,128)(2,1)S(1)}, u32[]{:S(2)}, u32[]{:S(2)}) %collective-permute-start.15) | collective-permute-done | bytes 589856 | tf_op jit(solution)/shard_map/ppermute | solution.py:452
  65.8 4.6 collective-permute-start.10
  70.3 7.4 collective-permute-done.17
  81.2 18.3 %collective-permute-done.8 = bf16[128,1536]{1,0:T(8,128)(2,1)S(1)} collective-permute-done((bf16[128,1536]{1,0:T(8,128)(2,1)}, bf16[128,1536]{1,0:T(8,128)(2,1)S(1)}, u32[]{:S(2)}, u32[]{:S(2)}) %collective-permute-start.8) | collective-permute-done | bytes 393248 | tf_op jit(solution)/shard_map/ppermute | solution.py:481
  103.6 4.6 collective-permute-start.4
  108.2 23.7 %collective-permute-done.9 = bf16[128,1536]{1,0:T(8,128)(2,1)S(1)} collective-permute-done((bf16[128,1536]{1,0:T(8,128)(2,1)S(1)}, bf16[128,1536]{1,0:T(8,128)(2,1)S(1)}, u32[]{:S(2)}, u32[]{:S(2)}) %collective-permute-start.9) | collective-permute-done | bytes 393248 | tf_op jit(solution)/shard_map/ppermute | solution.py:481
  137.8 5.0 collective-permute-done.11
  143.4 4.4 collective-permute-start.5
  149.7 6.8 collective-permute-done.3
  171.9 4.4 collective-permute-start.19
  176.3 4.2 collective-permute-start.20
  188.6 11.3 %collective-permute-done.20.refs_1_.refs_5_ = bf16[256,1024]{1,0:T(8,128)(2,1)S(1)} collective-permute-done((bf16[256,1024]{1,0:T(8,128)(2,1)S(1)}, bf16[256,1024]{1,0:T(8,128)(2,1)S(1)}, u32[]{:S(2)}, u32[]{:S(2)}) %collective-permute-start.20) | collective-permute-done | bytes 524320 | tf_op jit(solution)/shard_map/ppermute | solution.py:481
  199.9 7.4 collective-permute-done.21.refs_0_.refs_4_
  209.9 10.3 %collective-permute-start.25 = (bf16[256,1024]{1,0:T(8,128)(2,1)S(1)}, bf16[256,1024]{1,0:T(8,128)(2,1)S(1)}, u32[]{:S(2)}, u32[]{:S(2)}) collective-permute-start(bf16[256,1024]{1,0:T(8,128)(2,1)S(1)} %fusion.87.refs_3_.refs_7_), channel_id=1, source_target_pairs={{0,16},{8,24},{1,17},{9,25},{2,18},{10,26},{3,19},{11,27},{4,20},{... | collective-permute-start | bytes 1572872 | tf_op jit(solution)/shard_map/ppermute | solution.py:481
  220.3 15.1 %path_attention.2 = (bf16[256,1536]{1,0:T(8,128)(2,1)S(1)}, f32[4,8,256]{2,1,0:T(8,128)S(1)}) custom-call(bf16[256,1536]{1,0:T(8,128)(2,1)S(1)} %fusion.31.q_ref, bf16[256,1024]{1,0:T(8,128)(2,1)S(1)} %collective-permute-done.21.refs_0_.refs_4_, bf16[256,1024]{1,0:T(8,128)(2,1)S(1)} %collective-permute-done.20.refs_1_.refs_5_, ...), custom_call_target="tpu_custom_call" | custom-call | flops 12884901888 | bytes 4194304 | tf_op jit(solution)/shard_map/path_attention/pallas_call | solution.py:106
  235.4 4.1 multiply_reduce_fusion.7
  242.6 10.8 %collective-permute-start.28 = (bf16[256,1024]{1,0:T(8,128)(2,1)S(1)}, bf16[256,1024]{1,0:T(8,128)(2,1)S(1)}, u32[]{:S(2)}, u32[]{:S(2)}) collective-permute-start(bf16[256,1024]{1,0:T(8,128)(2,1)S(1)} %fusion.87.refs_3_.refs_7_), channel_id=1, source_target_pairs={{0,8},{8,16},{16,24},{1,9},{9,17},{17,25},{2,10},{10,18},{18,26},{... | collective-permute-start | bytes 1572872 | tf_op jit(solution)/shard_map/ppermute | solution.py:481
  255.0 16.2 %collective-permute-done.28.refs_2_.refs_6_ = bf16[256,1024]{1,0:T(8,128)(2,1)S(1)} collective-permute-done((bf16[256,1024]{1,0:T(8,128)(2,1)S(1)}, bf16[256,1024]{1,0:T(8,128)(2,1)S(1)}, u32[]{:S(2)}, u32[]{:S(2)}) %collective-permute-start.28) | collective-permute-done | bytes 524320 | tf_op jit(solution)/shard_map/ppermute | solution.py:481
  271.2 22.1 %collective-permute-done.29.refs_0_.refs_4_ = bf16[256,1024]{1,0:T(8,128)(2,1)S(1)} collective-permute-done((bf16[256,1024]{1,0:T(8,128)(2,1)S(1)}, bf16[256,1024]{1,0:T(8,128)(2,1)S(1)}, u32[]{:S(2)}, u32[]{:S(2)}) %collective-permute-start.29) | collective-permute-done | bytes 524320 | tf_op jit(solution)/shard_map/ppermute | solution.py:481
  294.4 15.1 %path_attention.3 = (bf16[256,1536]{1,0:T(8,128)(2,1)S(1)}, f32[4,8,256]{2,1,0:T(8,128)S(1)}) custom-call(bf16[256,1536]{1,0:T(8,128)(2,1)S(1)} %copy-done.24, bf16[256,1024]{1,0:T(8,128)(2,1)S(1)} %collective-permute-done.29.refs_0_.refs_4_, bf16[256,1024]{1,0:T(8,128)(2,1)S(1)} %collective-permute-done.25.refs_1_.refs_5_, ...), custom_call_target="tpu_custom_call" | custom-call | flops 12884901888 | bytes 4194304 | tf_op jit(solution)/shard_map/path_attention/pallas_call | solution.py:106
  309.5 4.1 multiply_reduce_fusion.6
  324.8 40.2 %expert_pass.4 = (bf16[1024,1536]{1,0:T(8,128)(2,1)}, bf16[1024,1536]{1,0:T(8,128)(2,1)}, bf16[1024,1536]{1,0:T(8,128)(2,1)}, bf16[1024,1536]{1,0:T(8,128)(2,1)}...) custom-call(bf16[256,1536]{1,0:T(8,128)(2,1)} %collective-permute-done.31.refs_0_, ...), custom_call_target="tpu_custom_call" | custom-call | flops 28991029248 | bytes 37748736 | tf_op jit(solution)/shard_map/expert_pass/pallas_call | solution.py:416
  373.3 9.3 %all-gather.8.cloned.1.call-done = bf16[1,1536,1024]{2,1,0:T(8,128)(2,1)} async-done(((bf16[1,384,1024]{2,1,0:T(8,128)(2,1)}), bf16[1,1536,1024]{2,1,0:T(8,128)(2,1)}) %all-gather.8.cloned.1.call-update) | async-done | bytes 3145744 | tf_op jit(solution)/shard_map/all_gather | solution.py:571
  382.6 40.7 %expert_pass.5 = (bf16[1024,1536]{1,0:T(8,128)(2,1)}, bf16[1024,1536]{1,0:T(8,128)(2,1)}, bf16[1024,1536]{1,0:T(8,128)(2,1)}, bf16[1024,1536]{1,0:T(8,128)(2,1)}...) custom-call(bf16[256,1536]{1,0:T(8,128)(2,1)} %collective-permute-do, ...), custom_call_target="tpu_custom_call", output_to_operand_aliasing={{0}: (11, {}), {1}: (12, {}), {2}: (13, {}), {3}: (14, {})} | custom-call | flops 28991029248 | bytes 37748736 | tf_op jit(solution)/shard_map/expert_pass/pallas_call | solution.py:416
  427.7 8.0 collective-permute-done.45.refs_5_
  443.6 40.6 %expert_pass.6 = (bf16[1024,1536]{1,0:T(8,128)(2,1)}, bf16[1024,1536]{1,0:T(8,128)(2,1)}, bf16[1024,1536]{1,0:T(8,128)(2,1)}, bf16[1024,1536]{1,0:T(8,128)(2,1)}...) custom-call(bf16[256,1536]{1,0:T(8,128)(2,1)} %collective-permute-done.38.refs_0_, ...), custom_call_target="tpu_custom_call" | custom-call | flops 28991029248 | bytes 37748736 | tf_op jit(solution)/shard_map/expert_pass/pallas_call | solution.py:416
  484.3 5.7 add_convert_fusion.8
  495.0 41.7 %expert_pass.7 = (bf16[1024,1536]{1,0:T(8,128)(2,1)}, bf16[1024,1536]{1,0:T(8,128)(2,1)}, bf16[1024,1536]{1,0:T(8,128)(2,1)}, bf16[1024,1536]{1,0:T(8,128)(2,1)}...) custom-call(bf16[256,1536]{1,0:T(8,128)(2,1)} %collective-permute-do, ...), custom_call_target="tpu_custom_call", output_to_operand_aliasing={{0}: (11, {}), {1}: (12, {}), {2}: (13, {}), {3}: (14, {})} | custom-call | flops 28991029248 | bytes 37748736 | tf_op jit(solution)/shard_map/expert_pass/pallas_call | solution.py:416
  540.6 5.0 multiply_reduce_fusion.3
  547.3 4.1 convolution_convert_fusion.1.g_ref
  559.3 24.2 %path_attention_back.2 = (bf16[256,1536]{1,0:T(8,128)(2,1)S(1)}, bf16[2,256,512]{2,1,0:T(8,128)(2,1)S(1)}, bf16[2,256,512]{2,1,0:T(8,128)(2,1)S(1)}, bf16[2,256,...) custom-call(bf16[256,1536]{1,0:T(8,128)(2,1)S(1)} %copy-done.27, bf16[256,1536]{1,0:T(8,128)(2,1)S(1)} %convolution_convert_fusion.1.g_ref, ...), custom_call_target="tpu_custom_call" | custom-call | flops 24159191040 | bytes 8388608 | tf_op jit(solution)/shard_map/path_attention_back/pallas_call | solution.py:179
  593.4 41.3 %collective-permute-done.56 = bf16[2,256,512]{2,1,0:T(8,128)(2,1)S(1)} collective-permute-done((bf16[2,256,512]{2,1,0:T(8,128)(2,1)S(1)}, bf16[2,256,512]{2,1,0:T(8,128)(2,1)S(1)}, u32[]{:S(2)}, u32[]{:S(2)}) %collective-permute-start.56) | collective-permute-done | bytes 524320 | tf_op jit(solution)/shard_map/ppermute | solution.py:481
  645.3 24.5 %path_attention_back.3 = (bf16[256,1536]{1,0:T(8,128)(2,1)S(1)}, bf16[2,256,512]{2,1,0:T(8,128)(2,1)S(1)}, bf16[2,256,512]{2,1,0:T(8,128)(2,1)S(1)}, bf16[2,256,...) custom-call(bf16[256,1536]{1,0:T(8,128)(2,1)S(1)} %copy-done.25, bf16[256,1536]{1,0:T(8,128)(2,1)S(1)} %convolution_convert_fusion.g_ref, ...), custom_call_target="tpu_custom_call" | custom-call | flops 24159191040 | bytes 8388608 | tf_op jit(solution)/shard_map/path_attention_back/pallas_call | solution.py:179
  669.8 9.5 %collective-permute-done.62 = bf16[256,1536]{1,0:T(8,128)(2,1)S(1)} collective-permute-done((bf16[256,1536]{1,0:T(8,128)(2,1)S(1)}, bf16[256,1536]{1,0:T(8,128)(2,1)S(1)}, u32[]{:S(2)}, u32[]{:S(2)}) %collective-permute-start.62) | collective-permute-done | bytes 786464 | tf_op jit(solution)/shard_map/ppermute | solution.py:452
  716.9 9.2 %collective-permute-done.75 = bf16[4,48,1536]{2,1,0:T(8,128)(2,1)S(1)} collective-permute-done((bf16[4,48,1536]{2,1,0:T(8,128)(2,1)S(1)}, bf16[4,48,1536]{2,1,0:T(8,128)(2,1)S(1)}, u32[]{:S(2)}, u32[]{:S(2)}) %collective-permute-start.75) | collective-permute-done | bytes 589856 | tf_op jit(solution)/shard_map/ppermute | solution.py:452
  727.6 8.6 collective-permute-done.76
  736.2 4.9 collective-permute-start.70
  743.9 7.5 collective-permute-done.68
  752.4 9.9 %collective-permute-done.69 = bf16[4,48,1536]{2,1,0:T(8,128)(2,1)S(1)} collective-permute-done((bf16[4,48,1536]{2,1,0:T(8,128)(2,1)S(1)}, bf16[4,48,1536]{2,1,0:T(8,128)(2,1)S(1)}, u32[]{:S(2)}, u32[]{:S(2)}) %collective-permute-start.69) | collective-permute-done | bytes 589856 | tf_op jit(solution)/shard_map/ppermute | solution.py:452
  776.1 38.9 %collective-permute-done.72 = bf16[48,1536]{1,0:T(8,128)(2,1)S(1)} collective-permute-done((bf16[48,1536]{1,0:T(8,128)(2,1)S(1)}, bf16[48,1536]{1,0:T(8,128)(2,1)S(1)}, u32[]{:S(2)}, u32[]{:S(2)}) %collective-permute-start.72) | collective-permute-done | bytes 147488 | tf_op jit(solution)/shard_map/ppermute | solution.py:476
  820.3 4.6 copy.81
  831.9 4.0 fusion.25
  840.4 7.5 all-to-all-start.1
  866.0 9.1 %collective-permute-done.83 = bf16[4,48,1024]{2,1,0:T(8,128)(2,1)S(1)} collective-permute-done((bf16[4,48,1024]{2,1,0:T(8,128)(2,1)S(1)}, bf16[4,48,1024]{2,1,0:T(8,128)(2,1)S(1)}, u32[]{:S(2)}, u32[]{:S(2)}) %collective-permute-start.83) | collective-permute-done | bytes 393248 | tf_op jit(solution)/shard_map/ppermute | solution.py:452
  882.7 5.1 collective-permute-done.86
  (527 shorter events, 251.0 us)
Async XLA Ops:
  8.1 158.8 %all-gather.6.cloned.1.call-start = ((), (), s32[]{:S(2)}) async-start(), calls=%async_computation.6 | async-start | bytes 8515584 | tf_op jit(solution)/shard_map/all_gather | solution.py:565
  29.6 343.7 %all-gather.10.cloned.1.call-start = ((), (), s32[]{:S(2)}) async-start(), calls=%async_computation.12 | async-start | bytes 1966080 | tf_op jit(solution)/shard_map/all_gather | solution.py:572
  50.0 51.6 %collective-permute-start = (bf16[384,1024]{1,0:T(8,128)(2,1)S(1)}, bf16[384,1024]{1,0:T(8,128)(2,1)S(1)}, u32[]{:S(2)}, u32[]{:S(2)}) collective-permute-start(bf16[384,1024]{1,0:T(8,128)(2,1)S(1)} %copy-done.81), channel_id=1, source_target_pairs={{0,8},{8,16},{16,24},{1,9},{9,17},{17,25},{2,10},{10,18},{18,26},{... | collective-permute-start | bytes 2359304 | tf_op jit(solution)/shard_map/ppermute | solution.py:481
  65.8 37.9 %collective-permute-start.10 = (bf16[128,1536]{1,0:T(8,128)(2,1)}, bf16[128,1536]{1,0:T(8,128)(2,1)S(1)}, u32[]{:S(2)}, u32[]{:S(2)}) collective-permute-start(bf16[128,1536]{1,0:T(8,128)(2,1)} %collective-permute-done.6), channel_id=1, source_target_pairs={{0,8},{8,16},{16,24},{1,9},{9,17},{17,25},{2,10},{10,18},{18,26},{... | collective-permute-start | bytes 1179656 | tf_op jit(solution)/shard_map/ppermute | solution.py:481
  78.0 85.0 %collective-permute-start.18 = (bf16[4,4,48,1536]{3,2,1,0:T(8,128)(2,1)S(1)}, bf16[4,4,48,1536]{3,2,1,0:T(8,128)(2,1)S(1)}, u32[]{:S(2)}, u32[]{:S(2)}) collective-permute-start(bf16[4,4,48,1536]{3,2,1,0:T(8,128)(2,1)S(1)} %pad_maximum_fusion.1), channel_id=1, source_target_pairs={{0,1},{1,0},{2,3},{3,2},{4,5},{5,4},{6,7},{7,6},{8,9},{9,8},{10,11... | collective-permute-start | bytes 7077896 | tf_op jit(solution)/shard_map/ppermute | solution.py:449
  79.9 55.8 %collective-permute-start.2 = (bf16[384,1024]{1,0:T(8,128)(2,1)S(1)}, bf16[384,1024]{1,0:T(8,128)(2,1)S(1)}, u32[]{:S(2)}, u32[]{:S(2)}) collective-permute-start(bf16[384,1024]{1,0:T(8,128)(2,1)S(1)} %collective-permute-done.1), channel_id=1, source_target_pairs={{8,0},{16,8},{24,16},{9,1},{17,9},{25,17},{10,2},{18,10},{26,18},{... | collective-permute-start | bytes 2359304 | tf_op jit(solution)/shard_map/ppermute | solution.py:481
  101.7 82.2 %collective-permute-start.22 = (bf16[256,1536]{1,0:T(8,128)(2,1)}, bf16[256,1536]{1,0:T(8,128)(2,1)S(1)}, u32[]{:S(2)}, u32[]{:S(2)}) collective-permute-start(bf16[256,1536]{1,0:T(8,128)(2,1)} %get-tuple-element.454.refs_6_), channel_id=1, source_target_pairs={{0,2},{1,3},{2,0},{3,1},{4,6},{5,7},{6,4},{7,5},{8,10},{9,11},{10,... | collective-permute-start | bytes 2359304 | tf_op jit(solution)/shard_map/ppermute | solution.py:452
  103.6 39.8 %collective-permute-start.4 = (bf16[384,1024]{1,0:T(8,128)(2,1)S(1)}, bf16[384,1024]{1,0:T(8,128)(2,1)S(1)}, u32[]{:S(2)}, u32[]{:S(2)}) collective-permute-start(bf16[384,1024]{1,0:T(8,128)(2,1)S(1)} %collective-permute-done), channel_id=1, source_target_pairs={{0,8},{8,16},{16,24},{1,9},{9,17},{17,25},{2,10},{10,18},{18,26},{... | collective-permute-start | bytes 2359304 | tf_op jit(solution)/shard_map/ppermute | solution.py:481
  142.8 44.4 %collective-permute-start.23 = (bf16[256,1536]{1,0:T(8,128)(2,1)}, bf16[256,1536]{1,0:T(8,128)(2,1)}, u32[]{:S(2)}, u32[]{:S(2)}) collective-permute-start(bf16[256,1536]{1,0:T(8,128)(2,1)} %get-tuple-element.454.refs_6_), channel_id=1, source_target_pairs={{0,4},{1,5},{2,6},{3,7},{4,0},{5,1},{6,2},{7,3},{8,12},{9,13},{10,... | collective-permute-start | bytes 2359304 | tf_op jit(solution)/shard_map/ppermute | solution.py:452
  187.2 53.7 %collective-permute-start.26 = (bf16[256,1536]{1,0:T(8,128)(2,1)}, bf16[256,1536]{1,0:T(8,128)(2,1)S(1)}, u32[]{:S(2)}, u32[]{:S(2)}) collective-permute-start(bf16[256,1536]{1,0:T(8,128)(2,1)} %get-tuple-element.454.refs_6_), channel_id=1, source_target_pairs={{0,1},{1,0},{2,3},{3,2},{4,5},{5,4},{6,7},{7,6},{8,9},{9,8},{10,11... | collective-permute-start | bytes 2359304 | tf_op jit(solution)/shard_map/ppermute | solution.py:449
  240.9 52.3 %collective-permute-start.30 = (bf16[256,1536]{1,0:T(8,128)(2,1)}, bf16[256,1536]{1,0:T(8,128)(2,1)}, u32[]{:S(2)}, u32[]{:S(2)}) collective-permute-start(bf16[256,1536]{1,0:T(8,128)(2,1)} %multiply_convert_fusion.1.refs_2_), channel_id=1, source_target_pairs={{0,6},{1,7},{2,4},{3,5},{4,2},{5,3},{6,0},{7,1},{8,14},{9,15},{10,... | collective-permute-start | bytes 2359304 | tf_op jit(solution)/shard_map/ppermute | solution.py:452
  242.6 50.7 %collective-permute-start.31 = (bf16[256,1536]{1,0:T(8,128)(2,1)}, bf16[256,1536]{1,0:T(8,128)(2,1)}, u32[]{:S(2)}, u32[]{:S(2)}) collective-permute-start(bf16[256,1536]{1,0:T(8,128)(2,1)} %multiply_convert_fusion.1.refs_2_), channel_id=1, source_target_pairs={{0,1},{1,0},{2,3},{3,2},{4,5},{5,4},{6,7},{7,6},{8,9},{9,8},{10,11... | collective-permute-start | bytes 2359304 | tf_op jit(solution)/shard_map/ppermute | solution.py:449
  253.4 39.8 %collective-permute-start.29 = (bf16[256,1024]{1,0:T(8,128)(2,1)S(1)}, bf16[256,1024]{1,0:T(8,128)(2,1)S(1)}, u32[]{:S(2)}, u32[]{:S(2)}) collective-permute-start(bf16[256,1024]{1,0:T(8,128)(2,1)S(1)} %fusion.87.refs_3_.refs_7_), channel_id=1, source_target_pairs={{0,24},{1,25},{2,26},{3,27},{4,28},{5,29},{6,30},{7,31}} | collective-permute-start | bytes 1572872 | tf_op jit(solution)/shard_map/ppermute | solution.py:481
  254.8 127.8 %all-gather.8.cloned.1.call-start = ((), (), s32[]{:S(2)}) async-start(), calls=%async_computation.11 | async-start | bytes 3932160 | tf_op jit(solution)/shard_map/all_gather | solution.py:571
  254.8 60.1 %collective-permute-start.32 = (bf16[256,1536]{1,0:T(8,128)(2,1)}, bf16[256,1536]{1,0:T(8,128)(2,1)S(1)}, u32[]{:S(2)}, u32[]{:S(2)}) collective-permute-start(bf16[256,1536]{1,0:T(8,128)(2,1)} %multiply_convert_fusion.1.refs_2_), channel_id=1, source_target_pairs={{0,2},{1,3},{2,0},{3,1},{4,6},{5,7},{6,4},{7,5},{8,10},{9,11},{10,... | collective-permute-start | bytes 2359304 | tf_op jit(solution)/shard_map/ppermute | solution.py:452
  271.2 43.7 %collective-permute-start.33 = (bf16[256,1536]{1,0:T(8,128)(2,1)}, bf16[256,1536]{1,0:T(8,128)(2,1)S(1)}, u32[]{:S(2)}, u32[]{:S(2)}) collective-permute-start(bf16[256,1536]{1,0:T(8,128)(2,1)} %multiply_convert_fusion.1.refs_2_), channel_id=1, source_target_pairs={{0,4},{1,5},{2,6},{3,7},{4,0},{5,1},{6,2},{7,3},{8,12},{9,13},{10,... | collective-permute-start | bytes 2359304 | tf_op jit(solution)/shard_map/ppermute | solution.py:452
  318.9 540.0 %reduce-scatter.7.cloned.1.call-start = ((), (), s32[]{:S(2)}) async-start(), calls=%async_computation.8 | async-start | bytes 1966080 | tf_op jit(solution)/shard_map/reduce_scatter | solution.py:747
  319.3 45.7 %collective-permute-start.39 = (bf16[256,1536]{1,0:T(8,128)(2,1)}, bf16[256,1536]{1,0:T(8,128)(2,1)}, u32[]{:S(2)}, u32[]{:S(2)}) collective-permute-start(bf16[256,1536]{1,0:T(8,128)(2,1)} %get-tuple-element.241.refs_6_), channel_id=1, source_target_pairs={{0,1},{1,0},{2,3},{3,2},{4,5},{5,4},{6,7},{7,6},{8,9},{9,8},{10,11... | collective-permute-start | bytes 2359304 | tf_op jit(solution)/shard_map/ppermute | solution.py:449
  321.3 43.7 %collective-permute-start.35 = (bf16[256,1536]{1,0:T(8,128)(2,1)}, bf16[256,1536]{1,0:T(8,128)(2,1)S(1)}, u32[]{:S(2)}, u32[]{:S(2)}) collective-permute-start(bf16[256,1536]{1,0:T(8,128)(2,1)} %multiply_convert_fusion.refs_2_), channel_id=1, source_target_pairs={{0,2},{1,3},{2,0},{3,1},{4,6},{5,7},{6,4},{7,5},{8,10},{9,11},{10,... | collective-permute-start | bytes 2359304 | tf_op jit(solution)/shard_map/ppermute | solution.py:452
  321.3 43.8 %collective-permute-start.36 = (bf16[256,1536]{1,0:T(8,128)(2,1)}, bf16[256,1536]{1,0:T(8,128)(2,1)S(1)}, u32[]{:S(2)}, u32[]{:S(2)}) collective-permute-start(bf16[256,1536]{1,0:T(8,128)(2,1)} %multiply_convert_fusion.refs_2_), channel_id=1, source_target_pairs={{0,4},{1,5},{2,6},{3,7},{4,0},{5,1},{6,2},{7,3},{8,12},{9,13},{10,... | collective-permute-start | bytes 2359304 | tf_op jit(solution)/shard_map/ppermute | solution.py:452
  321.7 43.4 %collective-permute-start.37 = (bf16[256,1536]{1,0:T(8,128)(2,1)}, bf16[256,1536]{1,0:T(8,128)(2,1)S(1)}, u32[]{:S(2)}, u32[]{:S(2)}) collective-permute-start(bf16[256,1536]{1,0:T(8,128)(2,1)} %multiply_convert_fusion.refs_2_), channel_id=1, source_target_pairs={{0,6},{1,7},{2,4},{3,5},{4,2},{5,3},{6,0},{7,1},{8,14},{9,15},{10,... | collective-permute-start | bytes 2359304 | tf_op jit(solution)/shard_map/ppermute | solution.py:452
  324.8 40.3 %collective-permute-start.38 = (bf16[256,1536]{1,0:T(8,128)(2,1)}, bf16[256,1536]{1,0:T(8,128)(2,1)}, u32[]{:S(2)}, u32[]{:S(2)}) collective-permute-start(bf16[256,1536]{1,0:T(8,128)(2,1)} %multiply_convert_fusion.refs_2_), channel_id=1, source_target_pairs={{0,1},{1,0},{2,3},{3,2},{4,5},{5,4},{6,7},{7,6},{8,9},{9,8},{10,11... | collective-permute-start | bytes 2359304 | tf_op jit(solution)/shard_map/ppermute | solution.py:449
  368.3 54.9 %collective-permute-start.41 = (bf16[256,1536]{1,0:T(8,128)(2,1)}, bf16[256,1536]{1,0:T(8,128)(2,1)}, u32[]{:S(2)}, u32[]{:S(2)}) collective-permute-start(bf16[256,1536]{1,0:T(8,128)(2,1)} %get-tuple-element.241.refs_6_), channel_id=1, source_target_pairs={{0,2},{1,3},{2,0},{3,1},{4,6},{5,7},{6,4},{7,5},{8,10},{9,11},{10,... | collective-permute-start | bytes 2359304 | tf_op jit(solution)/shard_map/ppermute | solution.py:452
  368.4 54.9 %collective-permute-start.42 = (bf16[256,1536]{1,0:T(8,128)(2,1)}, bf16[256,1536]{1,0:T(8,128)(2,1)}, u32[]{:S(2)}, u32[]{:S(2)}) collective-permute-start(bf16[256,1536]{1,0:T(8,128)(2,1)} %get-tuple-element.241.refs_6_), channel_id=1, source_target_pairs={{0,4},{1,5},{2,6},{3,7},{4,0},{5,1},{6,2},{7,3},{8,12},{9,13},{10,... | collective-permute-start | bytes 2359304 | tf_op jit(solution)/shard_map/ppermute | solution.py:452
  368.6 54.7 %collective-permute-start.43 = (bf16[256,1536]{1,0:T(8,128)(2,1)}, bf16[256,1536]{1,0:T(8,128)(2,1)}, u32[]{:S(2)}, u32[]{:S(2)}) collective-permute-start(bf16[256,1536]{1,0:T(8,128)(2,1)} %get-tuple-element.241.refs_6_), channel_id=1, source_target_pairs={{0,6},{1,7},{2,4},{3,5},{4,2},{5,3},{6,0},{7,1},{8,14},{9,15},{10,... | collective-permute-start | bytes 2359304 | tf_op jit(solution)/shard_map/ppermute | solution.py:452
  373.3 50.0 %collective-permute-start.40 = (bf16[768,1536]{1,0:T(8,128)(2,1)S(1)}, bf16[768,1536]{1,0:T(8,128)(2,1)}, u32[]{:S(2)}, u32[]{:S(2)}) collective-permute-start(bf16[768,1536]{1,0:T(8,128)(2,1)S(1)} %pad_maximum_fusion.2.refs_3_), channel_id=1, source_target_pairs={{0,1},{1,0},{2,3},{3,2},{4,5},{5,4},{6,7},{7,6},{8,9},{9,8},{10,11... | collective-permute-start | bytes 7077896 | tf_op jit(solution)/shard_map/ppermute | solution.py:449
  427.6 56.5 %collective-permute-start.49 = (bf16[1024,1536]{1,0:T(8,128)(2,1)}, bf16[1024,1536]{1,0:T(8,128)(2,1)}, u32[]{:S(2)}, u32[]{:S(2)}) collective-permute-start(bf16[1024,1536]{1,0:T(8,128)(2,1)} %get-tuple-element.267), channel_id=1, source_target_pairs={{0,1},{1,0},{2,3},{3,2},{4,5},{5,4},{6,7},{7,6},{8,9},{9,8},{10,11... | collective-permute-start | bytes 9437192 | tf_op jit(solution)/shard_map/ppermute | solution.py:449
  440.1 44.1 %collective-permute-start.46 = (bf16[256,1536]{1,0:T(8,128)(2,1)}, bf16[256,1536]{1,0:T(8,128)(2,1)S(1)}, u32[]{:S(2)}, u32[]{:S(2)}) collective-permute-start(bf16[256,1536]{1,0:T(8,128)(2,1)} %get-tuple-element.264), channel_id=1, source_target_pairs={{0,2},{1,3},{2,0},{3,1},{4,6},{5,7},{6,4},{7,5},{8,10},{9,11},{10,... | collective-permute-start | bytes 2359304 | tf_op jit(solution)/shard_map/ppermute | solution.py:452
  441.6 42.6 %collective-permute-start.47 = (bf16[256,1536]{1,0:T(8,128)(2,1)}, bf16[256,1536]{1,0:T(8,128)(2,1)S(1)}, u32[]{:S(2)}, u32[]{:S(2)}) collective-permute-start(bf16[256,1536]{1,0:T(8,128)(2,1)} %get-tuple-element.265), channel_id=1, source_target_pairs={{0,4},{1,5},{2,6},{3,7},{4,0},{5,1},{6,2},{7,3},{8,12},{9,13},{10,... | collective-permute-start | bytes 2359304 | tf_op jit(solution)/shard_map/ppermute | solution.py:452
  443.1 41.2 %collective-permute-start.48 = (bf16[256,1536]{1,0:T(8,128)(2,1)}, bf16[256,1536]{1,0:T(8,128)(2,1)S(1)}, u32[]{:S(2)}, u32[]{:S(2)}) collective-permute-start(bf16[256,1536]{1,0:T(8,128)(2,1)} %get-tuple-element.266), channel_id=1, source_target_pairs={{0,6},{1,7},{2,4},{3,5},{4,2},{5,3},{6,0},{7,1},{8,14},{9,15},{10,... | collective-permute-start | bytes 2359304 | tf_op jit(solution)/shard_map/ppermute | solution.py:452
  484.3 374.6 %reduce-scatter.11.cloned.1.call-start = ((), (), s32[]{:S(2)}) async-start(), calls=%async_computation.10 | async-start | bytes 1966080 | tf_op jit(solution)/shard_map/reduce_scatter | solution.py:747
  491.5 45.2 %collective-permute-start.50 = (bf16[256,1536]{1,0:T(8,128)(2,1)}, bf16[256,1536]{1,0:T(8,128)(2,1)S(1)}, u32[]{:S(2)}, u32[]{:S(2)}) collective-permute-start(bf16[256,1536]{1,0:T(8,128)(2,1)} %get-tuple-element.283), channel_id=1, source_target_pairs={{0,2},{1,3},{2,0},{3,1},{4,6},{5,7},{6,4},{7,5},{8,10},{9,11},{10,... | collective-permute-start | bytes 2359304 | tf_op jit(solution)/shard_map/ppermute | solution.py:452
  493.0 43.7 %collective-permute-start.51 = (bf16[256,1536]{1,0:T(8,128)(2,1)}, bf16[256,1536]{1,0:T(8,128)(2,1)S(1)}, u32[]{:S(2)}, u32[]{:S(2)}) collective-permute-start(bf16[256,1536]{1,0:T(8,128)(2,1)} %get-tuple-element.284), channel_id=1, source_target_pairs={{0,4},{1,5},{2,6},{3,7},{4,0},{5,1},{6,2},{7,3},{8,12},{9,13},{10,... | collective-permute-start | bytes 2359304 | tf_op jit(solution)/shard_map/ppermute | solution.py:452
  494.4 42.3 %collective-permute-start.52 = (bf16[256,1536]{1,0:T(8,128)(2,1)}, bf16[256,1536]{1,0:T(8,128)(2,1)}, u32[]{:S(2)}, u32[]{:S(2)}) collective-permute-start(bf16[256,1536]{1,0:T(8,128)(2,1)} %get-tuple-element.285), channel_id=1, source_target_pairs={{0,6},{1,7},{2,4},{3,5},{4,2},{5,3},{6,0},{7,1},{8,14},{9,15},{10,... | collective-permute-start | bytes 2359304 | tf_op jit(solution)/shard_map/ppermute | solution.py:452
  537.8 321.0 %reduce-scatter.5.cloned.1.call-start = ((), (), s32[]{:S(2)}) async-start(), calls=%async_computation.7 | async-start | bytes 3932160 | tf_op jit(solution)/shard_map/reduce_scatter | solution.py:747
  538.6 320.3 %reduce-scatter.9.cloned.1.call-start = ((), (), s32[]{:S(2)}) async-start(), calls=%async_computation.9 | async-start | bytes 3932160 | tf_op jit(solution)/shard_map/reduce_scatter | solution.py:747
  558.1 35.3 %collective-permute-start.57 = (bf16[256,1536]{1,0:T(8,128)(2,1)S(1)}, bf16[256,1536]{1,0:T(8,128)(2,1)S(1)}, u32[]{:S(2)}, u32[]{:S(2)}) collective-permute-start(bf16[256,1536]{1,0:T(8,128)(2,1)S(1)} %get-tuple-element.309), channel_id=1, source_target_pairs={{0,2},{1,3},{2,0},{3,1},{4,6},{5,7},{6,4},{7,5},{8,10},{9,11},{10,... | collective-permute-start | bytes 2359304 | tf_op jit(solution)/shard_map/ppermute | solution.py:452
  583.5 51.2 %collective-permute-start.56 = (bf16[2,256,512]{2,1,0:T(8,128)(2,1)S(1)}, bf16[2,256,512]{2,1,0:T(8,128)(2,1)S(1)}, u32[]{:S(2)}, u32[]{:S(2)}) collective-permute-start(bf16[2,256,512]{2,1,0:T(8,128)(2,1)S(1)} %get-tuple-element.308), channel_id=1, source_target_pairs={{16,0},{24,8},{17,1},{25,9},{18,2},{26,10},{19,3},{27,11},{20,4},{... | collective-permute-start | bytes 1572872 | tf_op jit(solution)/shard_map/ppermute | solution.py:481
  584.9 84.9 %collective-permute-start.59 = (bf16[2,256,512]{2,1,0:T(8,128)(2,1)S(1)}, bf16[2,256,512]{2,1,0:T(8,128)(2,1)S(1)}, u32[]{:S(2)}, u32[]{:S(2)}) collective-permute-start(bf16[2,256,512]{2,1,0:T(8,128)(2,1)S(1)} %get-tuple-element.324), channel_id=1, source_target_pairs={{8,0},{16,8},{24,16},{9,1},{17,9},{25,17},{10,2},{18,10},{26,18},{... | collective-permute-start | bytes 1572872 | tf_op jit(solution)/shard_map/ppermute | solution.py:481
  586.2 83.6 %collective-permute-start.60 = (bf16[2,256,512]{2,1,0:T(8,128)(2,1)S(1)}, bf16[2,256,512]{2,1,0:T(8,128)(2,1)S(1)}, u32[]{:S(2)}, u32[]{:S(2)}) collective-permute-start(bf16[2,256,512]{2,1,0:T(8,128)(2,1)S(1)} %get-tuple-element.326), channel_id=1, source_target_pairs={{24,0},{25,1},{26,2},{27,3},{28,4},{29,5},{30,6},{31,7}} | collective-permute-start | bytes 1572872 | tf_op jit(solution)/shard_map/ppermute | solution.py:481
  643.2 36.1 %collective-permute-start.62 = (bf16[256,1536]{1,0:T(8,128)(2,1)S(1)}, bf16[256,1536]{1,0:T(8,128)(2,1)S(1)}, u32[]{:S(2)}, u32[]{:S(2)}) collective-permute-start(bf16[256,1536]{1,0:T(8,128)(2,1)S(1)} %get-tuple-element.328), channel_id=1, source_target_pairs={{0,4},{1,5},{2,6},{3,7},{4,0},{5,1},{6,2},{7,3},{8,12},{9,13},{10,... | collective-permute-start | bytes 2359304 | tf_op jit(solution)/shard_map/ppermute | solution.py:452
  700.3 115.4 %collective-permute-start.64 = (bf16[2,256,512]{2,1,0:T(8,128)(2,1)}, bf16[2,256,512]{2,1,0:T(8,128)(2,1)}, u32[]{:S(2)}, u32[]{:S(2)}) collective-permute-start(bf16[2,256,512]{2,1,0:T(8,128)(2,1)} %get-tuple-element.342), channel_id=1, source_target_pairs={{8,0},{16,8},{24,16},{9,1},{17,9},{25,17},{10,2},{18,10},{26,18},{... | collective-permute-start | bytes 1572872 | tf_op jit(solution)/shard_map/ppermute | solution.py:481
  715.9 35.5 %collective-permute-start.68 = (bf16[4,48,1536]{2,1,0:T(8,128)(2,1)S(1)}, bf16[4,48,1536]{2,1,0:T(8,128)(2,1)S(1)}, u32[]{:S(2)}, u32[]{:S(2)}) collective-permute-start(bf16[4,48,1536]{2,1,0:T(8,128)(2,1)S(1)} %get-tuple-element.440), channel_id=1, source_target_pairs={{0,2},{1,3},{2,0},{3,1},{4,6},{5,7},{6,4},{7,5},{8,10},{9,11},{10,... | collective-permute-start | bytes 1769480 | tf_op jit(solution)/shard_map/ppermute | solution.py:452
  726.1 36.2 %collective-permute-start.69 = (bf16[4,48,1536]{2,1,0:T(8,128)(2,1)S(1)}, bf16[4,48,1536]{2,1,0:T(8,128)(2,1)S(1)}, u32[]{:S(2)}, u32[]{:S(2)}) collective-permute-start(bf16[4,48,1536]{2,1,0:T(8,128)(2,1)S(1)} %get-tuple-element.442), channel_id=1, source_target_pairs={{0,4},{1,5},{2,6},{3,7},{4,0},{5,1},{6,2},{7,3},{8,12},{9,13},{10,... | collective-permute-start | bytes 1769480 | tf_op jit(solution)/shard_map/ppermute | solution.py:452
  768.0 47.7 %collective-permute-start.65 = (bf16[2,256,512]{2,1,0:T(8,128)(2,1)S(1)}, bf16[2,256,512]{2,1,0:T(8,128)(2,1)S(1)}, u32[]{:S(2)}, u32[]{:S(2)}) collective-permute-start(bf16[2,256,512]{2,1,0:T(8,128)(2,1)S(1)} %copy-done.23), channel_id=1, source_target_pairs={{16,0},{24,8},{17,1},{25,9},{18,2},{26,10},{19,3},{27,11},{20,4},{... | collective-permute-start | bytes 1572872 | tf_op jit(solution)/shard_map/ppermute | solution.py:481
  769.3 46.4 %collective-permute-start.66 = (bf16[2,256,512]{2,1,0:T(8,128)(2,1)S(1)}, bf16[2,256,512]{2,1,0:T(8,128)(2,1)S(1)}, u32[]{:S(2)}, u32[]{:S(2)}) collective-permute-start(bf16[2,256,512]{2,1,0:T(8,128)(2,1)S(1)} %copy-done.21), channel_id=1, source_target_pairs={{24,0},{25,1},{26,2},{27,3},{28,4},{29,5},{30,6},{31,7}} | collective-permute-start | bytes 1572872 | tf_op jit(solution)/shard_map/ppermute | solution.py:481
  770.7 44.3 %collective-permute-start.72 = (bf16[48,1536]{1,0:T(8,128)(2,1)S(1)}, bf16[48,1536]{1,0:T(8,128)(2,1)S(1)}, u32[]{:S(2)}, u32[]{:S(2)}) collective-permute-start(bf16[48,1536]{1,0:T(8,128)(2,1)S(1)} %get-tuple-element.462), channel_id=1, source_target_pairs={{0,16},{8,24},{16,0},{24,8},{1,17},{9,25},{17,1},{25,9},{2,18},{10... | collective-permute-start | bytes 442376 | tf_op jit(solution)/shard_map/ppermute | solution.py:476
  773.7 41.2 %collective-permute-start.73 = (bf16[48,1536]{1,0:T(8,128)(2,1)S(1)}, bf16[48,1536]{1,0:T(8,128)(2,1)S(1)}, u32[]{:S(2)}, u32[]{:S(2)}) collective-permute-start(bf16[48,1536]{1,0:T(8,128)(2,1)S(1)} %get-tuple-element.461), channel_id=1, source_target_pairs={{0,24},{8,16},{16,8},{24,0},{1,25},{9,17},{17,9},{25,1},{2,26},{10... | collective-permute-start | bytes 442376 | tf_op jit(solution)/shard_map/ppermute | solution.py:476
  (155 other events, 2767.2 us)
Sparse Core Ops, SparseCore 0:
  12.4 103.6 all-gather.5
Sparse Core Ops, SparseCore 1:
  254.9 47.0 all-gather.9
  319.0 63.5 all-gather.7
  484.4 33.9 reduce-scatter.6
  537.9 33.9 reduce-scatter.10
  574.2 92.4 reduce-scatter.4
  669.6 84.5 reduce-scatter.8

commit v2 on v1

v2 whole, which is shorter than its diff:
```python
import functools

import jax
import jax.numpy as jnp
from jax import lax
from jax.experimental import pallas as pl
from jax.experimental.pallas import tpu as pltpu
from jax.sharding import PartitionSpec as P

H = 24
KV = 8
HD = 64
FFE = 512
BLOCK = 128
PAIRS = KV // 2
GROUP = H // KV
PAIR_Q = 2 * GROUP * HD
PAIR_K = 2 * HD

EPSILON = 1e-06
NEGATIVE = -1e30
F32 = jnp.float32
BF16 = jnp.bfloat16


def mm(a, b):
    return jnp.dot(a, b, preferred_element_type=F32)


def mm_nt(a, b):
    return lax.dot_general(a, b, (((1,), (1,)), ((), ())), preferred_element_type=F32)


def mm_tn(a, b):
    return lax.dot_general(a, b, (((0,), (0,)), ((), ())), preferred_element_type=F32)


def rms_norm(values_in, gain):
    return (
        values_in
        * lax.rsqrt(jnp.mean(values_in * values_in, axis=-1, keepdims=True) + EPSILON)
        * gain
    )


def rms_back(values, gain, grad):
    inv = lax.rsqrt(jnp.mean(values * values, axis=-1, keepdims=True) + EPSILON)
    unit = values * inv
    scaled = grad * gain
    grad_values = inv * (scaled - unit * jnp.mean(scaled * unit, axis=-1, keepdims=True))
    return grad_values, jnp.sum(grad * unit, axis=0)


def padded_rows(rows, half):
    blank = jnp.zeros_like(rows)
    return jnp.concatenate([rows, blank] if half == 0 else [blank, rows], axis=0)


def attend_kernel(chunks, q_ref, *refs):
    k_refs, v_refs = refs[:chunks], refs[chunks : 2 * chunks]
    bias_ref, o_ref, lse_ref, s_scr, p_scr = refs[2 * chunks :]
    rows = q_ref.shape[0]
    keys = k_refs[0].shape[0]
    q_t = q_ref[...].T * jnp.asarray(HD**-0.5, BF16)
    v_t = [v[...].T for v in v_refs]
    outs, totals = [], []
    for head in range(2 * GROUP):
        half = head // GROUP
        slot = head % 2
        q_pad = padded_rows(q_t[head * HD : (head + 1) * HD], half)
        peak = None
        for c in range(chunks):
            part = slice(c * keys, (c + 1) * keys)
            scores = mm(k_refs[c][...], q_pad) + bias_ref[part, :]
            s_scr[slot, part, :] = scores
            top = jnp.max(scores, axis=0, keepdims=True)
            peak = top if peak is None else jnp.maximum(peak, top)
        total = jnp.zeros((1, rows), F32)
        mixed = jnp.zeros((HD, rows), F32)
        for c in range(chunks):
            part = slice(c * keys, (c + 1) * keys)
            prob = jnp.exp(s_scr[slot, part, :] - peak)
            total = total + jnp.sum(prob, axis=0, keepdims=True)
            p_scr[slot, part, :] = prob.astype(BF16)
        for c in range(chunks):
            part = slice(c * keys, (c + 1) * keys)
            mixed = mixed + mm(v_t[c][half * HD : (half + 1) * HD], p_scr[slot, part, :])
        outs.append(mixed / total)
        totals.append(peak + jnp.log(total))
    o_ref[...] = jnp.concatenate(outs, axis=0).T.astype(BF16)
    blank = jnp.zeros((8 - 2 * GROUP, rows), F32)
    lse_ref[0] = jnp.concatenate(totals + [blank], axis=0)


def kv_specs(chunks, keys):
    k_spec = pl.BlockSpec((keys, PAIR_K), lambda j: (0, j))
    v_spec = pl.BlockSpec((keys, PAIR_K), lambda j: (0, PAIRS + j))
    return [k_spec] * chunks + [v_spec] * chunks


def attend(queries, kv_chunks, bias):
    rows, width = queries.shape
    chunks, keys = len(kv_chunks), kv_chunks[0].shape[0]
    work = 4 * H * rows * chunks * keys * HD
    q_spec = pl.BlockSpec((rows, PAIR_Q), lambda j: (0, j))
    return pl.pallas_call(
        functools.partial(attend_kernel, chunks),
        grid=(PAIRS,),
        in_specs=[q_spec]
        + kv_specs(chunks, keys)
        + [pl.BlockSpec((chunks * keys, rows), lambda j: (0, 0))],
        out_specs=[q_spec, pl.BlockSpec((1, 8, rows), lambda j: (j, 0, 0))],
        out_shape=[
            jax.ShapeDtypeStruct(queries.shape, BF16),
            jax.ShapeDtypeStruct((PAIRS, 8, rows), F32),
        ],
        scratch_shapes=[
            pltpu.VMEM((2, chunks * keys, rows), F32),
            pltpu.VMEM((2, chunks * keys, rows), BF16),
        ],
        compiler_params=pltpu.CompilerParams(vmem_limit_bytes=60 * 1024 * 1024),
        cost_estimate=pl.CostEstimate(
            flops=work // 64, bytes_accessed=1024 * 1024, transcendentals=0
        ),
        name="path_attention",
    )(queries, *kv_chunks, *kv_chunks, bias)


def attend_back_kernel(chunks, q_ref, g_ref, *refs):
    k_refs, v_refs = refs[:chunks], refs[chunks : 2 * chunks]
    bias_ref, lse_ref, dq_ref = refs[2 * chunks : 2 * chunks + 3]
    out_refs = refs[2 * chunks + 3 : 3 * chunks + 3]
    p_scr, gp_scr, ps_scr, ds_scr = refs[3 * chunks + 3 :]
    rows = q_ref.shape[0]
    keys = k_refs[0].shape[0]
    q_t = q_ref[...].T * jnp.asarray(HD**-0.5, BF16)
    g_t = g_ref[...].T
    k_t = [k[...].T for k in k_refs]
    dqs, q_pads, g_pads = [], [], []
    for head in range(2 * GROUP):
        half = head // GROUP
        slot = head % 2
        here = slice(head * rows, (head + 1) * rows)
        q_pad = padded_rows(q_t[head * HD : (head + 1) * HD], half)
        g_pad = padded_rows(g_t[head * HD : (head + 1) * HD], half)
        q_pads.append(q_pad)
        g_pads.append(g_pad)
        lse = lse_ref[0, head : head + 1, :]
        delta = jnp.zeros((1, rows), F32)
        for c in range(chunks):
            part = slice(c * keys, (c + 1) * keys)
            prob = jnp.exp(mm(k_refs[c][...], q_pad) + bias_ref[part, :] - lse)
            grad_prob = mm(v_refs[c][...], g_pad)
            delta = delta + jnp.sum(prob * grad_prob, axis=0, keepdims=True)
            p_scr[slot, part, :] = prob
            gp_scr[slot, part, :] = grad_prob
            ps_scr[part, here] = prob.astype(BF16)
        dq = jnp.zeros((HD, rows), F32)
        for c in range(chunks):
            part = slice(c * keys, (c + 1) * keys)
            ds = (p_scr[slot, part, :] * (gp_scr[slot, part, :] - delta)).astype(BF16)
            ds_scr[part, here] = ds
            dq = dq + mm(k_t[c][half * HD : (half + 1) * HD], ds)
        dqs.append(dq * HD**-0.5)
    dq_ref[...] = jnp.concatenate(dqs, axis=0).T.astype(BF16)
    q_all = jnp.concatenate(q_pads, axis=1)
    g_all = jnp.concatenate(g_pads, axis=1)
    for c in range(chunks):
        part = slice(c * keys, (c + 1) * keys)
        out_refs[c][0] = mm_nt(ds_scr[part, :], q_all).astype(BF16)
        out_refs[c][1] = mm_nt(ps_scr[part, :], g_all).astype(BF16)


def attend_back(queries, grad_mixed, kv_chunks, bias, lse):
    rows, width = queries.shape
    chunks, keys = len(kv_chunks), kv_chunks[0].shape[0]
    work = 10 * H * rows * chunks * keys * HD
    q_spec = pl.BlockSpec((rows, PAIR_Q), lambda j: (0, j))
    return pl.pallas_call(
        functools.partial(attend_back_kernel, chunks),
        grid=(PAIRS,),
        in_specs=[q_spec, q_spec]
        + kv_specs(chunks, keys)
        + [
            pl.BlockSpec((chunks * keys, rows), lambda j: (0, 0)),
            pl.BlockSpec((1, 8, rows), lambda j: (j, 0, 0)),
        ],
        out_specs=[q_spec] + [pl.BlockSpec((2, keys, PAIR_K), lambda j: (0, 0, j))] * chunks,
        out_shape=[jax.ShapeDtypeStruct(queries.shape, BF16)]
        + [jax.ShapeDtypeStruct((2, keys, KV * HD), BF16)] * chunks,
        scratch_shapes=[
            pltpu.VMEM((2, chunks * keys, rows), F32),
            pltpu.VMEM((2, chunks * keys, rows), F32),
            pltpu.VMEM((chunks * keys, 2 * GROUP * rows), BF16),
            pltpu.VMEM((chunks * keys, 2 * GROUP * rows), BF16),
        ],
        compiler_params=pltpu.CompilerParams(vmem_limit_bytes=60 * 1024 * 1024),
        cost_estimate=pl.CostEstimate(
            flops=work // 64, bytes_accessed=1024 * 1024, transcendentals=0
        ),
        name="path_attention_back",
    )(queries, grad_mixed, *kv_chunks, *kv_chunks, bias, lse)


def ancestry(parents_in):
    count = parents_in.shape[-1]
    labels = jnp.arange(count, dtype=jnp.int32)
    reach = (parents_in[..., :, None] == labels) | (labels[:, None] == labels)
    steps = 1
    while steps < count:
        reach = jnp.any(reach[..., :, :, None] & reach[..., None, :, :], axis=-2)
        steps *= 2
    return reach


def mask_bias(parents, valid, dp_index, n_dp, rows):
    micro = parents.shape[0]
    per = rows // BLOCK
    reach = lax.dynamic_slice_in_dim(ancestry(parents), dp_index * per, per, 1)
    early = (n_dp - 1) * per
    reach = jnp.pad(reach, ((0, 0), (0, 0), (early, 0)))
    reach = lax.dynamic_slice_in_dim(reach, dp_index * per, n_dp * per, 2)
    ok = jnp.pad(valid > 0, ((0, 0), (early * BLOCK, 0)))
    ok = lax.dynamic_slice_in_dim(ok, dp_index * rows, n_dp * rows, 1)
    by_key = jnp.repeat(jnp.swapaxes(reach, 1, 2), BLOCK, axis=1)
    shape = (micro, n_dp * rows, rows)
    key = lax.broadcasted_iota(jnp.int32, shape, 1) - (n_dp - 1) * rows
    query = lax.broadcasted_iota(jnp.int32, shape, 2)
    onpath = jnp.zeros(shape, bool)
    for i in range(per):
        onpath = onpath | ((query // BLOCK == i) & by_key[:, :, i : i + 1])
    allowed = onpath & (key <= query) & (ok[:, :, None] | (key == query))
    return jnp.where(allowed, 0.0, NEGATIVE).astype(F32)


def expert_kernel(block, chips, shards, has_prev, has_acc, last, *refs):
    refs = list(refs)

    def take(n):
        out = refs[:n]
        del refs[:n]
        return out

    h_refs, c_refs = take(2 * chips), take(2)
    order_ref, gate_ref, w_ref = take(3)
    prev = take(4) if has_prev else None
    acc_in = take(2) if has_acc else None
    y_sib, y_own, gh_sib, gh_own = take(4)
    grad_refs = take(2)
    hb, cb, yb, gb, acc_gu, acc_d, wg_ref, wu_ref, wd_ref, sem_in, sem_out, sem_acc, sem_w = take(13)
    if has_prev:
        yp, gp, sem_prev = take(3)
    lead = h_refs[0].shape[0]
    per = block // lead
    half = chips // per
    steps = 2 * half

    def fetch(i, slot):
        for j in range(steps):

            @pl.when(i == j)
            def _():
                for r in range(per):
                    at = j * per + r
                    rows = pl.ds(r * lead, lead)
                    pltpu.make_async_copy(
                        h_refs[at], hb.at[slot, rows], sem_in.at[0, slot]
                    ).start()
                    pltpu.make_async_copy(
                        c_refs[at // chips].at[order_ref[at % chips]],
                        cb.at[slot, rows],
                        sem_in.at[1, slot],
                    ).start()
                if has_prev:
                    rows = pl.ds((j % half) * block, block)
                    for n, buffer in enumerate((yp, gp)):
                        pltpu.make_async_copy(
                            prev[2 * n + j // half].at[rows], buffer.at[slot], sem_prev.at[n, slot]
                        ).start()

    def fetched(slot):
        for n, buffer in enumerate((hb, cb)):
            pltpu.make_async_copy(buffer.at[slot], buffer.at[slot], sem_in.at[n, slot]).wait()
        if has_prev:
            for n, buffer in enumerate((yp, gp)):
                pltpu.make_async_copy(
                    buffer.at[slot], buffer.at[slot], sem_prev.at[n, slot]
                ).wait()

    def copies_out(y_ref, g_ref, at, slot):
        rows = pl.ds(pl.multiple_of(at * block, block), block)
        return (
            pltpu.make_async_copy(yb.at[slot], y_ref.at[rows], sem_out.at[0, slot]),
            pltpu.make_async_copy(gb.at[slot], g_ref.at[rows], sem_out.at[1, slot]),
        )

    def stored(slot):
        for copy in copies_out(y_own, gh_own, 0, slot):
            copy.wait()

    hidden, width = acc_d.shape
    tiles = width // hidden
    band = hidden // shards
    weight_copies = [
        pltpu.make_async_copy(w_ref.at[:, pl.ds(0, hidden)], wg_ref, sem_w.at[0]),
        pltpu.make_async_copy(w_ref.at[:, pl.ds(hidden, hidden)], wu_ref, sem_w.at[1]),
    ]
    for z in range(shards):
        for j in range(tiles):
            copy = pltpu.make_async_copy(
                w_ref.at[pl.ds((z * tiles + j) * band, band), pl.ds(2 * hidden, hidden)],
                wd_ref.at[pl.ds(z * band, band), pl.ds(j * hidden, hidden)],
                sem_w.at[2 + z * tiles + j],
            )
            weight_copies.append(copy)
    for copy in weight_copies:
        copy.start()
    fetch(0, 0)
    if has_acc:
        acc_copies = [
            pltpu.make_async_copy(acc_in[0], acc_gu, sem_acc.at[0]),
            pltpu.make_async_copy(acc_in[1], acc_d, sem_acc.at[1]),
        ]
        for copy in acc_copies:
            copy.start()
    else:
        acc_gu[...] = jnp.zeros_like(acc_gu)
        acc_d[...] = jnp.zeros_like(acc_d)

    for copy in weight_copies:
        copy.wait()

    def step(i, carry):
        slot = lax.rem(i, 2)

        @pl.when(i + 1 < steps)
        def _():
            fetch(i + 1, 1 - slot)

        fetched(slot)

        @pl.when(i >= 2)
        def _():
            stored(slot)

        tokens = hb[slot]
        grads = cb[slot]
        scale = jnp.broadcast_to(gate_ref[i], (8, block)).T[:, :1]
        gate = mm(tokens, wg_ref[...])
        up = mm(tokens, wu_ref[...])
        grad_act = mm_nt(grads, wd_ref[...]) * scale
        sig = jax.nn.sigmoid(gate)
        silu = gate * sig
        act = (silu * up * scale).astype(BF16)
        grad_gate = (grad_act * up * (sig + silu * (1.0 - sig))).astype(BF16)
        grad_up = (grad_act * silu).astype(BF16)
        y = mm(act, wd_ref[...])
        gh = mm_nt(grad_gate, wg_ref[...]) + mm_nt(grad_up, wu_ref[...])
        if has_prev:
            y = y + yp[slot].astype(F32)
            gh = gh + gp[slot].astype(F32)
        yb[slot] = y.astype(BF16)
        gb[slot] = gh.astype(BF16)

        @pl.when(i < half)
        def _():
            for copy in copies_out(y_sib, gh_sib, i, slot):
                copy.start()

        @pl.when(i >= half)
        def _():
            for copy in copies_out(y_own, gh_own, i - half, slot):
                copy.start()

        if has_acc:

            @pl.when(i == 0)
            def _():
                for copy in acc_copies:
                    copy.wait()

        acc_d[...] += mm_tn(act, grads)
        acc_gu[:, :FFE] += mm_tn(tokens, grad_gate)
        acc_gu[:, FFE:] += mm_tn(tokens, grad_up)
        return carry

    lax.fori_loop(0, steps, step, 0)
    stored(steps % 2)
    stored((steps - 1) % 2)
    if last:
        cut = grad_refs[0].shape[1] - 2 * hidden
        grad_refs[0][:, : 2 * hidden] = acc_gu[...].astype(BF16)
        for z in range(shards):
            for j in range(tiles):
                rows = slice((z * tiles + j) * band, (z * tiles + j + 1) * band)
                piece = acc_d[z * band : (z + 1) * band, j * hidden : (j + 1) * hidden].astype(BF16)
                grad_refs[0][rows, 2 * hidden :] = piece[:, :cut]
                grad_refs[1][rows, :] = piece[:, cut:]
    else:
        out = [
            pltpu.make_async_copy(acc_gu, grad_refs[0], sem_acc.at[0]),
            pltpu.make_async_copy(acc_d, grad_refs[1], sem_acc.at[1]),
        ]
        for copy in out:
            copy.start()
        for copy in out:
            copy.wait()


def expert_pass(h_all, c_all, order, gates, weight, shards, previous, totals, last, block=512):
    chips = len(h_all) // 2
    lead, width = h_all[0].shape
    rows = chips * lead
    hidden = weight.shape[1] // 3
    far = pl.BlockSpec(memory_space=pl.ANY)
    near = pl.BlockSpec(memory_space=pltpu.VMEM)
    scalars = pl.BlockSpec(memory_space=pltpu.SMEM)
    token_out = jax.ShapeDtypeStruct((rows, width), BF16)
    token_buffer = pltpu.VMEM((2, block, width), BF16)
    if last:
        first = 2 * hidden + hidden // 4
        grads = [((width, first), BF16), ((width, 3 * hidden - first), BF16)]
    else:
        grads = [((width, 2 * hidden), F32), ((hidden, width), F32)]
    scratch = [token_buffer] * 4 + [
        pltpu.VMEM((width, 2 * hidden), F32),
        pltpu.VMEM((hidden, width), F32),
        pltpu.VMEM((width, hidden), BF16),
        pltpu.VMEM((width, hidden), BF16),
        pltpu.VMEM((hidden, width), BF16),
        pltpu.SemaphoreType.DMA((2, 2)),
        pltpu.SemaphoreType.DMA((2, 2)),
        pltpu.SemaphoreType.DMA((2,)),
        pltpu.SemaphoreType.DMA((2 + shards * (width // hidden),)),
    ]
    extra, aliases = [], {}
    if previous is not None:
        scratch += [token_buffer] * 2 + [pltpu.SemaphoreType.DMA((2, 2))]
        aliases = {2 * chips + 5 + n: n for n in range(4)}
        extra += list(previous)
    if totals is not None:
        extra += list(totals)
    return pl.pallas_call(
        functools.partial(
            expert_kernel, block, chips, shards, previous is not None, totals is not None, last
        ),
        in_specs=[far] * (2 * chips + 2) + [scalars, near, far] + [far] * len(extra),
        out_specs=[far] * 4 + [near if last else far] * len(grads),
        out_shape=[token_out] * 4 + [jax.ShapeDtypeStruct(*g) for g in grads],
        scratch_shapes=scratch,
        input_output_aliases=aliases,
        compiler_params=pltpu.CompilerParams(vmem_limit_bytes=60 * 1024 * 1024),
        cost_estimate=pl.CostEstimate(
            flops=rows * width, bytes_accessed=rows * width, transcendentals=0
        ),
        name="expert_pass",
    )(*h_all, *c_all, order, gates, weight, *extra)


SMALL = pl.CostEstimate(flops=1024, bytes_accessed=1024, transcendentals=0)
FAR = pl.BlockSpec(memory_space=pl.ANY)
NEAR = pl.BlockSpec(memory_space=pltpu.VMEM)
SCALARS = pl.BlockSpec(memory_space=pltpu.SMEM)


def small_call(kernel, name, inputs, outs, in_specs=None, scratch=()):
    return pl.pallas_call(
        kernel,
        in_specs=in_specs or [NEAR] * len(inputs),
        out_specs=[NEAR] * len(outs),
        out_shape=[jax.ShapeDtypeStruct(shape, dtype) for shape, dtype in outs],
        scratch_shapes=list(scratch),
        compiler_params=pltpu.CompilerParams(vmem_limit_bytes=48 * 1024 * 1024),
        cost_estimate=SMALL,
        name=name,
    )(*inputs)


def assemble_kernel(counts, chunk, place_ref, *refs):
    out_ref, sem = refs[len(counts) :]
    copies, n = [], 0
    for ref, count in zip(refs, counts):
        for at in range(count):
            rows = pl.ds(pl.multiple_of(place_ref[n] * chunk, chunk), chunk)
            copies.append(pltpu.make_async_copy(ref.at[at], out_ref.at[rows], sem))
            n += 1
    for copy in copies:
        copy.start()
    for copy in copies:
        copy.wait()


def assemble(blocks, places):
    chunk, width = blocks[0].shape[1:]
    counts = [x.shape[0] for x in blocks]
    rows = sum(counts) * chunk
    if chunk % 16:
        bands = jnp.concatenate(blocks, axis=0)
        whole = jnp.zeros_like(bands).at[places].set(bands)
        return whole.reshape(rows, width)
    return pl.pallas_call(
        functools.partial(assemble_kernel, counts, chunk),
        in_specs=[SCALARS] + [FAR] * len(blocks),
        out_specs=NEAR,
        out_shape=jax.ShapeDtypeStruct((rows, width), BF16),
        scratch_shapes=[pltpu.SemaphoreType.DMA],
        compiler_params=pltpu.CompilerParams(vmem_limit_bytes=32 * 1024 * 1024),
        cost_estimate=SMALL,
        name="assemble",
    )(places, *blocks)


def project_kernel(width, *refs):
    micro = (len(refs) - 2) // 3
    x_refs, w_ref = refs[:micro], refs[micro]
    h_refs, kv_refs, gains_ref = refs[micro + 1 : -1 - micro], refs[-1 - micro : -1], refs[-1]
    kv_from = w_ref.shape[1] - 128 - kv_refs[0].shape[1]
    gains = w_ref[:, -128:].astype(F32).T
    gains_ref[...] = gains[:8]
    for x_ref, h_ref, kv_ref in zip(x_refs, h_refs, kv_refs):
        h = rms_norm(x_ref[...].astype(F32), gains[:1]).astype(BF16)
        h_ref[...] = h
        kv_ref[...] = mm(h, w_ref[:, kv_from:-128]).astype(BF16)


def project(xs, weight, kv_width):
    rows, width = xs[0].shape
    outs = (
        [((rows, width), BF16)] * len(xs)
        + [((rows, kv_width), BF16)] * len(xs)
        + [((8, width), F32)]
    )
    got = small_call(functools.partial(project_kernel, width), "project", [*xs, weight], outs)
    return list(got[: len(xs)]), list(got[len(xs) : -1]), got[-1]


def middle_kernel(attn_ref, x_ref, gains_ref, w_ref, mid_ref, h_ref):
    mid = x_ref[...].astype(F32) + mm_nt(attn_ref[...], w_ref[...])
    mid_ref[...] = mid
    h_ref[...] = rms_norm(mid, gains_ref[1:2]).astype(BF16)


def middle(attn, x, gains, w_out_t):
    return small_call(
        middle_kernel,
        "middle",
        [attn, x, gains, w_out_t],
        [(x.shape, F32), (x.shape, BF16)],
    )


def middle_back_kernel(got_ref, mid_ref, c_ref, gains_ref, w_ref, gx_ref, branch_ref, gain_ref, mixed_ref):
    grad = got_ref[0].astype(F32)
    for k in range(1, got_ref.shape[0]):
        grad = grad + got_ref[k].astype(F32)
    part, gain_part = rms_back(mid_ref[...], gains_ref[1:2], grad)
    grad_x = c_ref[...].astype(F32) + part
    branch = grad_x.astype(BF16)
    gx_ref[...] = grad_x
    branch_ref[...] = branch
    gain_ref[...] = jnp.broadcast_to(gain_part[None], gain_ref.shape)
    mixed_ref[...] = mm(branch, w_ref[...]).astype(BF16)


def middle_back(got, mid, c, gains, w_out_t):
    return small_call(
        middle_back_kernel,
        "middle_back",
        [got, mid, c, gains, w_out_t],
        [(c.shape, F32), (c.shape, BF16), ((8, c.shape[1]), F32), (c.shape, BF16)],
    )


def input_back_kernel(q_ref, kv_ref, x_ref, mid_ref, gains_ref, w_ref, grad_ref):
    query_width = q_ref.shape[1]
    cut = query_width + kv_ref.shape[1]
    grad_h = mm_nt(q_ref[...], w_ref[:, :query_width])
    grad_h = grad_h + mm_nt(kv_ref[...], w_ref[:, query_width:cut])
    part, _ = rms_back(x_ref[...].astype(F32), gains_ref[:1], grad_h)
    grad_ref[...] = (mid_ref[...] + part).astype(BF16)


def input_back(grad_q, grad_kv, x, grad_x_mid, gains, weight):
    return small_call(
        input_back_kernel,
        "input_back",
        [grad_q, grad_kv, x, grad_x_mid, gains, weight],
        [(x.shape, BF16)],
    )[0]


def unpack_kernel(*refs):
    up_ref, down_ref = refs[-2:]
    for e in range(up_ref.shape[0]):
        first, second = refs[2 * e][...], refs[2 * e + 1][...]
        cut = up_ref.shape[2]
        up_ref[e] = first[:, :cut].astype(F32)
        pieces = jnp.concatenate([first[:, cut:], second], axis=1).astype(F32)
        rows, wide = down_ref.shape[1], pieces.shape[1]
        for j in range(down_ref.shape[2] // wide):
            down_ref[e, :, j * wide : (j + 1) * wide] = pieces[j * rows : (j + 1) * rows]


def unpack(totals, up_shape, down_shape):
    flat = [t for pair in totals for t in pair]
    return small_call(unpack_kernel, "unpack", flat, [(up_shape, F32), (down_shape, F32)])


def band_totals_kernel(counts, dp_ref, *refs):
    refs = list(refs)
    groups = []
    for count in counts:
        groups.append(refs[:count])
        del refs[:count]
    own_ref, piece_refs = refs[0], refs[1:]

    def total(ref):
        held = ref[0].astype(F32)
        for k in range(1, ref.shape[0]):
            held = held + ref[k].astype(F32)
        return held

    columns = []
    for group in groups:
        if len(group) == 1 and len(group[0].shape) == 4:
            columns.append(total(group[0]))
        else:
            columns.append(functools.reduce(jnp.add, [ref[...].astype(F32) for ref in group]))
    whole = jnp.concatenate(columns, axis=-1)
    dp_index = dp_ref[0]
    for z in range(whole.shape[0]):

        @pl.when(dp_index == z)
        def _():
            own_ref[...] = whole[z]

        for k, ref in enumerate(piece_refs):

            @pl.when((dp_index ^ (k + 1)) == z)
            def _():
                ref[...] = whole[z].astype(BF16)


def band_totals(groups, dp_index):
    n_dp, chunk = groups[0][0].shape[-3:-1]
    width = sum(group[0].shape[-1] for group in groups)
    inputs = [dp_index.reshape(1)] + [x for group in groups for x in group]
    own, *pieces = small_call(
        functools.partial(band_totals_kernel, [len(group) for group in groups]),
        "band_totals",
        inputs,
        [((chunk, width), F32)] + [((chunk, width), BF16)] * (n_dp - 1),
        in_specs=[SCALARS] + [NEAR] * (len(inputs) - 1),
    )
    return own, pieces


def sums_kernel(order_ref, own_ref, other_ref, out_ref):
    out_ref[...] = (own_ref[...].astype(F32) + other_ref[...].astype(F32)).astype(BF16)


def sums(own, other, order):
    blank = (0,) * (own.ndim - 1)
    block = (1,) + own.shape[1:]
    spec = pl.BlockSpec(block, lambda i, order: (i,) + blank)
    return pl.pallas_call(
        sums_kernel,
        grid_spec=pltpu.PrefetchScalarGridSpec(
            num_scalar_prefetch=1,
            grid=(own.shape[0],),
            in_specs=[spec, spec],
            out_specs=pl.BlockSpec(block, lambda i, order: (order[i],) + blank),
        ),
        out_shape=jax.ShapeDtypeStruct(own.shape, BF16),
        compiler_params=pltpu.CompilerParams(vmem_limit_bytes=32 * 1024 * 1024),
        cost_estimate=SMALL,
        name="sums",
    )(order, own, other)


def weight_grad_kernel(parts, chunk, n_dp, core_ref, *refs):
    left, right = refs[:parts], refs[parts : 2 * parts]
    own_ref, other_ref = refs[2 * parts :]
    total = mm_tn(left[0][...], right[0][...])
    for a, b in zip(left[1:], right[1:]):
        total = total + mm_tn(a[...], b[...])
    total = total.astype(BF16)
    chips = total.shape[0] // (2 * chunk * n_dp)
    pairs = total.reshape(n_dp, chips, 2, chunk, total.shape[1])
    first = core_ref[0] == 0
    for z in range(n_dp):
        for j in range(chips):
            own_ref[j, z] = jnp.where(first, pairs[z, j, 0], pairs[z, j, 1])
            other_ref[j, z] = jnp.where(first, pairs[z, j, 1], pairs[z, j, 0])


def weight_grad(left, right, n_dp, chips, core):
    width, columns = left[0].shape[1], right[0].shape[1]
    chunk = width // (2 * n_dp * chips)
    if chunk % 16:
        total = sum(mm_tn(a, b) for a, b in zip(left, right)).astype(BF16)
        pairs = total.reshape(n_dp, chips, 2, chunk, columns)
        return [
            jnp.swapaxes(lax.dynamic_index_in_dim(pairs, c, 2, keepdims=False), 0, 1)
            for c in (core, 1 - core)
        ]
    parts, tokens = len(left), left[0].shape[0]
    block = 512
    shape = (chips, n_dp, chunk)
    band = jax.ShapeDtypeStruct(shape + (columns,), BF16)
    band_spec = pl.BlockSpec(shape + (block,), lambda j: (0, 0, 0, j))
    return pl.pallas_call(
        functools.partial(weight_grad_kernel, parts, chunk, n_dp),
        grid=(columns // block,),
        in_specs=[SCALARS]
        + [pl.BlockSpec((tokens, width), lambda j: (0, 0))] * parts
        + [pl.BlockSpec((tokens, block), lambda j: (0, j))] * parts,
        out_specs=[band_spec, band_spec],
        out_shape=[band, band],
        compiler_params=pltpu.CompilerParams(vmem_limit_bytes=32 * 1024 * 1024),
        cost_estimate=SMALL,
        name="weight_grad",
    )(core.reshape(1).astype(jnp.int32), *left, *right)


def join(*items):
    return lax.optimization_barrier(items)


class Plane:
    def __init__(self, count):
        self.count = count
        self.chips = count // 2

    def swap(self, x):
        return lax.ppermute(x, "expert", [(i, i ^ 1) for i in range(self.count)])

    def cross(self, x, k):
        return lax.ppermute(x, "expert", [(i, i ^ (2 * k)) for i in range(self.count)])

    def exchange(self, x):
        groups = [[chip * 2 + c for chip in range(self.chips)] for c in range(2)]
        return lax.all_to_all(
            x, "expert", split_axis=0, concat_axis=0, axis_index_groups=groups, tiled=True
        )

    def spread(self, x):
        return self.exchange(jnp.broadcast_to(x[None], (self.chips,) + x.shape))

    def doubled(self, held, n):
        bits = [1 << i for i in range(self.chips.bit_length() - 1)]
        return [
            {**blocks, **{k ^ bit: self.cross(x, bit) for k, x in blocks.items()}}
            for blocks, bit in zip(held, (bits[n], bits[-1 - n]))
        ]

    def crosses(self, x, ks):
        return [self.cross(x, k) for k in ks]


def added(first, others):
    for x in others:
        first = first + x.astype(F32)
    return first


def dp_cross(x, k, n_dp):
    return lax.ppermute(x, "dp", [(i, i ^ k) for i in range(n_dp)])


def dp_along(x, by, n_dp):
    pairs = [(i, i + by) for i in range(n_dp) if 0 <= i + by < n_dp]
    return lax.ppermute(x, "dp", pairs)


def dp_others(x, n_dp):
    return [dp_cross(x, k, n_dp) for k in range(1, n_dp)]


def body(
    n_dp,
    n_expert,
    tokens,
    cotangent,
    parents,
    valid_mask,
    routes,
    route_gates,
    norm_gains,
    w_qkv,
    w_out,
    w_gate_up,
    w_down,
):
    both = ("dp", "expert")
    micro, _, rows, width = tokens.shape
    micros = range(micro)
    count = micro * rows
    top = routes.shape[-1]
    query_width = H * HD
    kv_width = KV * HD
    local_experts = w_gate_up.shape[0]
    experts = local_experts * n_expert
    plane = Plane(n_expert)
    dp_index = lax.axis_index("dp")

    x_in = [tokens[m, 0] for m in micros]
    grad_out = [cotangent[m, 0] for m in micros]
    expert_index = lax.axis_index("expert")
    core, chip = expert_index % 2, expert_index // 2
    every, lags = range(1, plane.chips), range(1, n_dp)
    near, far = every[:-1], every[-1:]

    def over_dp(x):
        return lax.all_gather(x, "dp", axis=0, tiled=True)

    chosen = routes.reshape(count, top)[:, :, None] == jnp.arange(experts, dtype=jnp.int32)
    table = jnp.sum(jnp.where(chosen, route_gates.reshape(count, top)[:, :, None], 0.0), axis=1)
    table = table.T.reshape(n_expert, local_experts, micro, rows)
    table = lax.all_to_all(table, "expert", split_axis=0, concat_axis=0, tiled=True)
    sides = [2 * k + 1 for k in range(plane.chips)] + [2 * k for k in range(plane.chips)]
    table = jnp.take(table, expert_index ^ jnp.array(sides, jnp.int32), axis=0)
    gates = [[table[:, e, m].reshape(-1, 1, 512) for m in micros] for e in range(local_experts)]
    bias = mask_bias(
        parents.reshape(micro, -1), valid_mask.reshape(micro, -1), dp_index, n_dp, rows
    )
    bias = [bias[m] for m in micros]
    same = jnp.arange(plane.chips, dtype=jnp.int32)
    order = chip ^ same

    half = n_dp // 2

    def bands(line, chip_at, core_at):
        return [((dp_index ^ z) * plane.chips + chip_at) * 2 + core_at for z in line]

    def wide(x):
        return jnp.broadcast_to(x[None], (plane.chips,) + x.shape)

    packed = [
        jnp.concatenate(
            [w_gate_up[e], w_down[e].reshape(-1, width // FFE, FFE).swapaxes(0, 1).reshape(-1, FFE)],
            axis=1,
        )
        for e in range(local_experts)
    ]
    gains_t = jnp.pad(norm_gains.T, ((0, 0), (0, 126)))
    own_rows = jnp.concatenate([w_qkv, gains_t], axis=1)
    qkv_line, out_rows, gates, bias, order, w_first = join(
        [own_rows] + dp_others(own_rows, n_dp),
        jnp.broadcast_to(w_out.T[None], (n_dp,) + w_out.shape[::-1]),
        gates,
        bias,
        order,
        packed[0],
    )
    expert_w = [over_dp(w_first)]
    line = jnp.stack(qkv_line)
    held = plane.doubled([{0: line[:half]}, {0: line[half:]}], 0)
    out_line = lax.all_to_all(out_rows, "dp", split_axis=0, concat_axis=0, tiled=True)
    held, line_swap = join(held, plane.swap(line))
    for n in range(1, plane.chips.bit_length() - 1):
        held = plane.doubled(held, n)
    held, out_line, c_wide, w_last = join(
        held, out_line, [wide(c) for c in grad_out], packed[1]
    )
    moved = [(h, k, held[h][k]) for k in every for h in range(2)]
    out_spread = plane.exchange(wide(out_line))
    swapped = list(join(*[plane.swap(x) for _, _, x in moved]))
    lines = [range(half), range(half, n_dp)]
    places = bands(range(n_dp), chip, core) + bands(range(n_dp), chip, 1 - core)
    for c in (core, 1 - core):
        for h, k, _ in moved:
            places += bands(lines[h], chip ^ k, c)
    weight = assemble(
        [line, line_swap] + [x for _, _, x in moved] + swapped, jnp.stack(places)
    )

    (h_in, kv, gains), out_spread = join(project(x_in, weight, 2 * kv_width), out_spread)
    w_q = weight[:, :query_width]
    queries = [mm(h, w_q).astype(BF16) for h in h_in]

    c_0 = plane.exchange(c_wide[0])
    out_swap = plane.swap(out_spread)
    places = []
    for c in (core, 1 - core):
        for j in range(plane.chips):
            places += [(z * plane.chips + j) * 2 + c for z in range(n_dp)]
    w_out_t = assemble(
        [x.reshape((-1,) + x.shape[2:]) for x in (out_spread, out_swap)], jnp.stack(places)
    )
    chunks_0, kv[1], queries, w_out_t, c_0, expert_w[0] = join(
        [dp_along(kv[0], d, n_dp) for d in reversed(lags)],
        kv[1],
        queries,
        w_out_t,
        c_0,
        expert_w[0],
    )
    kv_chunks = [list(chunks_0) + [kv[0]]]
    ends = [lags[0], lags[-1]]
    between = [d for d in lags if d not in ends]
    (mixed, total), held, c_swap = join(
        attend(queries[0], kv_chunks[0], bias[0]),
        [dp_along(kv[1], d, n_dp) for d in between],
        plane.swap(c_0),
    )
    held_1 = dict(zip(between, held))
    c_1 = plane.exchange(c_wide[1])
    c_all = [[c_swap, c_0]]
    attn, lse = [mixed], [total]
    x, h = middle(attn[0], x_in[0], gains, w_out_t)
    x_mid, h_mid = [x], [h]
    held, h_others, w_last, c_1 = join(
        [dp_along(kv[1], d, n_dp) for d in ends], plane.crosses(h, every), w_last, c_1
    )
    held_1.update(zip(ends, held))
    kv_chunks.append([held_1[d] for d in reversed(lags)] + [kv[1]])
    (mixed, total), h_swap = join(
        attend(queries[1], kv_chunks[1], bias[1]),
        [plane.swap(x) for x in [h] + list(h_others)],
    )
    attn.append(mixed)
    lse.append(total)
    h_all = [[*h_swap, h, *h_others], None]
    (x, h), c_swap = join(middle(attn[1], x_in[1], gains, w_out_t), plane.swap(c_1))
    c_all.append([c_swap, c_1])
    x_mid.append(x)
    h_mid.append(h)

    def run(e, m, gate):
        out = expert_pass(
            h_all[m],
            c_all[m],
            order,
            gate,
            expert_w[e],
            n_dp,
            carried[m],
            totals[e],
            m + 1 == micro,
        )
        return out[:4], out[4:]

    def split(x):
        return x.reshape((plane.chips, -1) + x.shape[1:])

    totals, carried = [None] * local_experts, [None] * micro
    (carried[0], totals[0]), h_cross, h_swap = join(
        run(0, 0, gates[0][0]), plane.crosses(h_mid[1], every), plane.swap(h_mid[1])
    )
    h_all[1] = [h_swap] + [plane.swap(x) for x in h_cross] + [h_mid[1]] + h_cross
    (carried[1], totals[0]), w_whole, gate = join(
        run(0, 1, gates[0][1]), over_dp(w_last), gates[1][0]
    )
    expert_w.append(w_whole)

    def summed(x):
        return lax.psum_scatter(x, "dp", scatter_dimension=0, tiled=True)

    totals_s = [[summed(t) for t in totals[0]]]
    carried[0], totals[1] = run(1, 0, gate)
    y_sib_0, y_own_0, gh_sib_0, gh_own_0 = carried[0]
    gh_chips = sums(split(gh_own_0), split(plane.swap(gh_sib_0)), order)
    gate, gh_chips, y_sib_0 = join(gates[1][1], gh_chips, y_sib_0)
    (carried[1], totals[1]), gh_got, y_swap_0, totals_s[0] = join(
        run(1, 1, gate), plane.exchange(gh_chips), plane.swap(y_sib_0), totals_s[0]
    )
    y_sib_1, y_own_1, gh_sib_1, gh_own_1 = carried[1]

    def back_of(m, got):
        return middle_back(got, x_mid[m], grad_out[m], gains, w_out_t)

    def attention_back(m, grad_mixed):
        dq, *dkv = attend_back(queries[m], grad_mixed, kv_chunks[m], bias[m], lse[m])
        return dq, dkv

    def returned(dkv, ds):
        return [dp_along(dkv[n_dp - 1 - d], -d, n_dp) for d in ds]

    def weights_of(left, right):
        return weight_grad(left, right, n_dp, plane.chips, core)

    back_0, gh_swap, y_sib_1 = join(back_of(0, gh_got), plane.swap(gh_sib_1), y_sib_1)
    gh_chips = sums(split(gh_own_1), split(gh_swap), order)
    grad_mixed, gh_chips, y_swap_0 = join(back_0[3], gh_chips, y_swap_0)
    gh_got = plane.exchange(gh_chips)
    totals_s.append([summed(totals[1][0])])
    grad_q_0, dkv_0 = attention_back(0, grad_mixed)
    y_swap_0, grad_q_0 = join(y_swap_0, grad_q_0)
    grad_q_0, dkv_0, gh_got, y_chips_0, y_swap_1 = join(
        grad_q_0,
        dkv_0,
        gh_got,
        sums(split(y_own_0), split(y_swap_0), order),
        plane.swap(y_sib_1),
    )
    back_1 = back_of(1, gh_got)
    grad_x_mid, grad_branch, gain_parts, _ = zip(back_0, back_1)
    gain_mid = sum(g[:1] for g in gain_parts)
    soon, late = [lags[0], *between], [lags[-1]]
    out_bands = weights_of(grad_branch, attn)
    (grad_q_1, dkv_1), held, totals_s[1][0], y_got_0, y_swap_1, gain_swap, out_swap = join(
        attention_back(1, back_1[3]),
        returned(dkv_0, soon),
        totals_s[1][0],
        plane.exchange(y_chips_0),
        y_swap_1,
        plane.swap(gain_mid),
        plane.swap(out_bands[1]),
    )
    gain_mid = gain_mid + gain_swap
    out_got = plane.exchange(sums(out_bands[0], out_swap, same))
    held_0 = dict(zip(soon, held))
    grad_q = [grad_q_0, grad_q_1]

    held, q_bands, last_half, y_chips_1, gain_near = join(
        returned(dkv_1, ends),
        weights_of(h_in, grad_q),
        totals[1][1],
        sums(split(y_own_1), split(y_swap_1), order),
        plane.crosses(gain_mid, near),
    )
    held_1 = dict(zip(ends, held))
    held, held_late, q_swap, gain_far = join(
        returned(dkv_1, between),
        returned(dkv_0, late),
        plane.swap(q_bands[1]),
        plane.crosses(gain_mid, far),
    )
    gain_mid = added(gain_mid, gain_near + gain_far)
    held_1.update(zip(between, held))
    held_0.update(zip(late, held_late))
    totals_s[1].append(summed(last_half))
    total_0 = added(dkv_0[-1].astype(F32), [held_0[d] for d in lags])
    total_1 = added(dkv_1[-1].astype(F32), [held_1[d] for d in lags])
    grad_kv = [jnp.concatenate([t[0], t[1]], axis=1).astype(BF16) for t in (total_0, total_1)]
    kv_bands = weights_of(h_in, grad_kv)
    gain_rows = lax.dynamic_index_in_dim(
        gain_mid.reshape(n_dp, n_expert, -1), expert_index, 1, keepdims=False
    )
    gain_rows = jnp.pad(gain_rows[:, :, None], ((0, 0), (0, 0), (0, 127)))
    kv_swap, q_chips, gain_rows, out_got = join(
        plane.swap(kv_bands[1]), sums(q_bands[0], q_swap, same), gain_rows, out_got
    )
    kv_chips = sums(kv_bands[0], kv_swap, order)
    kv_own, grad_kv, q_chips = join([kv_chips[k] for k in range(plane.chips)], grad_kv, q_chips)
    grad_x = [
        input_back(grad_q[m], grad_kv[m], x_in[m], grad_x_mid[m], gains, weight) for m in micros
    ]
    out_total, out_pieces = band_totals([[out_got]], dp_index)

    def over_dp_links(pieces):
        return [dp_cross(x, z, n_dp) for z, x in zip(lags, pieces)]

    kv_sent, q_got, grad_x, totals_s, y_chips_1, out_sent = join(
        [plane.cross(kv_own[k], k) for k in every],
        plane.exchange(q_chips),
        grad_x,
        totals_s,
        y_chips_1,
        over_dp_links(out_pieces),
    )
    y_got_1 = plane.exchange(y_chips_1)
    grad_gu_s, grad_down_s = unpack(totals_s, w_gate_up.shape, w_down.shape)
    total, pieces = band_totals([[q_got], [kv_own[0], *kv_sent], [gain_rows]], dp_index)
    sent, y_got_1, grad_gu_s, grad_down_s = join(
        over_dp_links(pieces), y_got_1, grad_gu_s, grad_down_s
    )
    out_total, total = added(out_total, out_sent), added(total, sent)

    qkv_width = w_qkv.shape[1]
    grad_wqkv = total[:, :qkv_width]
    gain_in = jnp.sum(w_qkv.astype(F32) * grad_wqkv, axis=1) / norm_gains[0].astype(F32)
    x_out = [
        x_mid[m] + jnp.sum(y.astype(F32), axis=0) for m, y in enumerate((y_got_0, y_got_1))
    ]
    return (
        jnp.stack([x.astype(BF16) for x in x_out])[:, None],
        jnp.stack(grad_x)[:, None],
        jnp.stack([gain_in, total[:, qkv_width]]),
        grad_wqkv,
        out_total.T,
        grad_gu_s,
        grad_down_s,
    )


def solution(mesh):
    tokens_spec = P(None, "expert", "dp", None)
    experts_spec = P("expert", "dp", None)
    rows_spec = P(("dp", "expert"), None)
    columns_spec = P(None, ("dp", "expert"))
    return jax.shard_map(
        functools.partial(body, mesh.shape["dp"], mesh.shape["expert"]),
        mesh=mesh,
        in_specs=(
            tokens_spec,
            tokens_spec,
            P(None, "expert", None),
            P(None, "expert", None),
            tokens_spec,
            tokens_spec,
            columns_spec,
            rows_spec,
            columns_spec,
            experts_spec,
            experts_spec,
        ),
        out_specs=(
            tokens_spec,
            tokens_spec,
            columns_spec,
            rows_spec,
            columns_spec,
            experts_spec,
            experts_spec,
        ),
        check_vma=False,
    )
```

time: 906 us -> 794 us (0.88)
  waiting for transfers between devices: 295 us -> 171 us
  Pallas kernels: 242 us -> 339 us
  matrix products: 51.9 us -> 9.49 us
  other arithmetic: 70.4 us -> 29.2 us
  local copies, waits for them, and re-layouts: 61.7 us -> 73.3 us
    pallas_call x4 -> x26, Pallas kernels: 163 us -> 255 us  [the longest x4 162 us: expert_pass(): pl.pallas_call(functools.partial(expert_kernel, block, chips, shards, pre...]
    ppermute x24 -> x12, waiting for transfers between devices: 157 us -> 76.6 us  [dp_along(): return lax.ppermute(x, 'dp', pairs)]
    ppermute x36 -> x18, waiting for transfers between devices: 76.6 us -> 29 us  [cross(): lax.ppermute(x, 'expert', [(i, i ^ 2 * k) for i in range(self.count)])]
    all_to_all x1 -> x10, starting transfers between devices: 7.48 us -> 48.9 us  [the longest x9 42 us: exchange(): lax.all_to_all(x, 'expert', split_axis=0, concat_axis=0, axis_index_group...]
    dot_general x16 -> x0, matrix products: 35.8 us -> none  [the longest x8 25.8 us: mm_nt(): lax.dot_general(a, b, (((1,), (1,)), ((), ())), preferred_element_type=F32)]
    convert_element_type x17 -> x0, other arithmetic: 34.6 us -> none  [the longest x4 16.3 us: sums(): return [parts[0]] + [p.astype(BF16) for p in parts[1:]]]
    unnamed x220 -> x186, local copies, waits for them, and re-layouts: 19.9 us -> 53 us
    all_to_all x1 -> x10, waiting for transfers between devices: 0.01 us -> 30.9 us  [the longest x1 18.4 us: body(): lax.all_to_all(out_rows, 'dp', split_axis=0, concat_axis=0, tiled=True)]
  transfers between devices with their start and end apart: 97 -> 82, of which waited for: 25 -> 26; matrix products, arithmetic and copies ran while one was open for 19% -> 7% of each run, Pallas kernels for 27% -> 43%
where the time goes in v2:
time: 794 us; the launch traced here: 785 us
  Pallas kernels  339 us (43%)
  waiting for transfers between devices  171 us (22%)
  starting transfers between devices  148 us (19%)
  local copies, waits for them, and re-layouts  73.3 us (9%)
  other arithmetic  29.2 us (4%)
  between operations  15.8 us (2%)
  matrix products  9.49 us (1%)
    pallas_call x4, Pallas kernels, expert_pass(): pl.pallas_call(functools.partial(expert_kernel, block, chips, shards, pre...  162 us
    ppermute x12, waiting for transfers between devices, dp_along(): return lax.ppermute(x, 'dp', pairs)  76.6 us
    ppermute x12, starting transfers between devices, dp_along(): return lax.ppermute(x, 'dp', pairs)  53.1 us
    unnamed x186, local copies, waits for them, and re-layouts  53 us
    pallas_call x2, Pallas kernels, attend_back(): pl.pallas_call(functools.partial(attend_back_kernel, chunks), grid=(PAIRS...  50.9 us
    pallas_call x10, Pallas kernels, small_call(): pl.pallas_call(kernel, in_specs=in_specs or [NEAR] * len(inputs), out_spe...  46.8 us
    all_to_all x9, starting transfers between devices, exchange(): lax.all_to_all(x, 'expert', split_axis=0, concat_axis=0, axis_index_group...  42 us
    pallas_call x2, Pallas kernels, attend(): pl.pallas_call(functools.partial(attend_kernel, chunks), grid=(PAIRS,), i...  33.5 us
  transfers between devices with their start and end apart: 82, of which 26 were waited for; matrix products, arithmetic and copies ran while one was open for 7% of the time, Pallas kernels for 43%

profile of v2, /device:TPU:0, one launch (start us, length us, event | category | flops | bytes accessed | tf_op | source)
XLA Modules:
  0.0 785.3 jit_solution(187708585588722094)
XLA Ops:
  41.3 6.9 all-to-all-start.1
  60.8 18.4 %all-to-all-done.1 = bf16[4,48,1536]{2,1,0:T(8,128)(2,1)} async-done(((bf16[4,48,1536]{2,1,0:T(8,128)(2,1)}), bf16[4,48,1536]{2,1,0:T(8,128)(2,1)}, u32[]{:S(2)}, u32[]{:S(2)}) %all-to-all-start.1) | async-done | bytes 589856 | tf_op jit(solution)/shard_map/all_to_all | solution.py:859
  87.9 4.6 all-to-all-start.2
  100.0 9.2 %assemble.2.refs_2_.w_ref = bf16[1536,2688]{1,0:T(8,128)(2,1)S(1)} custom-call(s32[32]{0:T(128)S(1)} %stack.271.place_ref, bf16[4,48,2688]{2,1,0:T(8,128)(2,1)S(1)} %copy-done.23, bf16[4,48,2688]{2,1,0:T(8,128)(2,1)S(1)} %copy-done.53, bf16[2,48,2688]{2,1,0:T(8,128)(2,1)S(1)} %copy-done.61, bf16[2,48,2688]{2,1,0:T(8,128)(2,1)} %collective-permute-done.8.refs_3_, ...), custom_call_target="tpu_custom_call" | custom-call | flops 1024 | bytes 1024 | tf_op jit(solution)/shard_map/assemble/pallas_call | solution.py:501
  112.5 5.5 project.1
  120.2 4.7 all-to-all-start.3
  125.0 5.6 collective-permute-start.16
  135.2 4.8 fusion.4.q_ref
  140.1 4.6 fusion.7.q_ref
  149.9 5.1 collective-permute-done.17.refs_1_.refs_5_
  155.8 10.2 %collective-permute-done.18.refs_2_.refs_6_ = bf16[256,1024]{1,0:T(8,128)(2,1)} collective-permute-done((bf16[256,1024]{1,0:T(8,128)(2,1)S(1)}, bf16[256,1024]{1,0:T(8,128)(2,1)}, u32[]{:S(2)}, u32[]{:S(2)}) %collective-permute-start.18) | collective-permute-done | bytes 524320 | tf_op jit(solution)/shard_map/ppermute | solution.py:773
  166.0 4.6 all-to-all-start.4
  170.7 31.5 %collective-permute-start.20 = (bf16[256,1024]{1,0:T(8,128)(2,1)S(1)}, bf16[256,1024]{1,0:T(8,128)(2,1)S(1)}, u32[]{:S(2)}, u32[]{:S(2)}) collective-permute-start(bf16[256,1024]{1,0:T(8,128)(2,1)S(1)} %get-tuple-element.294.refs_3_.refs_7_), channel_id=1, source_target_pairs={{0,16},{8,24},{1,17},{9,25},{2,18},{10,26},{3,19},{11,27},{4,20},{... | collective-permute-start | bytes 1572872 | tf_op jit(solution)/shard_map/ppermute | solution.py:773
  202.2 16.7 %path_attention.2 = (bf16[256,1536]{1,0:T(8,128)(2,1)}, f32[4,8,256]{2,1,0:T(8,128)}) custom-call(bf16[256,1536]{1,0:T(8,128)(2,1)} %fusion.4.q_ref, bf16[256,1024]{1,0:T(8,128)(2,1)} %copy-done.72, bf16[256,1024]{1,0:T(8,128)(2,1)} %copy-done.73, bf16[256,1024]{1,0:T(8,128)(2,1)} %collective-permute-done.18.refs_2_.refs_6_, bf16[256,1024]{1,0:T(8,128)(2,1)} %copy-done.13, ...), custom_call_target="tpu_custom_call" | custom-call | flops 25165824 | bytes 1048576 | tf_op jit(solution)/shard_map/path_attention/pallas_call | solution.py:106
  220.3 4.8 middle.2
  233.2 10.2 %collective-permute-done.22.refs_2_.refs_6_ = bf16[256,1024]{1,0:T(8,128)(2,1)S(1)} collective-permute-done((bf16[256,1024]{1,0:T(8,128)(2,1)S(1)}, bf16[256,1024]{1,0:T(8,128)(2,1)S(1)}, u32[]{:S(2)}, u32[]{:S(2)}) %collective-permute-start.22) | collective-permute-done | bytes 524320 | tf_op jit(solution)/shard_map/ppermute | solution.py:773
  243.4 10.1 %collective-permute-done.23.refs_0_.refs_4_ = bf16[256,1024]{1,0:T(8,128)(2,1)} collective-permute-done((bf16[256,1024]{1,0:T(8,128)(2,1)S(1)}, bf16[256,1024]{1,0:T(8,128)(2,1)}, u32[]{:S(2)}, u32[]{:S(2)}) %collective-permute-start.23) | collective-permute-done | bytes 524320 | tf_op jit(solution)/shard_map/ppermute | solution.py:773
  253.5 11.1 %collective-permute-done.25.refs_6_ = bf16[256,1536]{1,0:T(8,128)(2,1)} collective-permute-done((bf16[256,1536]{1,0:T(8,128)(2,1)}, bf16[256,1536]{1,0:T(8,128)(2,1)}, u32[]{:S(2)}, u32[]{:S(2)}) %collective-permute-start.25) | collective-permute-done | bytes 786464 | tf_op jit(solution)/shard_map/ppermute | solution.py:739
  265.8 16.7 %path_attention.3 = (bf16[256,1536]{1,0:T(8,128)(2,1)}, f32[4,8,256]{2,1,0:T(8,128)}) custom-call(bf16[256,1536]{1,0:T(8,128)(2,1)} %fusion.7.q_ref, bf16[256,1024]{1,0:T(8,128)(2,1)} %collective-permute-done.23.refs_0_.refs_4_, bf16[256,1024]{1,0:T(8,128)(2,1)} %copy-done.71, bf16[256,1024]{1,0:T(8,128)(2,1)} %copy-done.74, bf16[256,1024]{1,0:T(8,128)(2,1)} %copy-done.12, ...), custom_call_target="tpu_custom_call" | custom-call | flops 25165824 | bytes 1048576 | tf_op jit(solution)/shard_map/path_attention/pallas_call | solution.py:106
  293.2 39.3 %expert_pass.4 = (bf16[1024,1536]{1,0:T(8,128)(2,1)}, bf16[1024,1536]{1,0:T(8,128)(2,1)}, bf16[1024,1536]{1,0:T(8,128)(2,1)}, bf16[1024,1536]{1,0:T(8,128)(2,1)}...) custom-call(bf16[256,1536]{1,0:T(8,128)(2,1)} %copy-done.75, bf16[256,1536]{1,0:T(8,128)(2,1)} %collective-permute-done.28.refs_1_, ...), custom_call_target="tpu_custom_call" | custom-call | flops 1572864 | bytes 1572864 | tf_op jit(solution)/shard_map/expert_pass/pallas_call | solution.py:443
  337.7 41.2 %expert_pass.5 = (bf16[1024,1536]{1,0:T(8,128)(2,1)}, bf16[1024,1536]{1,0:T(8,128)(2,1)}, bf16[1024,1536]{1,0:T(8,128)(2,1)}, bf16[1024,1536]{1,0:T(8,128)(2,1)}...) custom-call(bf16[256,1536]{1,0:T(8,128)(2,1)} %collective-permute-done.35.refs_0_, bf16[256,1536]{1,0:T(8,128)(2,1)} %copy-done.76, ...), custom_call_target="tpu_custom_call" | custom-call | flops 1572864 | bytes 1572864 | tf_op jit(solution)/shard_map/expert_pass/pallas_call | solution.py:443
  379.5 40.5 %expert_pass.6 = (bf16[1024,1536]{1,0:T(8,128)(2,1)}, bf16[1024,1536]{1,0:T(8,128)(2,1)}, bf16[1024,1536]{1,0:T(8,128)(2,1)}, bf16[1024,1536]{1,0:T(8,128)(2,1)}...) custom-call(bf16[256,1536]{1,0:T(8,128)(2,1)} %copy-done.75, ...), custom_call_target="tpu_custom_call", output_to_operand_aliasing={{0}: (13, {}), {1}: (14, {}), {2}: (15, {}), {3}: (16, {})} | custom-call | flops 1572864 | bytes 1572864 | tf_op jit(solution)/shard_map/expert_pass/pallas_call | solution.py:443
  420.5 5.5 collective-permute-done.39
  431.3 4.7 all-to-all-start.5
  436.1 41.3 %expert_pass.7 = (bf16[1024,1536]{1,0:T(8,128)(2,1)}, bf16[1024,1536]{1,0:T(8,128)(2,1)}, bf16[1024,1536]{1,0:T(8,128)(2,1)}, bf16[1024,1536]{1,0:T(8,128)(2,1)}...) custom-call(bf16[256,1536]{1,0:T(8,128)(2,1)} %collective-permute-do, ...), custom_call_target="tpu_custom_call", output_to_operand_aliasing={{0}: (13, {}), {1}: (14, {}), {2}: (15, {}), {3}: (16, {})} | custom-call | flops 1572864 | bytes 1572864 | tf_op jit(solution)/shard_map/expert_pass/pallas_call | solution.py:443
  480.0 6.4 middle_back.2
  494.6 4.9 all-to-all-start.6
  499.5 25.3 %path_attention_back.2 = (bf16[256,1536]{1,0:T(8,128)(2,1)}, bf16[2,256,512]{2,1,0:T(8,128)(2,1)}, bf16[2,256,512]{2,1,0:T(8,128)(2,1)}, bf16[2,256,512]{2,1,0:T(8,128)(2,1)}, bf16[2,256,512]{2,1,0:T(8,128)(2,1)}) custom-call(bf16[256,1536]{1,0:T(8,128)(2,1)} %fusion.4.q_ref, bf16[256,1536]{1,0:T(8,128)(2,1)} %copy-done.59, bf16[256,1024]{1,0:T(8,128)(2,1)} %copy-done.72, ...), custom_call_target="tpu_custom_call" | custom-call | flops 62914560 | bytes 1048576 | tf_op jit(solution)/shard_map/path_attention_back/pallas_call | solution.py:179
  531.8 4.8 all-to-all-done.6.got_ref
  536.6 4.7 all-to-all-start.7
  542.7 5.7 middle_back.3
  548.5 4.3 weight_grad.3
  557.4 25.6 %path_attention_back.3 = (bf16[256,1536]{1,0:T(8,128)(2,1)}, bf16[2,256,512]{2,1,0:T(8,128)(2,1)}, bf16[2,256,512]{2,1,0:T(8,128)(2,1)}, bf16[2,256,512]{2,1,0:T(8,128)(2,1)}, bf16[2,256,512]{2,1,0:T(8,128)(2,1)}) custom-call(bf16[256,1536]{1,0:T(8,128)(2,1)} %fusion.7.q_ref, bf16[256,1536]{1,0:T(8,128)(2,1)} %copy-done.58, ...), custom_call_target="tpu_custom_call" | custom-call | flops 62914560 | bytes 1048576 | tf_op jit(solution)/shard_map/path_attention_back/pallas_call | solution.py:179
  583.1 7.4 collective-permute-done.44
  599.1 4.2 weight_grad.4
  610.0 7.8 collective-permute-done.49
  628.1 4.6 all-to-all-start.8
  636.7 22.0 %collective-permute-done.47 = bf16[2,256,512]{2,1,0:T(8,128)(2,1)} collective-permute-done((bf16[2,256,512]{2,1,0:T(8,128)(2,1)}, bf16[2,256,512]{2,1,0:T(8,128)(2,1)}, u32[]{:S(2)}, u32[]{:S(2)}) %collective-permute-start.47) | collective-permute-done | bytes 524320 | tf_op jit(solution)/shard_map/ppermute | solution.py:773
  678.5 4.5 all-to-all-start.9
  689.8 9.6 %collective-permute-done.59 = bf16[48,1536]{1,0:T(8,128)(2,1)S(1)} collective-permute-done((bf16[48,1536]{1,0:T(8,128)(2,1)S(1)}, bf16[48,1536]{1,0:T(8,128)(2,1)S(1)}, u32[]{:S(2)}, u32[]{:S(2)}) %collective-permute-start.59) | collective-permute-done | bytes 147488 | tf_op jit(solution)/shard_map/ppermute | solution.py:768
  701.2 5.9 input_back.2
  707.1 5.9 input_back.3
  713.9 6.7 collective-permute-done.56.refs_2_
  720.6 9.0 %collective-permute-done.58.refs_4_ = bf16[4,48,1024]{2,1,0:T(8,128)(2,1)} collective-permute-done((bf16[4,48,1024]{2,1,0:T(8,128)(2,1)}, bf16[4,48,1024]{2,1,0:T(8,128)(2,1)}, u32[]{:S(2)}, u32[]{:S(2)}) %collective-permute-start.58) | collective-permute-done | bytes 393248 | tf_op jit(solution)/shard_map/ppermute | solution.py:739
  729.7 4.7 all-to-all-start.10
  741.4 4.3 collective-permute-start.64
  753.0 9.4 %collective-permute-done.63 = bf16[48,2688]{1,0:T(8,128)(2,1)S(1)} collective-permute-done((bf16[48,2688]{1,0:T(8,128)(2,1)S(1)}, bf16[48,2688]{1,0:T(8,128)(2,1)S(1)}, u32[]{:S(2)}, u32[]{:S(2)}) %collective-permute-start.63) | collective-permute-done | bytes 258080 | tf_op jit(solution)/shard_map/ppermute | solution.py:768
  763.1 7.7 all-to-all-done.10
  (412 shorter events, 216.0 us)
Async XLA Ops:
  19.9 146.1 %all-gather.3.cloned.1.call-start = ((), (), s32[]{:S(2)}) async-start(), calls=%async_computation.15 | async-start | bytes 5898240 | tf_op jit(solution)/shard_map/all_gather | solution.py:815
  41.3 37.8 %all-to-all-start.1 = ((bf16[4,48,1536]{2,1,0:T(8,128)(2,1)}), bf16[4,48,1536]{2,1,0:T(8,128)(2,1)}, u32[]{:S(2)}, u32[]{:S(2)}) async-start(bf16[4,48,1536]{2,1,0:T(8,128)(2,1)} %broadcast_in_dim.84), calls=%async_computation.1 | async-start | bytes 1179648 | tf_op jit(solution)/shard_map/all_to_all | solution.py:859
  55.2 23.9 %collective-permute-start.6 = (bf16[2,48,2688]{2,1,0:T(8,128)(2,1)}, bf16[2,48,2688]{2,1,0:T(8,128)(2,1)}, u32[]{:S(2)}, u32[]{:S(2)}) collective-permute-start(bf16[2,48,2688]{2,1,0:T(8,128)(2,1)} %pad_maximum_fusion.5), channel_id=1, source_target_pairs={{0,4},{1,5},{2,6},{3,7},{4,0},{5,1},{6,2},{7,3},{8,12},{9,13},{10,... | collective-permute-start | bytes 1548296 | tf_op jit(solution)/shard_map/ppermute | solution.py:739
  56.4 23.4 %collective-permute-start.7 = (bf16[2,48,2688]{2,1,0:T(8,128)(2,1)S(1)}, bf16[2,48,2688]{2,1,0:T(8,128)(2,1)}, u32[]{:S(2)}, u32[]{:S(2)}) collective-permute-start(bf16[2,48,2688]{2,1,0:T(8,128)(2,1)S(1)} %collective-permute-done.3.refs_2_), channel_id=1, source_target_pairs={{0,4},{1,5},{2,6},{3,7},{4,0},{5,1},{6,2},{7,3},{8,12},{9,13},{10,... | collective-permute-start | bytes 1548296 | tf_op jit(solution)/shard_map/ppermute | solution.py:739
  57.2 22.6 %collective-permute-start.8 = (bf16[2,48,2688]{2,1,0:T(8,128)(2,1)}, bf16[2,48,2688]{2,1,0:T(8,128)(2,1)}, u32[]{:S(2)}, u32[]{:S(2)}) collective-permute-start(bf16[2,48,2688]{2,1,0:T(8,128)(2,1)} %pad_maximum_fusion.6), channel_id=1, source_target_pairs={{0,2},{1,3},{2,0},{3,1},{4,6},{5,7},{6,4},{7,5},{8,10},{9,11},{10,... | collective-permute-start | bytes 1548296 | tf_op jit(solution)/shard_map/ppermute | solution.py:739
  57.8 23.4 %collective-permute-start.9 = (bf16[2,48,2688]{2,1,0:T(8,128)(2,1)}, bf16[2,48,2688]{2,1,0:T(8,128)(2,1)}, u32[]{:S(2)}, u32[]{:S(2)}) collective-permute-start(bf16[2,48,2688]{2,1,0:T(8,128)(2,1)} %collective-permute-done.4.refs_5_), channel_id=1, source_target_pairs={{0,2},{1,3},{2,0},{3,1},{4,6},{5,7},{6,4},{7,5},{8,10},{9,11},{10,... | collective-permute-start | bytes 1548296 | tf_op jit(solution)/shard_map/ppermute | solution.py:739
  87.9 31.9 %all-to-all-start.2 = ((bf16[4,4,48,1536]{3,2,1,0:T(8,128)(2,1)}), bf16[4,4,48,1536]{3,2,1,0:T(8,128)(2,1)}, u32[]{:S(2)}, u32[]{:S(2)}) async-start(bf16[4,4,48,1536]{3,2,1,0:T(8,128)(2,1)} %broadcast_in_dim.98), calls=%async_computation.2 | async-start | bytes 4718592 | tf_op jit(solution)/shard_map/all_to_all | solution.py:743
  119.8 24.9 %collective-permute-start.19 = (bf16[4,4,48,1536]{3,2,1,0:T(8,128)(2,1)}, bf16[4,4,48,1536]{3,2,1,0:T(8,128)(2,1)}, u32[]{:S(2)}, u32[]{:S(2)}) collective-permute-start(bf16[4,4,48,1536]{3,2,1,0:T(8,128)(2,1)} %all-to-all-done.2), channel_id=1, source_target_pairs={{0,1},{1,0},{2,3},{3,2},{4,5},{5,4},{6,7},{7,6},{8,9},{9,8},{10,11... | collective-permute-start | bytes 7077896 | tf_op jit(solution)/shard_map/ppermute | solution.py:736
  120.2 45.8 %all-to-all-start.3 = ((bf16[4,256,1536]{2,1,0:T(8,128)(2,1)}), bf16[4,256,1536]{2,1,0:T(8,128)(2,1)}, u32[]{:S(2)}, u32[]{:S(2)}) async-start(bf16[4,256,1536]{2,1,0:T(8,128)(2,1)} %broadcast_in_dim.95), calls=%async_computation.3 | async-start | bytes 6291456 | tf_op jit(solution)/shard_map/all_to_all | solution.py:743
  125.0 24.9 %collective-permute-start.16 = (bf16[256,1024]{1,0:T(8,128)(2,1)S(1)}, bf16[256,1024]{1,0:T(8,128)(2,1)S(1)}, u32[]{:S(2)}, u32[]{:S(2)}) collective-permute-start(bf16[256,1024]{1,0:T(8,128)(2,1)S(1)} %get-tuple-element.280.refs_3_.refs_7_), channel_id=1, source_target_pairs={{0,24},{1,25},{2,26},{3,27},{4,28},{5,29},{6,30},{7,31}} | collective-permute-start | bytes 1572872 | tf_op jit(solution)/shard_map/ppermute | solution.py:773
  130.6 24.4 %collective-permute-start.17 = (bf16[256,1024]{1,0:T(8,128)(2,1)S(1)}, bf16[256,1024]{1,0:T(8,128)(2,1)S(1)}, u32[]{:S(2)}, u32[]{:S(2)}) collective-permute-start(bf16[256,1024]{1,0:T(8,128)(2,1)S(1)} %get-tuple-element.280.refs_3_.refs_7_), channel_id=1, source_target_pairs={{0,16},{8,24},{1,17},{9,25},{2,18},{10,26},{3,19},{11,27},{4,20},{... | collective-permute-start | bytes 1572872 | tf_op jit(solution)/shard_map/ppermute | solution.py:773
  132.8 33.2 %collective-permute-start.18 = (bf16[256,1024]{1,0:T(8,128)(2,1)S(1)}, bf16[256,1024]{1,0:T(8,128)(2,1)}, u32[]{:S(2)}, u32[]{:S(2)}) collective-permute-start(bf16[256,1024]{1,0:T(8,128)(2,1)S(1)} %get-tuple-element.280.refs_3_.refs_7_), channel_id=1, source_target_pairs={{0,8},{8,16},{16,24},{1,9},{9,17},{17,25},{2,10},{10,18},{18,26},{... | collective-permute-start | bytes 1572872 | tf_op jit(solution)/shard_map/ppermute | solution.py:773
  166.0 53.0 %collective-permute-start.21 = (bf16[4,256,1536]{2,1,0:T(8,128)(2,1)}, bf16[4,256,1536]{2,1,0:T(8,128)(2,1)}, u32[]{:S(2)}, u32[]{:S(2)}) collective-permute-start(bf16[4,256,1536]{2,1,0:T(8,128)(2,1)} %all-to-all-done.3.refs_9_), channel_id=1, source_target_pairs={{0,1},{1,0},{2,3},{3,2},{4,5},{5,4},{6,7},{7,6},{8,9},{9,8},{10,11... | collective-permute-start | bytes 9437192 | tf_op jit(solution)/shard_map/ppermute | solution.py:736
  166.0 67.2 %all-to-all-start.4 = ((bf16[4,256,1536]{2,1,0:T(8,128)(2,1)}), bf16[4,256,1536]{2,1,0:T(8,128)(2,1)}, u32[]{:S(2)}, u32[]{:S(2)}) async-start(bf16[4,256,1536]{2,1,0:T(8,128)(2,1)} %broadcast_in_dim.97), calls=%async_computation.4 | async-start | bytes 6291456 | tf_op jit(solution)/shard_map/all_to_all | solution.py:743
  170.6 208.2 %all-gather.5.cloned.1.call-start = ((), (), s32[]{:S(2)}) async-start(), calls=%async_computation.16 | async-start | bytes 5898240 | tf_op jit(solution)/shard_map/all_gather | solution.py:815
  170.7 48.3 %collective-permute-start.20 = (bf16[256,1024]{1,0:T(8,128)(2,1)S(1)}, bf16[256,1024]{1,0:T(8,128)(2,1)S(1)}, u32[]{:S(2)}, u32[]{:S(2)}) collective-permute-start(bf16[256,1024]{1,0:T(8,128)(2,1)S(1)} %get-tuple-element.294.refs_3_.refs_7_), channel_id=1, source_target_pairs={{0,16},{8,24},{1,17},{9,25},{2,18},{10,26},{3,19},{11,27},{4,20},{... | collective-permute-start | bytes 1572872 | tf_op jit(solution)/shard_map/ppermute | solution.py:773
  226.3 27.2 %collective-permute-start.24 = (bf16[256,1536]{1,0:T(8,128)(2,1)}, bf16[256,1536]{1,0:T(8,128)(2,1)}, u32[]{:S(2)}, u32[]{:S(2)}) collective-permute-start(bf16[256,1536]{1,0:T(8,128)(2,1)} %get-tuple-element.301.refs_4_), channel_id=1, source_target_pairs={{0,2},{1,3},{2,0},{3,1},{4,6},{5,7},{6,4},{7,5},{8,10},{9,11},{10,... | collective-permute-start | bytes 2359304 | tf_op jit(solution)/shard_map/ppermute | solution.py:739
  228.2 36.3 %collective-permute-start.25 = (bf16[256,1536]{1,0:T(8,128)(2,1)}, bf16[256,1536]{1,0:T(8,128)(2,1)}, u32[]{:S(2)}, u32[]{:S(2)}) collective-permute-start(bf16[256,1536]{1,0:T(8,128)(2,1)} %get-tuple-element.301.refs_4_), channel_id=1, source_target_pairs={{0,4},{1,5},{2,6},{3,7},{4,0},{5,1},{6,2},{7,3},{8,12},{9,13},{10,... | collective-permute-start | bytes 2359304 | tf_op jit(solution)/shard_map/ppermute | solution.py:739
  229.7 34.9 %collective-permute-start.26 = (bf16[256,1536]{1,0:T(8,128)(2,1)}, bf16[256,1536]{1,0:T(8,128)(2,1)}, u32[]{:S(2)}, u32[]{:S(2)}) collective-permute-start(bf16[256,1536]{1,0:T(8,128)(2,1)} %get-tuple-element.301.refs_4_), channel_id=1, source_target_pairs={{0,6},{1,7},{2,4},{3,5},{4,2},{5,3},{6,0},{7,1},{8,14},{9,15},{10,... | collective-permute-start | bytes 2359304 | tf_op jit(solution)/shard_map/ppermute | solution.py:739
  264.6 212.9 %reduce-scatter.7.cloned.1.call-start = ((), (), s32[]{:S(2)}) async-start(), calls=%async_computation.18 | async-start | bytes 1474560 | tf_op jit(solution)/shard_map/reduce_scatter | solution.py:958
  264.6 25.1 %collective-permute-start.31 = (bf16[4,256,1536]{2,1,0:T(8,128)(2,1)}, bf16[4,256,1536]{2,1,0:T(8,128)(2,1)}, u32[]{:S(2)}, u32[]{:S(2)}) collective-permute-start(bf16[4,256,1536]{2,1,0:T(8,128)(2,1)} %all-to-all-done.4.refs_9_), channel_id=1, source_target_pairs={{0,1},{1,0},{2,3},{3,2},{4,5},{5,4},{6,7},{7,6},{8,9},{9,8},{10,11... | collective-permute-start | bytes 9437192 | tf_op jit(solution)/shard_map/ppermute | solution.py:736
  289.7 42.9 %collective-permute-start.32 = (bf16[256,1536]{1,0:T(8,128)(2,1)S(1)}, bf16[256,1536]{1,0:T(8,128)(2,1)}, u32[]{:S(2)}, u32[]{:S(2)}) collective-permute-start(bf16[256,1536]{1,0:T(8,128)(2,1)S(1)} %get-tuple-element.331.refs_4_), channel_id=1, source_target_pairs={{0,2},{1,3},{2,0},{3,1},{4,6},{5,7},{6,4},{7,5},{8,10},{9,11},{10,... | collective-permute-start | bytes 2359304 | tf_op jit(solution)/shard_map/ppermute | solution.py:739
  291.1 41.5 %collective-permute-start.33 = (bf16[256,1536]{1,0:T(8,128)(2,1)S(1)}, bf16[256,1536]{1,0:T(8,128)(2,1)}, u32[]{:S(2)}, u32[]{:S(2)}) collective-permute-start(bf16[256,1536]{1,0:T(8,128)(2,1)S(1)} %get-tuple-element.331.refs_4_), channel_id=1, source_target_pairs={{0,4},{1,5},{2,6},{3,7},{4,0},{5,1},{6,2},{7,3},{8,12},{9,13},{10,... | collective-permute-start | bytes 2359304 | tf_op jit(solution)/shard_map/ppermute | solution.py:739
  291.8 40.8 %collective-permute-start.34 = (bf16[256,1536]{1,0:T(8,128)(2,1)S(1)}, bf16[256,1536]{1,0:T(8,128)(2,1)}, u32[]{:S(2)}, u32[]{:S(2)}) collective-permute-start(bf16[256,1536]{1,0:T(8,128)(2,1)S(1)} %get-tuple-element.331.refs_4_), channel_id=1, source_target_pairs={{0,6},{1,7},{2,4},{3,5},{4,2},{5,3},{6,0},{7,1},{8,14},{9,15},{10,... | collective-permute-start | bytes 2359304 | tf_op jit(solution)/shard_map/ppermute | solution.py:739
  293.2 39.4 %collective-permute-start.35 = (bf16[256,1536]{1,0:T(8,128)(2,1)S(1)}, bf16[256,1536]{1,0:T(8,128)(2,1)}, u32[]{:S(2)}, u32[]{:S(2)}) collective-permute-start(bf16[256,1536]{1,0:T(8,128)(2,1)S(1)} %get-tuple-element.331.refs_4_), channel_id=1, source_target_pairs={{0,1},{1,0},{2,3},{3,2},{4,5},{5,4},{6,7},{7,6},{8,9},{9,8},{10,11... | collective-permute-start | bytes 2359304 | tf_op jit(solution)/shard_map/ppermute | solution.py:736
  378.9 98.6 %reduce-scatter.5.cloned.1.call-start = ((), (), s32[]{:S(2)}) async-start(), calls=%async_computation.17 | async-start | bytes 4423680 | tf_op jit(solution)/shard_map/reduce_scatter | solution.py:958
  431.0 46.5 %collective-permute-start.40 = (bf16[1024,1536]{1,0:T(8,128)(2,1)}, bf16[1024,1536]{1,0:T(8,128)(2,1)}, u32[]{:S(2)}, u32[]{:S(2)}) collective-permute-start(bf16[1024,1536]{1,0:T(8,128)(2,1)} %get-tuple-element.372), channel_id=1, source_target_pairs={{0,1},{1,0},{2,3},{3,2},{4,5},{5,4},{6,7},{7,6},{8,9},{9,8},{10,11... | collective-permute-start | bytes 9437192 | tf_op jit(solution)/shard_map/ppermute | solution.py:736
  431.3 46.1 %all-to-all-start.5 = ((bf16[4,256,1536]{2,1,0:T(8,128)(2,1)}), bf16[4,256,1536]{2,1,0:T(8,128)(2,1)}, u32[]{:S(2)}, u32[]{:S(2)}) async-start(bf16[4,256,1536]{2,1,0:T(8,128)(2,1)} %copy-done.8), calls=%async_computation.5 | async-start | bytes 6291456 | tf_op jit(solution)/shard_map/all_to_all | solution.py:743
  436.0 154.4 %reduce-scatter.9.cloned.1.call-start = ((), (), s32[]{:S(2)}) async-start(), calls=%async_computation.19 | async-start | bytes 4423680 | tf_op jit(solution)/shard_map/reduce_scatter | solution.py:958
  489.3 47.3 %collective-permute-start.42 = (bf16[1024,1536]{1,0:T(8,128)(2,1)}, bf16[1024,1536]{1,0:T(8,128)(2,1)}, u32[]{:S(2)}, u32[]{:S(2)}) collective-permute-start(bf16[1024,1536]{1,0:T(8,128)(2,1)} %get-tuple-element.398), channel_id=1, source_target_pairs={{0,1},{1,0},{2,3},{3,2},{4,5},{5,4},{6,7},{7,6},{8,9},{9,8},{10,11... | collective-permute-start | bytes 9437192 | tf_op jit(solution)/shard_map/ppermute | solution.py:736
  494.6 42.0 %all-to-all-start.6 = ((bf16[4,256,1536]{2,1,0:T(8,128)(2,1)}), bf16[4,256,1536]{2,1,0:T(8,128)(2,1)}, u32[]{:S(2)}, u32[]{:S(2)}) async-start(bf16[4,256,1536]{2,1,0:T(8,128)(2,1)} %copy-done.9), calls=%async_computation.8 | async-start | bytes 6291456 | tf_op jit(solution)/shard_map/all_to_all | solution.py:743
  536.6 53.8 %all-to-all-start.7 = ((bf16[4,256,1536]{2,1,0:T(8,128)(2,1)}), bf16[4,256,1536]{2,1,0:T(8,128)(2,1)}, u32[]{:S(2)}, u32[]{:S(2)}) async-start(bf16[4,256,1536]{2,1,0:T(8,128)(2,1)} %copy-done.7), calls=%async_computation.10 | async-start | bytes 6291456 | tf_op jit(solution)/shard_map/all_to_all | solution.py:743
  554.2 36.2 %collective-permute-start.46 = (bf16[4,4,48,1536]{3,2,1,0:T(8,128)(2,1)}, bf16[4,4,48,1536]{3,2,1,0:T(8,128)(2,1)}, u32[]{:S(2)}, u32[]{:S(2)}) collective-permute-start(bf16[4,4,48,1536]{3,2,1,0:T(8,128)(2,1)} %get-tuple-element.417), channel_id=1, source_target_pairs={{0,1},{1,0},{2,3},{3,2},{4,5},{5,4},{6,7},{7,6},{8,9},{9,8},{10,11... | collective-permute-start | bytes 7077896 | tf_op jit(solution)/shard_map/ppermute | solution.py:736
  554.2 28.8 %collective-permute-start.43 = (bf16[2,256,512]{2,1,0:T(8,128)(2,1)}, bf16[2,256,512]{2,1,0:T(8,128)(2,1)}, u32[]{:S(2)}, u32[]{:S(2)}) collective-permute-start(bf16[2,256,512]{2,1,0:T(8,128)(2,1)} %get-tuple-element.408), channel_id=1, source_target_pairs={{8,0},{16,8},{24,16},{9,1},{17,9},{25,17},{10,2},{18,10},{26,18},{... | collective-permute-start | bytes 1572872 | tf_op jit(solution)/shard_map/ppermute | solution.py:773
  555.5 34.9 %collective-permute-start.44 = (bf16[2,256,512]{2,1,0:T(8,128)(2,1)S(1)}, bf16[2,256,512]{2,1,0:T(8,128)(2,1)}, u32[]{:S(2)}, u32[]{:S(2)}) collective-permute-start(bf16[2,256,512]{2,1,0:T(8,128)(2,1)S(1)} %copy-done.90), channel_id=1, source_target_pairs={{16,0},{24,8},{17,1},{25,9},{18,2},{26,10},{19,3},{27,11},{20,4},{... | collective-permute-start | bytes 1572872 | tf_op jit(solution)/shard_map/ppermute | solution.py:773
  556.9 26.2 %collective-permute-start.45 = (f32[1,1536]{1,0:T(1,128)S(1)}, f32[1,1536]{1,0:T(1,128)S(1)}, u32[]{:S(2)}, u32[]{:S(2)}) collective-permute-start(f32[1,1536]{1,0:T(1,128)S(1)} %slice_add_fusion), channel_id=1, source_target_pairs={{0,1},{1,0},{2,3},{3,2},{4,5},{5,4},{6,7},{7,6},{8,9},{9,8},{10,11... | collective-permute-start | bytes 18440 | tf_op jit(solution)/shard_map/ppermute | solution.py:736
  590.5 27.4 %collective-permute-start.49 = (bf16[2,256,512]{2,1,0:T(8,128)(2,1)}, bf16[2,256,512]{2,1,0:T(8,128)(2,1)S(1)}, u32[]{:S(2)}, u32[]{:S(2)}) collective-permute-start(bf16[2,256,512]{2,1,0:T(8,128)(2,1)} %get-tuple-element.424), channel_id=1, source_target_pairs={{8,0},{16,8},{24,16},{9,1},{17,9},{25,17},{10,2},{18,10},{26,18},{... | collective-permute-start | bytes 1572872 | tf_op jit(solution)/shard_map/ppermute | solution.py:773
  592.0 25.8 %collective-permute-start.50 = (bf16[2,256,512]{2,1,0:T(8,128)(2,1)}, bf16[2,256,512]{2,1,0:T(8,128)(2,1)S(1)}, u32[]{:S(2)}, u32[]{:S(2)}) collective-permute-start(bf16[2,256,512]{2,1,0:T(8,128)(2,1)} %get-tuple-element.425), channel_id=1, source_target_pairs={{24,0},{25,1},{26,2},{27,3},{28,4},{29,5},{30,6},{31,7}} | collective-permute-start | bytes 1572872 | tf_op jit(solution)/shard_map/ppermute | solution.py:773
  617.8 40.9 %collective-permute-start.53 = (bf16[4,4,48,1536]{3,2,1,0:T(8,128)(2,1)}, bf16[4,4,48,1536]{3,2,1,0:T(8,128)(2,1)}, u32[]{:S(2)}, u32[]{:S(2)}) collective-permute-start(bf16[4,4,48,1536]{3,2,1,0:T(8,128)(2,1)} %get-tuple-element.434), channel_id=1, source_target_pairs={{0,1},{1,0},{2,3},{3,2},{4,5},{5,4},{6,7},{7,6},{8,9},{9,8},{10,11... | collective-permute-start | bytes 7077896 | tf_op jit(solution)/shard_map/ppermute | solution.py:736
  619.2 39.5 %collective-permute-start.47 = (bf16[2,256,512]{2,1,0:T(8,128)(2,1)}, bf16[2,256,512]{2,1,0:T(8,128)(2,1)}, u32[]{:S(2)}, u32[]{:S(2)}) collective-permute-start(bf16[2,256,512]{2,1,0:T(8,128)(2,1)} %get-tuple-element.422), channel_id=1, source_target_pairs={{16,0},{24,8},{17,1},{25,9},{18,2},{26,10},{19,3},{27,11},{20,4},{... | collective-permute-start | bytes 1572872 | tf_op jit(solution)/shard_map/ppermute | solution.py:773
  628.1 45.0 %all-to-all-start.8 = ((bf16[4,4,48,1536]{3,2,1,0:T(8,128)(2,1)}), bf16[4,4,48,1536]{3,2,1,0:T(8,128)(2,1)}, u32[]{:S(2)}, u32[]{:S(2)}) async-start(bf16[4,4,48,1536]{3,2,1,0:T(8,128)(2,1)} %copy-done.11), calls=%async_computation.11 | async-start | bytes 4718592 | tf_op jit(solution)/shard_map/all_to_all | solution.py:743
  632.7 81.2 %reduce-scatter.11.cloned.1.call-start = ((), (), s32[]{:S(2)}) async-start(), calls=%async_computation.20 | async-start | bytes 1474560 | tf_op jit(solution)/shard_map/reduce_scatter | solution.py:958
  678.5 51.2 %all-to-all-start.9 = ((bf16[4,4,48,1536]{3,2,1,0:T(8,128)(2,1)}), bf16[4,4,48,1536]{3,2,1,0:T(8,128)(2,1)}, u32[]{:S(2)}, u32[]{:S(2)}) async-start(bf16[4,4,48,1536]{3,2,1,0:T(8,128)(2,1)} %copy-done.10), calls=%async_computation.12 | async-start | bytes 4718592 | tf_op jit(solution)/shard_map/all_to_all | solution.py:743
  683.1 37.6 %collective-permute-start.56 = (bf16[4,48,1024]{2,1,0:T(8,128)(2,1)}, bf16[4,48,1024]{2,1,0:T(8,128)(2,1)}, u32[]{:S(2)}, u32[]{:S(2)}) collective-permute-start(bf16[4,48,1024]{2,1,0:T(8,128)(2,1)} %get-tuple-element.451), channel_id=1, source_target_pairs={{0,2},{1,3},{2,0},{3,1},{4,6},{5,7},{6,4},{7,5},{8,10},{9,11},{10,... | collective-permute-start | bytes 1179656 | tf_op jit(solution)/shard_map/ppermute | solution.py:739
  685.1 35.6 %collective-permute-start.57 = (bf16[4,48,1024]{2,1,0:T(8,128)(2,1)}, bf16[4,48,1024]{2,1,0:T(8,128)(2,1)}, u32[]{:S(2)}, u32[]{:S(2)}) collective-permute-start(bf16[4,48,1024]{2,1,0:T(8,128)(2,1)} %get-tuple-element.452), channel_id=1, source_target_pairs={{0,4},{1,5},{2,6},{3,7},{4,0},{5,1},{6,2},{7,3},{8,12},{9,13},{10,... | collective-permute-start | bytes 1179656 | tf_op jit(solution)/shard_map/ppermute | solution.py:739
  686.5 43.2 %collective-permute-start.58 = (bf16[4,48,1024]{2,1,0:T(8,128)(2,1)}, bf16[4,48,1024]{2,1,0:T(8,128)(2,1)}, u32[]{:S(2)}, u32[]{:S(2)}) collective-permute-start(bf16[4,48,1024]{2,1,0:T(8,128)(2,1)} %get-tuple-element.453), channel_id=1, source_target_pairs={{0,6},{1,7},{2,4},{3,5},{4,2},{5,3},{6,0},{7,1},{8,14},{9,15},{10,... | collective-permute-start | bytes 1179656 | tf_op jit(solution)/shard_map/ppermute | solution.py:739
  689.8 24.1 %collective-permute-start.60 = (bf16[48,1536]{1,0:T(8,128)(2,1)}, bf16[48,1536]{1,0:T(8,128)(2,1)}, u32[]{:S(2)}, u32[]{:S(2)}) collective-permute-start(bf16[48,1536]{1,0:T(8,128)(2,1)} %get-tuple-element.466), channel_id=1, source_target_pairs={{0,16},{8,24},{16,0},{24,8},{1,17},{9,25},{17,1},{25,9},{2,18},{10... | collective-permute-start | bytes 442376 | tf_op jit(solution)/shard_map/ppermute | solution.py:768
  729.7 41.1 %all-to-all-start.10 = ((bf16[4,256,1536]{2,1,0:T(8,128)(2,1)}), bf16[4,256,1536]{2,1,0:T(8,128)(2,1)}, u32[]{:S(2)}, u32[]{:S(2)}) async-start(bf16[4,256,1536]{2,1,0:T(8,128)(2,1)} %copy-done.6), calls=%async_computation.14 | async-start | bytes 6291456 | tf_op jit(solution)/shard_map/all_to_all | solution.py:743
  (125 other events, 1267.3 us)
Sparse Core Ops, SparseCore 0:
  34.2 105.2 all-gather.2
  264.7 86.8 all-gather.4
  379.0 26.6 reduce-scatter.6
  407.9 65.0 reduce-scatter.4
  477.9 64.9 reduce-scatter.8
  666.6 29.5 reduce-scatter.10

commit v3 on v2

--- a/solution.py
+++ b/solution.py
@@ -388,14 +388,14 @@
     stored(steps % 2)
     stored((steps - 1) % 2)
     if last:
-        cut = grad_refs[0].shape[1] - 2 * hidden
-        grad_refs[0][:, : 2 * hidden] = acc_gu[...].astype(BF16)
+        cut = grad_refs[0].shape[1]
+        grad_refs[0][...] = acc_gu[:, :cut].astype(BF16)
+        grad_refs[1][:, : 2 * hidden - cut] = acc_gu[:, cut:].astype(BF16)
         for z in range(shards):
             for j in range(tiles):
                 rows = slice((z * tiles + j) * band, (z * tiles + j + 1) * band)
-                piece = acc_d[z * band : (z + 1) * band, j * hidden : (j + 1) * hidden].astype(BF16)
-                grad_refs[0][rows, 2 * hidden :] = piece[:, :cut]
-                grad_refs[1][rows, :] = piece[:, cut:]
+                piece = acc_d[z * band : (z + 1) * band, j * hidden : (j + 1) * hidden]
+                grad_refs[1][rows, 2 * hidden - cut :] = piece.astype(BF16)
     else:
         out = [
             pltpu.make_async_copy(acc_gu, grad_refs[0], sem_acc.at[0]),
@@ -418,7 +418,7 @@
     token_out = jax.ShapeDtypeStruct((rows, width), BF16)
     token_buffer = pltpu.VMEM((2, block, width), BF16)
     if last:
-        first = 2 * hidden + hidden // 4
+        first = 3 * hidden // 2
         grads = [((width, first), BF16), ((width, 3 * hidden - first), BF16)]
     else:
         grads = [((width, 2 * hidden), F32), ((hidden, width), F32)]
@@ -573,9 +573,9 @@
 
 def input_back_kernel(q_ref, kv_ref, x_ref, mid_ref, gains_ref, w_ref, grad_ref):
     query_width = q_ref.shape[1]
-    cut = query_width + kv_ref.shape[1]
+    cut = w_ref.shape[1] - 128
     grad_h = mm_nt(q_ref[...], w_ref[:, :query_width])
-    grad_h = grad_h + mm_nt(kv_ref[...], w_ref[:, query_width:cut])
+    grad_h = grad_h + mm_nt(kv_ref[:, : cut - query_width], w_ref[:, query_width:cut])
     part, _ = rms_back(x_ref[...].astype(F32), gains_ref[:1], grad_h)
     grad_ref[...] = (mid_ref[...] + part).astype(BF16)
 
@@ -593,9 +593,9 @@
     up_ref, down_ref = refs[-2:]
     for e in range(up_ref.shape[0]):
         first, second = refs[2 * e][...], refs[2 * e + 1][...]
-        cut = up_ref.shape[2]
-        up_ref[e] = first[:, :cut].astype(F32)
-        pieces = jnp.concatenate([first[:, cut:], second], axis=1).astype(F32)
+        cut = up_ref.shape[2] - first.shape[1]
+        up_ref[e] = jnp.concatenate([first, second[:, :cut]], axis=1).astype(F32)
+        pieces = second[:, cut:].astype(F32)
         rows, wide = down_ref.shape[1], pieces.shape[1]
         for j in range(down_ref.shape[2] // wide):
             down_ref[e, :, j * wide : (j + 1) * wide] = pieces[j * rows : (j + 1) * rows]
@@ -678,12 +678,14 @@
     )(order, own, other)
 
 
-def weight_grad_kernel(parts, chunk, n_dp, core_ref, *refs):
+def weight_grad_kernel(parts, chunk, n_dp, has_extra, core_ref, *refs):
     left, right = refs[:parts], refs[parts : 2 * parts]
-    own_ref, other_ref = refs[2 * parts :]
+    own_ref, other_ref = refs[-2:]
     total = mm_tn(left[0][...], right[0][...])
     for a, b in zip(left[1:], right[1:]):
         total = total + mm_tn(a[...], b[...])
+    if has_extra:
+        total = total + refs[2 * parts][...].astype(F32)
     total = total.astype(BF16)
     chips = total.shape[0] // (2 * chunk * n_dp)
     pairs = total.reshape(n_dp, chips, 2, chunk, total.shape[1])
@@ -694,33 +696,38 @@
             other_ref[j, z] = jnp.where(first, pairs[z, j, 1], pairs[z, j, 0])
 
 
-def weight_grad(left, right, n_dp, chips, core):
+def weight_grad(left, right, n_dp, chips, core, extra=None):
     width, columns = left[0].shape[1], right[0].shape[1]
     chunk = width // (2 * n_dp * chips)
     if chunk % 16:
-        total = sum(mm_tn(a, b) for a, b in zip(left, right)).astype(BF16)
+        total = sum(mm_tn(a, b) for a, b in zip(left, right))
+        if extra is not None:
+            total = total + extra.astype(F32)
+        total = total.astype(BF16)
         pairs = total.reshape(n_dp, chips, 2, chunk, columns)
         return [
             jnp.swapaxes(lax.dynamic_index_in_dim(pairs, c, 2, keepdims=False), 0, 1)
             for c in (core, 1 - core)
         ]
     parts, tokens = len(left), left[0].shape[0]
-    block = 512
+    block = 512 if columns % 512 == 0 else 384
     shape = (chips, n_dp, chunk)
+    extras = [] if extra is None else [extra]
     band = jax.ShapeDtypeStruct(shape + (columns,), BF16)
     band_spec = pl.BlockSpec(shape + (block,), lambda j: (0, 0, 0, j))
     return pl.pallas_call(
-        functools.partial(weight_grad_kernel, parts, chunk, n_dp),
+        functools.partial(weight_grad_kernel, parts, chunk, n_dp, bool(extras)),
         grid=(columns // block,),
         in_specs=[SCALARS]
         + [pl.BlockSpec((tokens, width), lambda j: (0, 0))] * parts
-        + [pl.BlockSpec((tokens, block), lambda j: (0, j))] * parts,
+        + [pl.BlockSpec((tokens, block), lambda j: (0, j))] * parts
+        + [pl.BlockSpec((width, block), lambda j: (0, j))] * len(extras),
         out_specs=[band_spec, band_spec],
         out_shape=[band, band],
         compiler_params=pltpu.CompilerParams(vmem_limit_bytes=32 * 1024 * 1024),
         cost_estimate=SMALL,
         name="weight_grad",
-    )(core.reshape(1).astype(jnp.int32), *left, *right)
+    )(core.reshape(1).astype(jnp.int32), *left, *right, *extras)
 
 
 def join(*items):
@@ -962,8 +969,8 @@
     y_sib_0, y_own_0, gh_sib_0, gh_own_0 = carried[0]
     gh_chips = sums(split(gh_own_0), split(plane.swap(gh_sib_0)), order)
     gate, gh_chips, y_sib_0 = join(gates[1][1], gh_chips, y_sib_0)
-    (carried[1], totals[1]), gh_got, y_swap_0, totals_s[0] = join(
-        run(1, 1, gate), plane.exchange(gh_chips), plane.swap(y_sib_0), totals_s[0]
+    (carried[1], totals[1]), gh_got, y_swap_0 = join(
+        run(1, 1, gate), plane.exchange(gh_chips), plane.swap(y_sib_0)
     )
     y_sib_1, y_own_1, gh_sib_1, gh_own_1 = carried[1]
 
@@ -977,8 +984,8 @@
     def returned(dkv, ds):
         return [dp_along(dkv[n_dp - 1 - d], -d, n_dp) for d in ds]
 
-    def weights_of(left, right):
-        return weight_grad(left, right, n_dp, plane.chips, core)
+    def weights_of(left, right, extra=None):
+        return weight_grad(left, right, n_dp, plane.chips, core, extra)
 
     back_0, gh_swap, y_sib_1 = join(back_of(0, gh_got), plane.swap(gh_sib_1), y_sib_1)
     gh_chips = sums(split(gh_own_1), split(gh_swap), order)
@@ -987,84 +994,88 @@
     totals_s.append([summed(totals[1][0])])
     grad_q_0, dkv_0 = attention_back(0, grad_mixed)
     y_swap_0, grad_q_0 = join(y_swap_0, grad_q_0)
-    grad_q_0, dkv_0, gh_got, y_chips_0, y_swap_1 = join(
+    grad_q_0, dkv_0, gh_got, y_chips_0, y_swap_1, totals_s[0], totals_s[1][0] = join(
         grad_q_0,
         dkv_0,
         gh_got,
         sums(split(y_own_0), split(y_swap_0), order),
         plane.swap(y_sib_1),
+        totals_s[0],
+        totals_s[1][0],
     )
     back_1 = back_of(1, gh_got)
     grad_x_mid, grad_branch, gain_parts, _ = zip(back_0, back_1)
-    gain_mid = sum(g[:1] for g in gain_parts)
-    soon, late = [lags[0], *between], [lags[-1]]
-    out_bands = weights_of(grad_branch, attn)
-    (grad_q_1, dkv_1), held, totals_s[1][0], y_got_0, y_swap_1, gain_swap, out_swap = join(
-        attention_back(1, back_1[3]),
-        returned(dkv_0, soon),
-        totals_s[1][0],
+    gain_mid = sum(g[0] for g in gain_parts)
+    gain_high = gain_mid.astype(BF16)
+    gain_mid = jnp.stack([gain_high, (gain_mid - gain_high.astype(F32)).astype(BF16)], axis=1)
+    gain_mid = jnp.pad(gain_mid, ((0, 0), (2 * kv_width, 126)))
+    soon, late = lags[:1], lags[-1:]
+    grad_mixed, out_bands, held = join(
+        back_1[3], weights_of(grad_branch, attn), returned(dkv_0, soon)
+    )
+    held_0 = dict(zip(soon, held))
+    (grad_q_1, dkv_1), held, y_got_0, y_swap_1, gain_mid, out_swap = join(
+        attention_back(1, grad_mixed),
+        returned(dkv_0, between),
         plane.exchange(y_chips_0),
         y_swap_1,
-        plane.swap(gain_mid),
+        gain_mid,
         plane.swap(out_bands[1]),
     )
-    gain_mid = gain_mid + gain_swap
-    out_got = plane.exchange(sums(out_bands[0], out_swap, same))
-    held_0 = dict(zip(soon, held))
+    held_0.update(zip(between, held))
     grad_q = [grad_q_0, grad_q_1]
 
-    held, q_bands, last_half, y_chips_1, gain_near = join(
+    held, q_bands, y_chips_1, gain_mid, out_chips = join(
         returned(dkv_1, ends),
         weights_of(h_in, grad_q),
-        totals[1][1],
         sums(split(y_own_1), split(y_swap_1), order),
-        plane.crosses(gain_mid, near),
+        gain_mid,
+        sums(out_bands[0], out_swap, same),
     )
     held_1 = dict(zip(ends, held))
-    held, held_late, q_swap, gain_far = join(
+    out_got = plane.exchange(out_chips)
+    held, held_late, q_chips, out_got, last_half = join(
         returned(dkv_1, between),
         returned(dkv_0, late),
-        plane.swap(q_bands[1]),
-        plane.crosses(gain_mid, far),
-    )
-    gain_mid = added(gain_mid, gain_near + gain_far)
+        sums(q_bands[0], plane.swap(q_bands[1]), same),
+        out_got,
+        totals[1][1],
+    )
     held_1.update(zip(between, held))
     held_0.update(zip(late, held_late))
     totals_s[1].append(summed(last_half))
     total_0 = added(dkv_0[-1].astype(F32), [held_0[d] for d in lags])
     total_1 = added(dkv_1[-1].astype(F32), [held_1[d] for d in lags])
-    grad_kv = [jnp.concatenate([t[0], t[1]], axis=1).astype(BF16) for t in (total_0, total_1)]
-    kv_bands = weights_of(h_in, grad_kv)
-    gain_rows = lax.dynamic_index_in_dim(
-        gain_mid.reshape(n_dp, n_expert, -1), expert_index, 1, keepdims=False
-    )
-    gain_rows = jnp.pad(gain_rows[:, :, None], ((0, 0), (0, 0), (0, 127)))
-    kv_swap, q_chips, gain_rows, out_got = join(
-        plane.swap(kv_bands[1]), sums(q_bands[0], q_swap, same), gain_rows, out_got
-    )
+    blank = jnp.zeros((rows, 128), F32)
+    grad_kv = [
+        jnp.concatenate([t[0], t[1], blank], axis=1).astype(BF16) for t in (total_0, total_1)
+    ]
+    kv_bands = weights_of(h_in, grad_kv, gain_mid)
+    q_got = plane.exchange(q_chips)
+    kv_swap, out_got = join(plane.swap(kv_bands[1]), out_got)
     kv_chips = sums(kv_bands[0], kv_swap, order)
-    kv_own, grad_kv, q_chips = join([kv_chips[k] for k in range(plane.chips)], grad_kv, q_chips)
+    kv_own = [kv_chips[k] for k in range(plane.chips)]
+    out_total, out_pieces = band_totals([[out_got]], dp_index)
+
+    def over_dp_links(pieces):
+        return [dp_cross(x, z, n_dp) for z, x in zip(lags, pieces)]
+
+    kv_sent, q_got, grad_kv, totals_s, y_chips_1, out_sent = join(
+        [plane.cross(kv_own[k], k) for k in every],
+        q_got,
+        grad_kv,
+        totals_s,
+        y_chips_1,
+        over_dp_links(out_pieces),
+    )
     grad_x = [
         input_back(grad_q[m], grad_kv[m], x_in[m], grad_x_mid[m], gains, weight) for m in micros
     ]
-    out_total, out_pieces = band_totals([[out_got]], dp_index)
-
-    def over_dp_links(pieces):
-        return [dp_cross(x, z, n_dp) for z, x in zip(lags, pieces)]
-
-    kv_sent, q_got, grad_x, totals_s, y_chips_1, out_sent = join(
-        [plane.cross(kv_own[k], k) for k in every],
-        plane.exchange(q_chips),
-        grad_x,
-        totals_s,
-        y_chips_1,
-        over_dp_links(out_pieces),
-    )
     y_got_1 = plane.exchange(y_chips_1)
     grad_gu_s, grad_down_s = unpack(totals_s, w_gate_up.shape, w_down.shape)
-    total, pieces = band_totals([[q_got], [kv_own[0], *kv_sent], [gain_rows]], dp_index)
-    sent, y_got_1, grad_gu_s, grad_down_s = join(
-        over_dp_links(pieces), y_got_1, grad_gu_s, grad_down_s
+    total, pieces = band_totals([[q_got], [kv_own[0], *kv_sent]], dp_index)
+    sent, y_got_1, grad_gu_s, grad_down_s, grad_x = join(
+        over_dp_links(pieces), y_got_1, grad_gu_s, grad_down_s, grad_x
     )
     out_total, total = added(out_total, out_sent), added(total, sent)
 
@@ -1077,7 +1088,7 @@
     return (
         jnp.stack([x.astype(BF16) for x in x_out])[:, None],
         jnp.stack(grad_x)[:, None],
-        jnp.stack([gain_in, total[:, qkv_width]]),
+        jnp.stack([gain_in, total[:, qkv_width] + total[:, qkv_width + 1]]),
         grad_wqkv,
         out_total.T,
         grad_gu_s,

time: 794 us -> 785 us (0.989)
  starting transfers between devices: 148 us -> 139 us
  local copies, waits for them, and re-layouts: 73.3 us -> 64.6 us
    unnamed x186 -> x200, local copies, waits for them, and re-layouts: 53 us -> 44.7 us
    ppermute x18 -> x15, starting transfers between devices: 24 us -> 17.5 us  [cross(): lax.ppermute(x, 'expert', [(i, i ^ 2 * k) for i in range(self.count)])]
    ppermute x18 -> x15, waiting for transfers between devices: 29 us -> 22.7 us  [cross(): lax.ppermute(x, 'expert', [(i, i ^ 2 * k) for i in range(self.count)])]
  transfers between devices with their start and end apart: 82 -> 78, of which waited for: 26 -> 27; matrix products, arithmetic and copies ran while one was open for 7% -> 7% of each run, Pallas kernels for 43% -> 44%
where the time goes in v3:
time: 785 us; the launch traced here: 777 us
  Pallas kernels  342 us (44%)
  waiting for transfers between devices  175 us (22%)
  starting transfers between devices  139 us (18%)
  local copies, waits for them, and re-layouts  64.6 us (8%)
  other arithmetic  30.6 us (4%)
  between operations  15.9 us (2%)
  matrix products  9.49 us (1%)
    pallas_call x4, Pallas kernels, expert_pass(): pl.pallas_call(functools.partial(expert_kernel, block, chips, shards, pre...  162 us
    ppermute x12, waiting for transfers between devices, dp_along(): return lax.ppermute(x, 'dp', pairs)  77.3 us
    ppermute x12, starting transfers between devices, dp_along(): return lax.ppermute(x, 'dp', pairs)  53.7 us
    pallas_call x2, Pallas kernels, attend_back(): pl.pallas_call(functools.partial(attend_back_kernel, chunks), grid=(PAIRS...  50.9 us
    unnamed x200, local copies, waits for them, and re-layouts  44.7 us
    pallas_call x10, Pallas kernels, small_call(): pl.pallas_call(kernel, in_specs=in_specs or [NEAR] * len(inputs), out_spe...  43.9 us
    all_to_all x9, starting transfers between devices, exchange(): lax.all_to_all(x, 'expert', split_axis=0, concat_axis=0, axis_index_group...  41.5 us
    pallas_call x2, Pallas kernels, attend(): pl.pallas_call(functools.partial(attend_kernel, chunks), grid=(PAIRS,), i...  33.4 us
  transfers between devices with their start and end apart: 78, of which 27 were waited for; matrix products, arithmetic and copies ran while one was open for 7% of the time, Pallas kernels for 44%

profile of v3, /device:TPU:0, one launch (start us, length us, event | category | flops | bytes accessed | tf_op | source)
XLA Modules:
  0.0 777.1 jit_solution(8148700808274332545)
XLA Ops:
  41.2 6.9 all-to-all-start.1
  60.4 18.8 %all-to-all-done.1 = bf16[4,48,1536]{2,1,0:T(8,128)(2,1)} async-done(((bf16[4,48,1536]{2,1,0:T(8,128)(2,1)}), bf16[4,48,1536]{2,1,0:T(8,128)(2,1)}, u32[]{:S(2)}, u32[]{:S(2)}) %all-to-all-start.1) | async-done | bytes 589856 | tf_op jit(solution)/shard_map/all_to_all | solution.py:866
  87.3 4.5 all-to-all-start.2
  98.9 9.2 %assemble.2.refs_2_.w_ref = bf16[1536,2688]{1,0:T(8,128)(2,1)S(1)} custom-call(s32[32]{0:T(128)S(1)} %stack.277.place_ref, bf16[4,48,2688]{2,1,0:T(8,128)(2,1)S(1)} %pad_maximum_fusion.2.refs_0_, bf16[4,48,2688]{2,1,0:T(8,128)(2,1)S(1)} %copy-done.59, bf16[2,48,2688]{2,1,0:T(8,128)(2,1)S(1)} %collective-permute-done.3.refs_2_, ...), custom_call_target="tpu_custom_call" | custom-call | flops 1024 | bytes 1024 | tf_op jit(solution)/shard_map/assemble/pallas_call | solution.py:501
  111.3 5.6 project.1
  118.9 4.6 all-to-all-start.3
  123.7 4.5 collective-permute-start.16
  134.2 4.9 fusion.4.q_ref
  139.1 4.6 fusion.7.q_ref
  148.9 6.1 collective-permute-done.17.refs_1_.refs_5_
  155.7 10.2 %collective-permute-done.18.refs_2_.refs_6_ = bf16[256,1024]{1,0:T(8,128)(2,1)} collective-permute-done((bf16[256,1024]{1,0:T(8,128)(2,1)S(1)}, bf16[256,1024]{1,0:T(8,128)(2,1)}, u32[]{:S(2)}, u32[]{:S(2)}) %collective-permute-start.18) | collective-permute-done | bytes 524320 | tf_op jit(solution)/shard_map/ppermute | solution.py:780
  166.0 4.7 all-to-all-start.4
  170.7 31.6 %collective-permute-start.20 = (bf16[256,1024]{1,0:T(8,128)(2,1)S(1)}, bf16[256,1024]{1,0:T(8,128)(2,1)S(1)}, u32[]{:S(2)}, u32[]{:S(2)}) collective-permute-start(bf16[256,1024]{1,0:T(8,128)(2,1)S(1)} %get-tuple-element.290.refs_3_.refs_7_), channel_id=1, source_target_pairs={{0,16},{8,24},{1,17},{9,25},{2,18},{10,26},{3,19},{11,27},{4,20},{... | collective-permute-start | bytes 1572872 | tf_op jit(solution)/shard_map/ppermute | solution.py:780
  202.3 16.7 %path_attention.2 = (bf16[256,1536]{1,0:T(8,128)(2,1)}, f32[4,8,256]{2,1,0:T(8,128)}) custom-call(bf16[256,1536]{1,0:T(8,128)(2,1)} %fusion.4.q_ref, bf16[256,1024]{1,0:T(8,128)(2,1)} %copy-done.78, bf16[256,1024]{1,0:T(8,128)(2,1)} %copy-done.79, bf16[256,1024]{1,0:T(8,128)(2,1)} %collective-permute-done.18.refs_2_.refs_6_, bf16[256,1024]{1,0:T(8,128)(2,1)} %copy-done.14, ...), custom_call_target="tpu_custom_call" | custom-call | flops 25165824 | bytes 1048576 | tf_op jit(solution)/shard_map/path_attention/pallas_call | solution.py:106
  232.5 10.1 %collective-permute-done.22.refs_2_.refs_6_ = bf16[256,1024]{1,0:T(8,128)(2,1)S(1)} collective-permute-done((bf16[256,1024]{1,0:T(8,128)(2,1)S(1)}, bf16[256,1024]{1,0:T(8,128)(2,1)S(1)}, u32[]{:S(2)}, u32[]{:S(2)}) %collective-permute-start.22) | collective-permute-done | bytes 524320 | tf_op jit(solution)/shard_map/ppermute | solution.py:780
  242.6 10.0 %collective-permute-done.23.refs_0_.refs_4_ = bf16[256,1024]{1,0:T(8,128)(2,1)} collective-permute-done((bf16[256,1024]{1,0:T(8,128)(2,1)S(1)}, bf16[256,1024]{1,0:T(8,128)(2,1)}, u32[]{:S(2)}, u32[]{:S(2)}) %collective-permute-start.23) | collective-permute-done | bytes 524320 | tf_op jit(solution)/shard_map/ppermute | solution.py:780
  252.6 10.9 %collective-permute-done.25.refs_6_ = bf16[256,1536]{1,0:T(8,128)(2,1)} collective-permute-done((bf16[256,1536]{1,0:T(8,128)(2,1)S(1)}, bf16[256,1536]{1,0:T(8,128)(2,1)}, u32[]{:S(2)}, u32[]{:S(2)}) %collective-permute-start.25) | collective-permute-done | bytes 786464 | tf_op jit(solution)/shard_map/ppermute | solution.py:746
  264.7 16.7 %path_attention.3 = (bf16[256,1536]{1,0:T(8,128)(2,1)}, f32[4,8,256]{2,1,0:T(8,128)}) custom-call(bf16[256,1536]{1,0:T(8,128)(2,1)} %fusion.7.q_ref, bf16[256,1024]{1,0:T(8,128)(2,1)} %collective-permute-done.23.refs_0_.refs_4_, bf16[256,1024]{1,0:T(8,128)(2,1)} %copy-done.76, bf16[256,1024]{1,0:T(8,128)(2,1)} %copy-done.77, bf16[256,1024]{1,0:T(8,128)(2,1)} %copy-done.13, ...), custom_call_target="tpu_custom_call" | custom-call | flops 25165824 | bytes 1048576 | tf_op jit(solution)/shard_map/path_attention/pallas_call | solution.py:106
  292.1 39.2 %expert_pass.4 = (bf16[1024,1536]{1,0:T(8,128)(2,1)}, bf16[1024,1536]{1,0:T(8,128)(2,1)}, bf16[1024,1536]{1,0:T(8,128)(2,1)}, bf16[1024,1536]{1,0:T(8,128)(2,1)}...) custom-call(bf16[256,1536]{1,0:T(8,128)(2,1)} %copy-done.82, bf16[256,1536]{1,0:T(8,128)(2,1)} %collective-permute-done.28.refs_1_, ...), custom_call_target="tpu_custom_call" | custom-call | flops 1572864 | bytes 1572864 | tf_op jit(solution)/shard_map/expert_pass/pallas_call | solution.py:443
  337.1 41.0 %expert_pass.5 = (bf16[1024,1536]{1,0:T(8,128)(2,1)}, bf16[1024,1536]{1,0:T(8,128)(2,1)}, bf16[1024,1536]{1,0:T(8,128)(2,1)}, bf16[1024,1536]{1,0:T(8,128)(2,1)}...) custom-call(bf16[256,1536]{1,0:T(8,128)(2,1)} %collective-permute-done.35.refs_0_, bf16[256,1536]{1,0:T(8,128)(2,1)} %copy-done.83, ...), custom_call_target="tpu_custom_call" | custom-call | flops 1572864 | bytes 1572864 | tf_op jit(solution)/shard_map/expert_pass/pallas_call | solution.py:443
  378.2 40.8 %expert_pass.6 = (bf16[1024,1536]{1,0:T(8,128)(2,1)}, bf16[1024,1536]{1,0:T(8,128)(2,1)}, bf16[1024,1536]{1,0:T(8,128)(2,1)}, bf16[1024,1536]{1,0:T(8,128)(2,1)}...) custom-call(bf16[256,1536]{1,0:T(8,128)(2,1)} %copy-done.82, ...), custom_call_target="tpu_custom_call", output_to_operand_aliasing={{0}: (13, {}), {1}: (14, {}), {2}: (15, {}), {3}: (16, {})} | custom-call | flops 1572864 | bytes 1572864 | tf_op jit(solution)/shard_map/expert_pass/pallas_call | solution.py:443
  419.3 5.6 collective-permute-done.39
  430.2 4.7 all-to-all-start.5
  434.9 41.1 %expert_pass.7 = (bf16[1024,1536]{1,0:T(8,128)(2,1)}, bf16[1024,1536]{1,0:T(8,128)(2,1)}, bf16[1024,1536]{1,0:T(8,128)(2,1)}, bf16[1024,1536]{1,0:T(8,128)(2,1)}...) custom-call(bf16[256,1536]{1,0:T(8,128)(2,1)} %collective-permute-do, ...), custom_call_target="tpu_custom_call", output_to_operand_aliasing={{0}: (13, {}), {1}: (14, {}), {2}: (15, {}), {3}: (16, {})} | custom-call | flops 1572864 | bytes 1572864 | tf_op jit(solution)/shard_map/expert_pass/pallas_call | solution.py:443
  477.7 5.7 middle_back.2
  486.6 5.0 sums.8
  491.6 4.9 all-to-all-start.6
  496.5 25.3 %path_attention_back.2 = (bf16[256,1536]{1,0:T(8,128)(2,1)}, bf16[2,256,512]{2,1,0:T(8,128)(2,1)}, bf16[2,256,512]{2,1,0:T(8,128)(2,1)}, bf16[2,256,512]{2,1,0:T(8,128)(2,1)}, bf16[2,256,512]{2,1,0:T(8,128)(2,1)}) custom-call(bf16[256,1536]{1,0:T(8,128)(2,1)} %fusion.4.q_ref, bf16[256,1536]{1,0:T(8,128)(2,1)} %copy-done.63, bf16[256,1024]{1,0:T(8,128)(2,1)} %copy-done.78, ...), custom_call_target="tpu_custom_call" | custom-call | flops 62914560 | bytes 1048576 | tf_op jit(solution)/shard_map/path_attention_back/pallas_call | solution.py:179
  527.0 6.6 all-to-all-done.6.got_ref
  535.0 4.7 all-to-all-start.7
  539.8 5.7 middle_back.3
  545.6 4.3 weight_grad.3
  555.0 25.6 %path_attention_back.3 = (bf16[256,1536]{1,0:T(8,128)(2,1)}, bf16[2,256,512]{2,1,0:T(8,128)(2,1)}, bf16[2,256,512]{2,1,0:T(8,128)(2,1)}, bf16[2,256,512]{2,1,0:T(8,128)(2,1)}, bf16[2,256,512]{2,1,0:T(8,128)(2,1)}) custom-call(bf16[256,1536]{1,0:T(8,128)(2,1)} %fusion.7.q_ref, bf16[256,1536]{1,0:T(8,128)(2,1)} %copy-done.62, ...), custom_call_target="tpu_custom_call" | custom-call | flops 62914560 | bytes 1048576 | tf_op jit(solution)/shard_map/path_attention_back/pallas_call | solution.py:179
  588.0 4.2 weight_grad.4
  593.7 5.3 sums.10
  603.5 8.9 %collective-permute-done.49 = bf16[2,256,512]{2,1,0:T(8,128)(2,1)} collective-permute-done((bf16[2,256,512]{2,1,0:T(8,128)(2,1)}, bf16[2,256,512]{2,1,0:T(8,128)(2,1)}, u32[]{:S(2)}, u32[]{:S(2)}) %collective-permute-start.49) | collective-permute-done | bytes 524320 | tf_op jit(solution)/shard_map/ppermute | solution.py:780
  612.4 4.5 all-to-all-start.8
  625.9 9.9 %collective-permute-done.47 = bf16[2,256,512]{2,1,0:T(8,128)(2,1)} collective-permute-done((bf16[2,256,512]{2,1,0:T(8,128)(2,1)}, bf16[2,256,512]{2,1,0:T(8,128)(2,1)}, u32[]{:S(2)}, u32[]{:S(2)}) %collective-permute-start.47) | collective-permute-done | bytes 524320 | tf_op jit(solution)/shard_map/ppermute | solution.py:780
  635.8 22.0 %collective-permute-done.46 = bf16[2,256,512]{2,1,0:T(8,128)(2,1)} collective-permute-done((bf16[2,256,512]{2,1,0:T(8,128)(2,1)}, bf16[2,256,512]{2,1,0:T(8,128)(2,1)}, u32[]{:S(2)}, u32[]{:S(2)}) %collective-permute-start.46) | collective-permute-done | bytes 524320 | tf_op jit(solution)/shard_map/ppermute | solution.py:780
  661.7 4.6 weight_grad.5
  683.9 16.4 %collective-permute-done.55 = bf16[48,1536]{1,0:T(8,128)(2,1)S(1)} collective-permute-done((bf16[48,1536]{1,0:T(8,128)(2,1)S(1)}, bf16[48,1536]{1,0:T(8,128)(2,1)S(1)}, u32[]{:S(2)}, u32[]{:S(2)}) %collective-permute-start.55) | collective-permute-done | bytes 147488 | tf_op jit(solution)/shard_map/ppermute | solution.py:775
  701.5 10.4 %collective-permute-done.57 = bf16[48,1536]{1,0:T(8,128)(2,1)} collective-permute-done((bf16[48,1536]{1,0:T(8,128)(2,1)S(1)}, bf16[48,1536]{1,0:T(8,128)(2,1)}, u32[]{:S(2)}, u32[]{:S(2)}) %collective-permute-start.57) | collective-permute-done | bytes 147488 | tf_op jit(solution)/shard_map/ppermute | solution.py:775
  711.9 8.2 %collective-permute-done.54.refs_4_ = bf16[4,48,1152]{2,1,0:T(8,128)(2,1)} collective-permute-done((bf16[4,48,1152]{2,1,0:T(8,128)(2,1)}, bf16[4,48,1152]{2,1,0:T(8,128)(2,1)}, u32[]{:S(2)}, u32[]{:S(2)}) %collective-permute-start.54) | collective-permute-done | bytes 442400 | tf_op jit(solution)/shard_map/ppermute | solution.py:746
  720.1 4.8 all-to-all-start.10
  731.2 4.3 collective-permute-start.60
  735.6 5.9 input_back.2
  741.5 6.0 input_back.3
  752.3 8.5 %all-to-all-done.10 = bf16[4,256,1536]{2,1,0:T(8,128)(2,1)} async-done(((bf16[4,256,1536]{2,1,0:T(8,128)(2,1)}), bf16[4,256,1536]{2,1,0:T(8,128)(2,1)}, u32[]{:S(2)}, u32[]{:S(2)}) %all-to-all-start.10) | async-done | bytes 3145760 | tf_op jit(solution)/shard_map/all_to_all | solution.py:750
  (417 shorter events, 196.5 us)
Async XLA Ops:
  8.9 21.8 %collective-permute-start = (bf16[48,2688]{1,0:T(8,128)(2,1)S(1)}, bf16[48,2688]{1,0:T(8,128)(2,1)S(1)}, u32[]{:S(2)}, u32[]{:S(2)}) collective-permute-start(bf16[48,2688]{1,0:T(8,128)(2,1)S(1)} %fusion.20), channel_id=1, source_target_pairs={{0,8},{8,0},{16,24},{24,16},{1,9},{9,1},{17,25},{25,17},{2,10},{10... | collective-permute-start | bytes 774152 | tf_op jit(solution)/shard_map/ppermute | solution.py:775
  12.0 21.2 %collective-permute-start.1 = (bf16[48,2688]{1,0:T(8,128)(2,1)S(1)}, bf16[48,2688]{1,0:T(8,128)(2,1)}, u32[]{:S(2)}, u32[]{:S(2)}) collective-permute-start(bf16[48,2688]{1,0:T(8,128)(2,1)S(1)} %fusion.20), channel_id=1, source_target_pairs={{0,16},{8,24},{16,0},{24,8},{1,17},{9,25},{17,1},{25,9},{2,18},{10... | collective-permute-start | bytes 774152 | tf_op jit(solution)/shard_map/ppermute | solution.py:775
  19.9 146.1 %all-gather.3.cloned.1.call-start = ((), (), s32[]{:S(2)}) async-start(), calls=%async_computation.15 | async-start | bytes 5898240 | tf_op jit(solution)/shard_map/all_gather | solution.py:822
  41.2 38.0 %all-to-all-start.1 = ((bf16[4,48,1536]{2,1,0:T(8,128)(2,1)}), bf16[4,48,1536]{2,1,0:T(8,128)(2,1)}, u32[]{:S(2)}, u32[]{:S(2)}) async-start(bf16[4,48,1536]{2,1,0:T(8,128)(2,1)} %broadcast_in_dim.84), calls=%async_computation.1 | async-start | bytes 1179648 | tf_op jit(solution)/shard_map/all_to_all | solution.py:866
  54.8 24.3 %collective-permute-start.6 = (bf16[2,48,2688]{2,1,0:T(8,128)(2,1)}, bf16[2,48,2688]{2,1,0:T(8,128)(2,1)}, u32[]{:S(2)}, u32[]{:S(2)}) collective-permute-start(bf16[2,48,2688]{2,1,0:T(8,128)(2,1)} %pad_maximum_fusion.3), channel_id=1, source_target_pairs={{0,4},{1,5},{2,6},{3,7},{4,0},{5,1},{6,2},{7,3},{8,12},{9,13},{10,... | collective-permute-start | bytes 1548296 | tf_op jit(solution)/shard_map/ppermute | solution.py:746
  56.3 22.9 %collective-permute-start.7 = (bf16[2,48,2688]{2,1,0:T(8,128)(2,1)S(1)}, bf16[2,48,2688]{2,1,0:T(8,128)(2,1)}, u32[]{:S(2)}, u32[]{:S(2)}) collective-permute-start(bf16[2,48,2688]{2,1,0:T(8,128)(2,1)S(1)} %collective-permute-done.3.refs_2_), channel_id=1, source_target_pairs={{0,4},{1,5},{2,6},{3,7},{4,0},{5,1},{6,2},{7,3},{8,12},{9,13},{10,... | collective-permute-start | bytes 1548296 | tf_op jit(solution)/shard_map/ppermute | solution.py:746
  56.9 22.4 %collective-permute-start.8 = (bf16[2,48,2688]{2,1,0:T(8,128)(2,1)}, bf16[2,48,2688]{2,1,0:T(8,128)(2,1)}, u32[]{:S(2)}, u32[]{:S(2)}) collective-permute-start(bf16[2,48,2688]{2,1,0:T(8,128)(2,1)} %pad_maximum_fusion.4), channel_id=1, source_target_pairs={{0,2},{1,3},{2,0},{3,1},{4,6},{5,7},{6,4},{7,5},{8,10},{9,11},{10,... | collective-permute-start | bytes 1548296 | tf_op jit(solution)/shard_map/ppermute | solution.py:746
  57.4 23.3 %collective-permute-start.9 = (bf16[2,48,2688]{2,1,0:T(8,128)(2,1)}, bf16[2,48,2688]{2,1,0:T(8,128)(2,1)}, u32[]{:S(2)}, u32[]{:S(2)}) collective-permute-start(bf16[2,48,2688]{2,1,0:T(8,128)(2,1)} %collective-permute-done.4.refs_5_), channel_id=1, source_target_pairs={{0,2},{1,3},{2,0},{3,1},{4,6},{5,7},{6,4},{7,5},{8,10},{9,11},{10,... | collective-permute-start | bytes 1548296 | tf_op jit(solution)/shard_map/ppermute | solution.py:746
  87.3 31.4 %all-to-all-start.2 = ((bf16[4,4,48,1536]{3,2,1,0:T(8,128)(2,1)}), bf16[4,4,48,1536]{3,2,1,0:T(8,128)(2,1)}, u32[]{:S(2)}, u32[]{:S(2)}) async-start(bf16[4,4,48,1536]{3,2,1,0:T(8,128)(2,1)} %broadcast_in_dim.98), calls=%async_computation.2 | async-start | bytes 4718592 | tf_op jit(solution)/shard_map/all_to_all | solution.py:750
  118.7 25.0 %collective-permute-start.19 = (bf16[4,4,48,1536]{3,2,1,0:T(8,128)(2,1)}, bf16[4,4,48,1536]{3,2,1,0:T(8,128)(2,1)}, u32[]{:S(2)}, u32[]{:S(2)}) collective-permute-start(bf16[4,4,48,1536]{3,2,1,0:T(8,128)(2,1)} %all-to-all-done.2), channel_id=1, source_target_pairs={{0,1},{1,0},{2,3},{3,2},{4,5},{5,4},{6,7},{7,6},{8,9},{9,8},{10,11... | collective-permute-start | bytes 7077896 | tf_op jit(solution)/shard_map/ppermute | solution.py:743
  118.9 47.1 %all-to-all-start.3 = ((bf16[4,256,1536]{2,1,0:T(8,128)(2,1)}), bf16[4,256,1536]{2,1,0:T(8,128)(2,1)}, u32[]{:S(2)}, u32[]{:S(2)}) async-start(bf16[4,256,1536]{2,1,0:T(8,128)(2,1)} %broadcast_in_dim.95), calls=%async_computation.3 | async-start | bytes 6291456 | tf_op jit(solution)/shard_map/all_to_all | solution.py:750
  123.7 25.2 %collective-permute-start.16 = (bf16[256,1024]{1,0:T(8,128)(2,1)S(1)}, bf16[256,1024]{1,0:T(8,128)(2,1)S(1)}, u32[]{:S(2)}, u32[]{:S(2)}) collective-permute-start(bf16[256,1024]{1,0:T(8,128)(2,1)S(1)} %get-tuple-element.276.refs_3_.refs_7_), channel_id=1, source_target_pairs={{0,24},{1,25},{2,26},{3,27},{4,28},{5,29},{6,30},{7,31}} | collective-permute-start | bytes 1572872 | tf_op jit(solution)/shard_map/ppermute | solution.py:780
  128.2 26.7 %collective-permute-start.17 = (bf16[256,1024]{1,0:T(8,128)(2,1)S(1)}, bf16[256,1024]{1,0:T(8,128)(2,1)S(1)}, u32[]{:S(2)}, u32[]{:S(2)}) collective-permute-start(bf16[256,1024]{1,0:T(8,128)(2,1)S(1)} %get-tuple-element.276.refs_3_.refs_7_), channel_id=1, source_target_pairs={{0,16},{8,24},{1,17},{9,25},{2,18},{10,26},{3,19},{11,27},{4,20},{... | collective-permute-start | bytes 1572872 | tf_op jit(solution)/shard_map/ppermute | solution.py:780
  132.1 33.9 %collective-permute-start.18 = (bf16[256,1024]{1,0:T(8,128)(2,1)S(1)}, bf16[256,1024]{1,0:T(8,128)(2,1)}, u32[]{:S(2)}, u32[]{:S(2)}) collective-permute-start(bf16[256,1024]{1,0:T(8,128)(2,1)S(1)} %get-tuple-element.276.refs_3_.refs_7_), channel_id=1, source_target_pairs={{0,8},{8,16},{16,24},{1,9},{9,17},{17,25},{2,10},{10,18},{18,26},{... | collective-permute-start | bytes 1572872 | tf_op jit(solution)/shard_map/ppermute | solution.py:780
  166.0 53.1 %collective-permute-start.21 = (bf16[4,256,1536]{2,1,0:T(8,128)(2,1)}, bf16[4,256,1536]{2,1,0:T(8,128)(2,1)}, u32[]{:S(2)}, u32[]{:S(2)}) collective-permute-start(bf16[4,256,1536]{2,1,0:T(8,128)(2,1)} %all-to-all-done.3.refs_9_), channel_id=1, source_target_pairs={{0,1},{1,0},{2,3},{3,2},{4,5},{5,4},{6,7},{7,6},{8,9},{9,8},{10,11... | collective-permute-start | bytes 9437192 | tf_op jit(solution)/shard_map/ppermute | solution.py:743
  166.0 66.5 %all-to-all-start.4 = ((bf16[4,256,1536]{2,1,0:T(8,128)(2,1)}), bf16[4,256,1536]{2,1,0:T(8,128)(2,1)}, u32[]{:S(2)}, u32[]{:S(2)}) async-start(bf16[4,256,1536]{2,1,0:T(8,128)(2,1)} %broadcast_in_dim.97), calls=%async_computation.4 | async-start | bytes 6291456 | tf_op jit(solution)/shard_map/all_to_all | solution.py:750
  170.7 207.4 %all-gather.5.cloned.1.call-start = ((), (), s32[]{:S(2)}) async-start(), calls=%async_computation.16 | async-start | bytes 5898240 | tf_op jit(solution)/shard_map/all_gather | solution.py:822
  170.7 48.3 %collective-permute-start.20 = (bf16[256,1024]{1,0:T(8,128)(2,1)S(1)}, bf16[256,1024]{1,0:T(8,128)(2,1)S(1)}, u32[]{:S(2)}, u32[]{:S(2)}) collective-permute-start(bf16[256,1024]{1,0:T(8,128)(2,1)S(1)} %get-tuple-element.290.refs_3_.refs_7_), channel_id=1, source_target_pairs={{0,16},{8,24},{1,17},{9,25},{2,18},{10,26},{3,19},{11,27},{4,20},{... | collective-permute-start | bytes 1572872 | tf_op jit(solution)/shard_map/ppermute | solution.py:780
  225.5 27.1 %collective-permute-start.24 = (bf16[256,1536]{1,0:T(8,128)(2,1)S(1)}, bf16[256,1536]{1,0:T(8,128)(2,1)}, u32[]{:S(2)}, u32[]{:S(2)}) collective-permute-start(bf16[256,1536]{1,0:T(8,128)(2,1)S(1)} %get-tuple-element.297.refs_4_), channel_id=1, source_target_pairs={{0,2},{1,3},{2,0},{3,1},{4,6},{5,7},{6,4},{7,5},{8,10},{9,11},{10,... | collective-permute-start | bytes 2359304 | tf_op jit(solution)/shard_map/ppermute | solution.py:746
  227.4 36.1 %collective-permute-start.25 = (bf16[256,1536]{1,0:T(8,128)(2,1)S(1)}, bf16[256,1536]{1,0:T(8,128)(2,1)}, u32[]{:S(2)}, u32[]{:S(2)}) collective-permute-start(bf16[256,1536]{1,0:T(8,128)(2,1)S(1)} %get-tuple-element.297.refs_4_), channel_id=1, source_target_pairs={{0,4},{1,5},{2,6},{3,7},{4,0},{5,1},{6,2},{7,3},{8,12},{9,13},{10,... | collective-permute-start | bytes 2359304 | tf_op jit(solution)/shard_map/ppermute | solution.py:746
  228.9 34.6 %collective-permute-start.26 = (bf16[256,1536]{1,0:T(8,128)(2,1)S(1)}, bf16[256,1536]{1,0:T(8,128)(2,1)}, u32[]{:S(2)}, u32[]{:S(2)}) collective-permute-start(bf16[256,1536]{1,0:T(8,128)(2,1)S(1)} %get-tuple-element.297.refs_4_), channel_id=1, source_target_pairs={{0,6},{1,7},{2,4},{3,5},{4,2},{5,3},{6,0},{7,1},{8,14},{9,15},{10,... | collective-permute-start | bytes 2359304 | tf_op jit(solution)/shard_map/ppermute | solution.py:746
  230.3 22.3 %collective-permute-start.23 = (bf16[256,1024]{1,0:T(8,128)(2,1)S(1)}, bf16[256,1024]{1,0:T(8,128)(2,1)}, u32[]{:S(2)}, u32[]{:S(2)}) collective-permute-start(bf16[256,1024]{1,0:T(8,128)(2,1)S(1)} %get-tuple-element.290.refs_3_.refs_7_), channel_id=1, source_target_pairs={{0,24},{1,25},{2,26},{3,27},{4,28},{5,29},{6,30},{7,31}} | collective-permute-start | bytes 1572872 | tf_op jit(solution)/shard_map/ppermute | solution.py:780
  263.5 263.6 %reduce-scatter.5.cloned.1.call-start = ((), (), s32[]{:S(2)}) async-start(), calls=%async_computation.17 | async-start | bytes 2949120 | tf_op jit(solution)/shard_map/reduce_scatter | solution.py:965
  263.5 25.0 %collective-permute-start.31 = (bf16[4,256,1536]{2,1,0:T(8,128)(2,1)}, bf16[4,256,1536]{2,1,0:T(8,128)(2,1)}, u32[]{:S(2)}, u32[]{:S(2)}) collective-permute-start(bf16[4,256,1536]{2,1,0:T(8,128)(2,1)} %all-to-all-done.4.refs_9_), channel_id=1, source_target_pairs={{0,1},{1,0},{2,3},{3,2},{4,5},{5,4},{6,7},{7,6},{8,9},{9,8},{10,11... | collective-permute-start | bytes 9437192 | tf_op jit(solution)/shard_map/ppermute | solution.py:743
  288.6 42.8 %collective-permute-start.32 = (bf16[256,1536]{1,0:T(8,128)(2,1)S(1)}, bf16[256,1536]{1,0:T(8,128)(2,1)S(1)}, u32[]{:S(2)}, u32[]{:S(2)}) collective-permute-start(bf16[256,1536]{1,0:T(8,128)(2,1)S(1)} %get-tuple-element.327.refs_4_), channel_id=1, source_target_pairs={{0,2},{1,3},{2,0},{3,1},{4,6},{5,7},{6,4},{7,5},{8,10},{9,11},{10,... | collective-permute-start | bytes 2359304 | tf_op jit(solution)/shard_map/ppermute | solution.py:746
  290.0 41.4 %collective-permute-start.33 = (bf16[256,1536]{1,0:T(8,128)(2,1)S(1)}, bf16[256,1536]{1,0:T(8,128)(2,1)S(1)}, u32[]{:S(2)}, u32[]{:S(2)}) collective-permute-start(bf16[256,1536]{1,0:T(8,128)(2,1)S(1)} %get-tuple-element.327.refs_4_), channel_id=1, source_target_pairs={{0,4},{1,5},{2,6},{3,7},{4,0},{5,1},{6,2},{7,3},{8,12},{9,13},{10,... | collective-permute-start | bytes 2359304 | tf_op jit(solution)/shard_map/ppermute | solution.py:746
  290.7 40.7 %collective-permute-start.34 = (bf16[256,1536]{1,0:T(8,128)(2,1)S(1)}, bf16[256,1536]{1,0:T(8,128)(2,1)}, u32[]{:S(2)}, u32[]{:S(2)}) collective-permute-start(bf16[256,1536]{1,0:T(8,128)(2,1)S(1)} %get-tuple-element.327.refs_4_), channel_id=1, source_target_pairs={{0,6},{1,7},{2,4},{3,5},{4,2},{5,3},{6,0},{7,1},{8,14},{9,15},{10,... | collective-permute-start | bytes 2359304 | tf_op jit(solution)/shard_map/ppermute | solution.py:746
  292.1 39.3 %collective-permute-start.35 = (bf16[256,1536]{1,0:T(8,128)(2,1)S(1)}, bf16[256,1536]{1,0:T(8,128)(2,1)}, u32[]{:S(2)}, u32[]{:S(2)}) collective-permute-start(bf16[256,1536]{1,0:T(8,128)(2,1)S(1)} %get-tuple-element.327.refs_4_), channel_id=1, source_target_pairs={{0,1},{1,0},{2,3},{3,2},{4,5},{5,4},{6,7},{7,6},{8,9},{9,8},{10,11... | collective-permute-start | bytes 2359304 | tf_op jit(solution)/shard_map/ppermute | solution.py:743
  378.1 148.9 %reduce-scatter.7.cloned.1.call-start = ((), (), s32[]{:S(2)}) async-start(), calls=%async_computation.18 | async-start | bytes 2949120 | tf_op jit(solution)/shard_map/reduce_scatter | solution.py:965
  429.9 46.2 %collective-permute-start.40 = (bf16[1024,1536]{1,0:T(8,128)(2,1)}, bf16[1024,1536]{1,0:T(8,128)(2,1)}, u32[]{:S(2)}, u32[]{:S(2)}) collective-permute-start(bf16[1024,1536]{1,0:T(8,128)(2,1)} %get-tuple-element.368), channel_id=1, source_target_pairs={{0,1},{1,0},{2,3},{3,2},{4,5},{5,4},{6,7},{7,6},{8,9},{9,8},{10,11... | collective-permute-start | bytes 9437192 | tf_op jit(solution)/shard_map/ppermute | solution.py:743
  430.2 45.9 %all-to-all-start.5 = ((bf16[4,256,1536]{2,1,0:T(8,128)(2,1)}), bf16[4,256,1536]{2,1,0:T(8,128)(2,1)}, u32[]{:S(2)}, u32[]{:S(2)}) async-start(bf16[4,256,1536]{2,1,0:T(8,128)(2,1)} %sums.7), calls=%async_computation.5 | async-start | bytes 6291456 | tf_op jit(solution)/shard_map/all_to_all | solution.py:750
  434.9 92.2 %reduce-scatter.9.cloned.1.call-start = ((), (), s32[]{:S(2)}) async-start(), calls=%async_computation.19 | async-start | bytes 2949120 | tf_op jit(solution)/shard_map/reduce_scatter | solution.py:965
  486.4 47.3 %collective-permute-start.42 = (bf16[1024,1536]{1,0:T(8,128)(2,1)}, bf16[1024,1536]{1,0:T(8,128)(2,1)}, u32[]{:S(2)}, u32[]{:S(2)}) collective-permute-start(bf16[1024,1536]{1,0:T(8,128)(2,1)} %get-tuple-element.392), channel_id=1, source_target_pairs={{0,1},{1,0},{2,3},{3,2},{4,5},{5,4},{6,7},{7,6},{8,9},{9,8},{10,11... | collective-permute-start | bytes 9437192 | tf_op jit(solution)/shard_map/ppermute | solution.py:743
  491.6 42.0 %all-to-all-start.6 = ((bf16[4,256,1536]{2,1,0:T(8,128)(2,1)}), bf16[4,256,1536]{2,1,0:T(8,128)(2,1)}, u32[]{:S(2)}, u32[]{:S(2)}) async-start(bf16[4,256,1536]{2,1,0:T(8,128)(2,1)} %sums.8), calls=%async_computation.6 | async-start | bytes 6291456 | tf_op jit(solution)/shard_map/all_to_all | solution.py:750
  535.0 45.6 %all-to-all-start.7 = ((bf16[4,256,1536]{2,1,0:T(8,128)(2,1)}), bf16[4,256,1536]{2,1,0:T(8,128)(2,1)}, u32[]{:S(2)}, u32[]{:S(2)}) async-start(bf16[4,256,1536]{2,1,0:T(8,128)(2,1)} %copy-done.10), calls=%async_computation.10 | async-start | bytes 6291456 | tf_op jit(solution)/shard_map/all_to_all | solution.py:750
  551.3 29.3 %collective-permute-start.45 = (bf16[4,4,48,1536]{3,2,1,0:T(8,128)(2,1)}, bf16[4,4,48,1536]{3,2,1,0:T(8,128)(2,1)}, u32[]{:S(2)}, u32[]{:S(2)}) collective-permute-start(bf16[4,4,48,1536]{3,2,1,0:T(8,128)(2,1)} %get-tuple-element.416), channel_id=1, source_target_pairs={{0,1},{1,0},{2,3},{3,2},{4,5},{5,4},{6,7},{7,6},{8,9},{9,8},{10,11... | collective-permute-start | bytes 7077896 | tf_op jit(solution)/shard_map/ppermute | solution.py:743
  551.4 29.2 %collective-permute-start.44 = (bf16[2,256,512]{2,1,0:T(8,128)(2,1)}, bf16[2,256,512]{2,1,0:T(8,128)(2,1)}, u32[]{:S(2)}, u32[]{:S(2)}) collective-permute-start(bf16[2,256,512]{2,1,0:T(8,128)(2,1)} %get-tuple-element.411), channel_id=1, source_target_pairs={{16,0},{24,8},{17,1},{25,9},{18,2},{26,10},{19,3},{27,11},{20,4},{... | collective-permute-start | bytes 1572872 | tf_op jit(solution)/shard_map/ppermute | solution.py:780
  580.6 22.9 %collective-permute-start.48 = (bf16[2,256,512]{2,1,0:T(8,128)(2,1)}, bf16[2,256,512]{2,1,0:T(8,128)(2,1)}, u32[]{:S(2)}, u32[]{:S(2)}) collective-permute-start(bf16[2,256,512]{2,1,0:T(8,128)(2,1)} %get-tuple-element.423), channel_id=1, source_target_pairs={{8,0},{16,8},{24,16},{9,1},{17,9},{25,17},{10,2},{18,10},{26,18},{... | collective-permute-start | bytes 1572872 | tf_op jit(solution)/shard_map/ppermute | solution.py:780
  582.2 30.2 %collective-permute-start.49 = (bf16[2,256,512]{2,1,0:T(8,128)(2,1)}, bf16[2,256,512]{2,1,0:T(8,128)(2,1)}, u32[]{:S(2)}, u32[]{:S(2)}) collective-permute-start(bf16[2,256,512]{2,1,0:T(8,128)(2,1)} %get-tuple-element.424), channel_id=1, source_target_pairs={{24,0},{25,1},{26,2},{27,3},{28,4},{29,5},{30,6},{31,7}} | collective-permute-start | bytes 1572872 | tf_op jit(solution)/shard_map/ppermute | solution.py:780
  612.4 45.4 %all-to-all-start.8 = ((bf16[4,4,48,1536]{3,2,1,0:T(8,128)(2,1)}), bf16[4,4,48,1536]{3,2,1,0:T(8,128)(2,1)}, u32[]{:S(2)}, u32[]{:S(2)}) async-start(bf16[4,4,48,1536]{3,2,1,0:T(8,128)(2,1)} %copy-done.12), calls=%async_computation.11 | async-start | bytes 4718592 | tf_op jit(solution)/shard_map/all_to_all | solution.py:750
  616.9 103.1 %reduce-scatter.11.cloned.1.call-start = ((), (), s32[]{:S(2)}) async-start(), calls=%async_computation.20 | async-start | bytes 2949120 | tf_op jit(solution)/shard_map/reduce_scatter | solution.py:965
  618.3 39.5 %collective-permute-start.46 = (bf16[2,256,512]{2,1,0:T(8,128)(2,1)}, bf16[2,256,512]{2,1,0:T(8,128)(2,1)}, u32[]{:S(2)}, u32[]{:S(2)}) collective-permute-start(bf16[2,256,512]{2,1,0:T(8,128)(2,1)} %get-tuple-element.421), channel_id=1, source_target_pairs={{16,0},{24,8},{17,1},{25,9},{18,2},{26,10},{19,3},{27,11},{20,4},{... | collective-permute-start | bytes 1572872 | tf_op jit(solution)/shard_map/ppermute | solution.py:780
  667.6 33.4 %all-to-all-start.9 = ((bf16[4,4,48,1536]{3,2,1,0:T(8,128)(2,1)}), bf16[4,4,48,1536]{3,2,1,0:T(8,128)(2,1)S(1)}, u32[]{:S(2)}, u32[]{:S(2)}) async-start(bf16[4,4,48,1536]{3,2,1,0:T(8,128)(2,1)} %copy-done.11), calls=%async_computation.12 | async-start | bytes 4718592 | tf_op jit(solution)/shard_map/all_to_all | solution.py:750
  677.4 34.5 %collective-permute-start.52 = (bf16[4,48,1152]{2,1,0:T(8,128)(2,1)}, bf16[4,48,1152]{2,1,0:T(8,128)(2,1)S(1)}, u32[]{:S(2)}, u32[]{:S(2)}) collective-permute-start(bf16[4,48,1152]{2,1,0:T(8,128)(2,1)} %get-tuple-element.526), channel_id=1, source_target_pairs={{0,2},{1,3},{2,0},{3,1},{4,6},{5,7},{6,4},{7,5},{8,10},{9,11},{10,... | collective-permute-start | bytes 1327112 | tf_op jit(solution)/shard_map/ppermute | solution.py:746
  679.4 32.5 %collective-permute-start.53 = (bf16[4,48,1152]{2,1,0:T(8,128)(2,1)}, bf16[4,48,1152]{2,1,0:T(8,128)(2,1)}, u32[]{:S(2)}, u32[]{:S(2)}) collective-permute-start(bf16[4,48,1152]{2,1,0:T(8,128)(2,1)} %get-tuple-element.525), channel_id=1, source_target_pairs={{0,4},{1,5},{2,6},{3,7},{4,0},{5,1},{6,2},{7,3},{8,12},{9,13},{10,... | collective-permute-start | bytes 1327112 | tf_op jit(solution)/shard_map/ppermute | solution.py:746
  680.9 39.2 %collective-permute-start.54 = (bf16[4,48,1152]{2,1,0:T(8,128)(2,1)}, bf16[4,48,1152]{2,1,0:T(8,128)(2,1)}, u32[]{:S(2)}, u32[]{:S(2)}) collective-permute-start(bf16[4,48,1152]{2,1,0:T(8,128)(2,1)} %get-tuple-element.524), channel_id=1, source_target_pairs={{0,6},{1,7},{2,4},{3,5},{4,2},{5,3},{6,0},{7,1},{8,14},{9,15},{10,... | collective-permute-start | bytes 1327112 | tf_op jit(solution)/shard_map/ppermute | solution.py:746
  720.1 40.8 %all-to-all-start.10 = ((bf16[4,256,1536]{2,1,0:T(8,128)(2,1)}), bf16[4,256,1536]{2,1,0:T(8,128)(2,1)}, u32[]{:S(2)}, u32[]{:S(2)}) async-start(bf16[4,256,1536]{2,1,0:T(8,128)(2,1)} %sums.10), calls=%async_computation.14 | async-start | bytes 6291456 | tf_op jit(solution)/shard_map/all_to_all | solution.py:750
  731.1 21.2 %collective-permute-start.59 = (bf16[48,2688]{1,0:T(8,128)(2,1)S(1)}, bf16[48,2688]{1,0:T(8,128)(2,1)S(1)}, u32[]{:S(2)}, u32[]{:S(2)}) collective-permute-start(bf16[48,2688]{1,0:T(8,128)(2,1)S(1)} %get-tuple-element.463), channel_id=1, source_target_pairs={{0,16},{8,24},{16,0},{24,8},{1,17},{9,25},{17,1},{25,9},{2,18},{10... | collective-permute-start | bytes 774152 | tf_op jit(solution)/shard_map/ppermute | solution.py:775
  (128 other events, 1785.1 us)
Sparse Core Ops, SparseCore 0:
  34.2 105.2 all-gather.2
  263.6 86.8 all-gather.4
  378.2 45.5 reduce-scatter.4
  430.3 45.4 reduce-scatter.6
  478.0 47.5 reduce-scatter.8
  657.9 55.9 reduce-scatter.10

commit v4 on v3

--- a/solution.py
+++ b/solution.py
@@ -476,6 +476,14 @@
     )(*inputs)
 
 
+def repeat_kernel(x_ref, out_ref):
+    out_ref[...] = jnp.broadcast_to(x_ref[...][None], out_ref.shape)
+
+
+def repeat(x, count):
+    return small_call(repeat_kernel, "repeat", [x], [((count,) + x.shape, x.dtype)])[0]
+
+
 def assemble_kernel(counts, chunk, place_ref, *refs):
     out_ref, sem = refs[len(counts) :]
     copies, n = [], 0
@@ -510,10 +518,29 @@
     )(places, *blocks)
 
 
-def project_kernel(width, *refs):
-    micro = (len(refs) - 2) // 3
-    x_refs, w_ref = refs[:micro], refs[micro]
-    h_refs, kv_refs, gains_ref = refs[micro + 1 : -1 - micro], refs[-1 - micro : -1], refs[-1]
+def project_kernel(micro, counts, chunk, place_ref, *refs):
+    refs = list(refs)
+
+    def take(n):
+        out = refs[:n]
+        del refs[:n]
+        return out
+
+    x_refs, blocks = take(micro), take(len(counts))
+    h_refs, kv_refs = take(micro), take(micro)
+    gains_ref, whole_ref, w_ref, sem_in, sem_out = refs
+    copies, n = [], 0
+    for ref, count in zip(blocks, counts):
+        for at in range(count):
+            rows = pl.ds(pl.multiple_of(place_ref[n] * chunk, chunk), chunk)
+            copies.append(pltpu.make_async_copy(ref.at[at], w_ref.at[rows], sem_in))
+            n += 1
+    for copy in copies:
+        copy.start()
+    for copy in copies:
+        copy.wait()
+    out = pltpu.make_async_copy(w_ref, whole_ref, sem_out)
+    out.start()
     kv_from = w_ref.shape[1] - 128 - kv_refs[0].shape[1]
     gains = w_ref[:, -128:].astype(F32).T
     gains_ref[...] = gains[:8]
@@ -521,17 +548,36 @@
         h = rms_norm(x_ref[...].astype(F32), gains[:1]).astype(BF16)
         h_ref[...] = h
         kv_ref[...] = mm(h, w_ref[:, kv_from:-128]).astype(BF16)
-
-
-def project(xs, weight, kv_width):
-    rows, width = xs[0].shape
+    out.wait()
+
+
+def project(xs, blocks, places, kv_width):
+    micro, (rows, width) = len(xs), xs[0].shape
+    if blocks[0].shape[1] % 16:
+        blocks, places = [assemble(blocks, places)[None]], jnp.zeros((1,), jnp.int32)
+    chunk, columns = blocks[0].shape[1:]
+    counts = [x.shape[0] for x in blocks]
+    weight = (sum(counts) * chunk, columns)
     outs = (
-        [((rows, width), BF16)] * len(xs)
-        + [((rows, kv_width), BF16)] * len(xs)
-        + [((8, width), F32)]
-    )
-    got = small_call(functools.partial(project_kernel, width), "project", [*xs, weight], outs)
-    return list(got[: len(xs)]), list(got[len(xs) : -1]), got[-1]
+        [((rows, width), BF16)] * micro
+        + [((rows, kv_width), BF16)] * micro
+        + [((8, width), F32), (weight, BF16)]
+    )
+    got = pl.pallas_call(
+        functools.partial(project_kernel, micro, counts, chunk),
+        in_specs=[SCALARS] + [NEAR] * micro + [FAR] * len(blocks),
+        out_specs=[NEAR] * (2 * micro + 1) + [FAR],
+        out_shape=[jax.ShapeDtypeStruct(shape, dtype) for shape, dtype in outs],
+        scratch_shapes=[
+            pltpu.VMEM(weight, BF16),
+            pltpu.SemaphoreType.DMA,
+            pltpu.SemaphoreType.DMA,
+        ],
+        compiler_params=pltpu.CompilerParams(vmem_limit_bytes=48 * 1024 * 1024),
+        cost_estimate=SMALL,
+        name="project",
+    )(places, *xs, *blocks)
+    return list(got[:micro]), list(got[micro : 2 * micro]), got[-2], got[-1]
 
 
 def middle_kernel(attn_ref, x_ref, gains_ref, w_ref, mid_ref, h_ref):
@@ -868,7 +914,7 @@
     for n in range(1, plane.chips.bit_length() - 1):
         held = plane.doubled(held, n)
     held, out_line, c_wide, w_last = join(
-        held, out_line, [wide(c) for c in grad_out], packed[1]
+        held, out_line, [repeat(c, plane.chips) for c in grad_out], packed[1]
     )
     moved = [(h, k, held[h][k]) for k in every for h in range(2)]
     out_spread = plane.exchange(wide(out_line))
@@ -878,11 +924,12 @@
     for c in (core, 1 - core):
         for h, k, _ in moved:
             places += bands(lines[h], chip ^ k, c)
-    weight = assemble(
-        [line, line_swap] + [x for _, _, x in moved] + swapped, jnp.stack(places)
-    )
-
-    (h_in, kv, gains), out_spread = join(project(x_in, weight, 2 * kv_width), out_spread)
+    blocks = [line, line_swap] + [x for _, _, x in moved] + swapped
+    places = jnp.stack(places)
+
+    (h_in, kv, gains, weight), out_spread = join(
+        project(x_in, blocks, places, 2 * kv_width), out_spread
+    )
     w_q = weight[:, :query_width]
     queries = [mm(h, w_q).astype(BF16) for h in h_in]
 

time: 785 us -> 785 us (level)
  local copies, waits for them, and re-layouts: 64.6 us -> 54.3 us
  Pallas kernels: 342 us -> 350 us
    pallas_call x0 -> x1, Pallas kernels: none -> 14.4 us  [project(): pl.pallas_call(functools.partial(project_kernel, micro, counts, chunk), i...]
    unnamed x200 -> x190, local copies, waits for them, and re-layouts: 44.7 us -> 34.5 us
    pallas_call x10 -> x11, Pallas kernels: 43.9 us -> 44 us  [small_call(): pl.pallas_call(kernel, in_specs=in_specs or [NEAR] * len(inputs), out_spe...]
  transfers between devices with their start and end apart: 78 -> 78, of which waited for: 27 -> 26; matrix products, arithmetic and copies ran while one was open for 7% -> 6% of each run, Pallas kernels for 44% -> 45%
where the time goes in v4:
time: 785 us; the launch traced here: 777 us
  Pallas kernels  350 us (45%)
  waiting for transfers between devices  180 us (23%)
  starting transfers between devices  139 us (18%)
  local copies, waits for them, and re-layouts  54.3 us (7%)
  other arithmetic  31.1 us (4%)
  between operations  15.8 us (2%)
    pallas_call x4, Pallas kernels, expert_pass(): pl.pallas_call(functools.partial(expert_kernel, block, chips, shards, pre...  162 us
    ppermute x12, waiting for transfers between devices, dp_along(): return lax.ppermute(x, 'dp', pairs)  82.5 us
    ppermute x12, starting transfers between devices, dp_along(): return lax.ppermute(x, 'dp', pairs)  54.2 us
    pallas_call x2, Pallas kernels, attend_back(): pl.pallas_call(functools.partial(attend_back_kernel, chunks), grid=(PAIRS...  51 us
    pallas_call x11, Pallas kernels, small_call(): pl.pallas_call(kernel, in_specs=in_specs or [NEAR] * len(inputs), out_spe...  44 us
    all_to_all x9, starting transfers between devices, exchange(): lax.all_to_all(x, 'expert', split_axis=0, concat_axis=0, axis_index_group...  40.6 us
    unnamed x190, local copies, waits for them, and re-layouts  34.5 us
    pallas_call x2, Pallas kernels, attend(): pl.pallas_call(functools.partial(attend_kernel, chunks), grid=(PAIRS,), i...  33.5 us
  transfers between devices with their start and end apart: 78, of which 26 were waited for; matrix products, arithmetic and copies ran while one was open for 6% of the time, Pallas kernels for 45%

profile of v4, /device:TPU:0, one launch (start us, length us, event | category | flops | bytes accessed | tf_op | source)
XLA Modules:
  0.0 776.8 jit_solution(7814493253222344482)
XLA Ops:
  41.4 6.9 all-to-all-start.1
  67.4 11.7 %all-to-all-done.1 = bf16[4,48,1536]{2,1,0:T(8,128)(2,1)} async-done(((bf16[4,48,1536]{2,1,0:T(8,128)(2,1)}), bf16[4,48,1536]{2,1,0:T(8,128)(2,1)}, u32[]{:S(2)}, u32[]{:S(2)}) %all-to-all-start.1) | async-done | bytes 589856 | tf_op jit(solution)/shard_map/all_to_all | solution.py:912
  92.6 14.4 %project.1 = (bf16[256,1536]{1,0:T(8,128)(2,1)}, bf16[256,1536]{1,0:T(8,128)(2,1)}, bf16[256,1024]{1,0:T(8,128)(2,1)}, bf16[256,1024]{1,0:T(8,128)(2,1)}, f32[8,...) custom-call(s32[32]{0:T(128)S(1)} %stack.277.place_ref, bf16[256,1536]{1,0:T(8,128)(2,1)} %get-tuple-element.536.refs_0_.x_ref, ...), custom_call_target="tpu_custom_call" | custom-call | flops 1024 | bytes 1024 | tf_op jit(solution)/shard_map/project/pallas_call | solution.py:566
  107.1 7.1 all-to-all-done.2
  114.2 4.7 all-to-all-start.3
  119.0 6.2 collective-permute-start.16
  130.1 4.8 fusion.4.q_ref
  137.2 5.4 assemble.1.w_ref
  144.8 10.1 %collective-permute-done.17.refs_1_.refs_5_ = bf16[256,1024]{1,0:T(8,128)(2,1)} collective-permute-done((bf16[256,1024]{1,0:T(8,128)(2,1)}, bf16[256,1024]{1,0:T(8,128)(2,1)}, u32[]{:S(2)}, u32[]{:S(2)}) %collective-permute-start.17) | collective-permute-done | bytes 524320 | tf_op jit(solution)/shard_map/ppermute | solution.py:826
  154.8 11.1 %collective-permute-done.18.refs_2_.refs_6_ = bf16[256,1024]{1,0:T(8,128)(2,1)} collective-permute-done((bf16[256,1024]{1,0:T(8,128)(2,1)}, bf16[256,1024]{1,0:T(8,128)(2,1)}, u32[]{:S(2)}, u32[]{:S(2)}) %collective-permute-start.18) | collective-permute-done | bytes 524320 | tf_op jit(solution)/shard_map/ppermute | solution.py:826
  165.9 4.7 all-to-all-start.4
  170.7 31.6 %collective-permute-start.20 = (bf16[256,1024]{1,0:T(8,128)(2,1)}, bf16[256,1024]{1,0:T(8,128)(2,1)S(1)}, u32[]{:S(2)}, u32[]{:S(2)}) collective-permute-start(bf16[256,1024]{1,0:T(8,128)(2,1)} %get-tuple-element.294.refs_3_.refs_7_), channel_id=1, source_target_pairs={{0,16},{8,24},{1,17},{9,25},{2,18},{10,26},{3,19},{11,27},{4,20},{... | collective-permute-start | bytes 1572872 | tf_op jit(solution)/shard_map/ppermute | solution.py:826
  202.3 16.7 %path_attention.2 = (bf16[256,1536]{1,0:T(8,128)(2,1)}, f32[4,8,256]{2,1,0:T(8,128)}) custom-call(bf16[256,1536]{1,0:T(8,128)(2,1)} %fusion.4.q_ref, bf16[256,1024]{1,0:T(8,128)(2,1)} %collective-permute-done.16.refs_0_.refs_4_, bf16[256,1024]{1,0:T(8,128)(2,1)} %collective-permute-done.17.refs_1_.refs_5_, ...), custom_call_target="tpu_custom_call" | custom-call | flops 25165824 | bytes 1048576 | tf_op jit(solution)/shard_map/path_attention/pallas_call | solution.py:106
  220.4 4.8 middle.2
  232.1 10.5 %collective-permute-done.22.refs_2_.refs_6_ = bf16[256,1024]{1,0:T(8,128)(2,1)S(1)} collective-permute-done((bf16[256,1024]{1,0:T(8,128)(2,1)}, bf16[256,1024]{1,0:T(8,128)(2,1)S(1)}, u32[]{:S(2)}, u32[]{:S(2)}) %collective-permute-start.22) | collective-permute-done | bytes 524320 | tf_op jit(solution)/shard_map/ppermute | solution.py:826
  242.6 10.1 %collective-permute-done.23.refs_0_.refs_4_ = bf16[256,1024]{1,0:T(8,128)(2,1)} collective-permute-done((bf16[256,1024]{1,0:T(8,128)(2,1)}, bf16[256,1024]{1,0:T(8,128)(2,1)}, u32[]{:S(2)}, u32[]{:S(2)}) %collective-permute-start.23) | collective-permute-done | bytes 524320 | tf_op jit(solution)/shard_map/ppermute | solution.py:826
  252.7 10.8 %collective-permute-done.25.refs_6_ = bf16[256,1536]{1,0:T(8,128)(2,1)} collective-permute-done((bf16[256,1536]{1,0:T(8,128)(2,1)}, bf16[256,1536]{1,0:T(8,128)(2,1)}, u32[]{:S(2)}, u32[]{:S(2)}) %collective-permute-start.25) | collective-permute-done | bytes 786464 | tf_op jit(solution)/shard_map/ppermute | solution.py:792
  264.8 16.7 %path_attention.3 = (bf16[256,1536]{1,0:T(8,128)(2,1)}, f32[4,8,256]{2,1,0:T(8,128)}) custom-call(bf16[256,1536]{1,0:T(8,128)(2,1)} %fusion.7.q_ref, bf16[256,1024]{1,0:T(8,128)(2,1)} %collective-permute-done.23.refs_0_.refs_4_, bf16[256,1024]{1,0:T(8,128)(2,1)} %copy-done.71, bf16[256,1024]{1,0:T(8,128)(2,1)} %copy-done.72, ...), custom_call_target="tpu_custom_call" | custom-call | flops 25165824 | bytes 1048576 | tf_op jit(solution)/shard_map/path_attention/pallas_call | solution.py:106
  282.7 4.9 middle.3
  292.2 39.3 %expert_pass.4 = (bf16[1024,1536]{1,0:T(8,128)(2,1)}, bf16[1024,1536]{1,0:T(8,128)(2,1)}, bf16[1024,1536]{1,0:T(8,128)(2,1)}, bf16[1024,1536]{1,0:T(8,128)(2,1)}...) custom-call(bf16[256,1536]{1,0:T(8,128)(2,1)} %collective-permute-done.27.refs_0_, ...), custom_call_target="tpu_custom_call" | custom-call | flops 1572864 | bytes 1572864 | tf_op jit(solution)/shard_map/expert_pass/pallas_call | solution.py:443
  337.3 40.9 %expert_pass.5 = (bf16[1024,1536]{1,0:T(8,128)(2,1)}, bf16[1024,1536]{1,0:T(8,128)(2,1)}, bf16[1024,1536]{1,0:T(8,128)(2,1)}, bf16[1024,1536]{1,0:T(8,128)(2,1)}...) custom-call(bf16[256,1536]{1,0:T(8,128)(2,1)} %collective-permute-done.35.refs_0_, bf16[256,1536]{1,0:T(8,128)(2,1)} %copy-done.75, ...), custom_call_target="tpu_custom_call" | custom-call | flops 1572864 | bytes 1572864 | tf_op jit(solution)/shard_map/expert_pass/pallas_call | solution.py:443
  378.3 40.8 %expert_pass.6 = (bf16[1024,1536]{1,0:T(8,128)(2,1)}, bf16[1024,1536]{1,0:T(8,128)(2,1)}, bf16[1024,1536]{1,0:T(8,128)(2,1)}, bf16[1024,1536]{1,0:T(8,128)(2,1)}...) custom-call(bf16[256,1536]{1,0:T(8,128)(2,1)} %collective-permute-do, ...), custom_call_target="tpu_custom_call", output_to_operand_aliasing={{0}: (13, {}), {1}: (14, {}), {2}: (15, {}), {3}: (16, {})} | custom-call | flops 1572864 | bytes 1572864 | tf_op jit(solution)/shard_map/expert_pass/pallas_call | solution.py:443
  419.4 5.7 collective-permute-done.39
  430.2 4.7 all-to-all-start.5
  434.9 41.0 %expert_pass.7 = (bf16[1024,1536]{1,0:T(8,128)(2,1)}, bf16[1024,1536]{1,0:T(8,128)(2,1)}, bf16[1024,1536]{1,0:T(8,128)(2,1)}, bf16[1024,1536]{1,0:T(8,128)(2,1)}...) custom-call(bf16[256,1536]{1,0:T(8,128)(2,1)} %collective-permute-do, ...), custom_call_target="tpu_custom_call", output_to_operand_aliasing={{0}: (13, {}), {1}: (14, {}), {2}: (15, {}), {3}: (16, {})} | custom-call | flops 1572864 | bytes 1572864 | tf_op jit(solution)/shard_map/expert_pass/pallas_call | solution.py:443
  477.1 5.7 middle_back.2
  486.2 5.0 sums.8
  491.2 4.9 all-to-all-start.6
  496.1 25.4 %path_attention_back.2 = (bf16[256,1536]{1,0:T(8,128)(2,1)}, bf16[2,256,512]{2,1,0:T(8,128)(2,1)}, bf16[2,256,512]{2,1,0:T(8,128)(2,1)}, bf16[2,256,512]{2,1,0:T(8,128)(2,1)}, bf16[2,256,512]{2,1,0:T(8,128)(2,1)}) custom-call(bf16[256,1536]{1,0:T(8,128)(2,1)} %fusion.4.q_ref, bf16[256,1536]{1,0:T(8,128)(2,1)} %copy-done.51, ...), custom_call_target="tpu_custom_call" | custom-call | flops 62914560 | bytes 1048576 | tf_op jit(solution)/shard_map/path_attention_back/pallas_call | solution.py:179
  526.7 6.5 all-to-all-done.6.got_ref
  534.6 4.7 all-to-all-start.7
  539.3 5.7 middle_back.3
  545.1 4.3 weight_grad.3
  554.5 25.6 %path_attention_back.3 = (bf16[256,1536]{1,0:T(8,128)(2,1)}, bf16[2,256,512]{2,1,0:T(8,128)(2,1)}, bf16[2,256,512]{2,1,0:T(8,128)(2,1)}, bf16[2,256,512]{2,1,0:T(8,128)(2,1)}, bf16[2,256,512]{2,1,0:T(8,128)(2,1)}) custom-call(bf16[256,1536]{1,0:T(8,128)(2,1)} %fusion.7.q_ref, bf16[256,1536]{1,0:T(8,128)(2,1)} %copy-done.50, ...), custom_call_target="tpu_custom_call" | custom-call | flops 62914560 | bytes 1048576 | tf_op jit(solution)/shard_map/path_attention_back/pallas_call | solution.py:179
  593.2 5.2 sums.10
  603.1 8.9 %collective-permute-done.49 = bf16[2,256,512]{2,1,0:T(8,128)(2,1)} collective-permute-done((bf16[2,256,512]{2,1,0:T(8,128)(2,1)}, bf16[2,256,512]{2,1,0:T(8,128)(2,1)}, u32[]{:S(2)}, u32[]{:S(2)}) %collective-permute-start.49) | collective-permute-done | bytes 524320 | tf_op jit(solution)/shard_map/ppermute | solution.py:826
  612.0 4.5 all-to-all-start.8
  625.4 9.9 %collective-permute-done.47 = bf16[2,256,512]{2,1,0:T(8,128)(2,1)} collective-permute-done((bf16[2,256,512]{2,1,0:T(8,128)(2,1)}, bf16[2,256,512]{2,1,0:T(8,128)(2,1)}, u32[]{:S(2)}, u32[]{:S(2)}) %collective-permute-start.47) | collective-permute-done | bytes 524320 | tf_op jit(solution)/shard_map/ppermute | solution.py:826
  635.4 22.0 %collective-permute-done.46 = bf16[2,256,512]{2,1,0:T(8,128)(2,1)} collective-permute-done((bf16[2,256,512]{2,1,0:T(8,128)(2,1)}, bf16[2,256,512]{2,1,0:T(8,128)(2,1)}, u32[]{:S(2)}, u32[]{:S(2)}) %collective-permute-start.46) | collective-permute-done | bytes 524320 | tf_op jit(solution)/shard_map/ppermute | solution.py:826
  661.4 4.6 weight_grad.5
  683.6 16.2 %collective-permute-done.55 = bf16[48,1536]{1,0:T(8,128)(2,1)S(1)} collective-permute-done((bf16[48,1536]{1,0:T(8,128)(2,1)S(1)}, bf16[48,1536]{1,0:T(8,128)(2,1)S(1)}, u32[]{:S(2)}, u32[]{:S(2)}) %collective-permute-start.55) | collective-permute-done | bytes 147488 | tf_op jit(solution)/shard_map/ppermute | solution.py:821
  701.0 10.4 %collective-permute-done.57 = bf16[48,1536]{1,0:T(8,128)(2,1)} collective-permute-done((bf16[48,1536]{1,0:T(8,128)(2,1)S(1)}, bf16[48,1536]{1,0:T(8,128)(2,1)}, u32[]{:S(2)}, u32[]{:S(2)}) %collective-permute-start.57) | collective-permute-done | bytes 147488 | tf_op jit(solution)/shard_map/ppermute | solution.py:821
  711.5 8.2 %collective-permute-done.54.refs_4_ = bf16[4,48,1152]{2,1,0:T(8,128)(2,1)} collective-permute-done((bf16[4,48,1152]{2,1,0:T(8,128)(2,1)}, bf16[4,48,1152]{2,1,0:T(8,128)(2,1)}, u32[]{:S(2)}, u32[]{:S(2)}) %collective-permute-start.54) | collective-permute-done | bytes 442400 | tf_op jit(solution)/shard_map/ppermute | solution.py:792
  719.7 4.8 all-to-all-start.10
  730.8 4.3 collective-permute-start.60
  735.2 5.9 input_back.2
  741.1 6.0 input_back.3
  751.9 8.5 %all-to-all-done.10 = bf16[4,256,1536]{2,1,0:T(8,128)(2,1)} async-done(((bf16[4,256,1536]{2,1,0:T(8,128)(2,1)}), bf16[4,256,1536]{2,1,0:T(8,128)(2,1)}, u32[]{:S(2)}, u32[]{:S(2)}) %all-to-all-start.10) | async-done | bytes 3145760 | tf_op jit(solution)/shard_map/all_to_all | solution.py:796
  (406 shorter events, 187.9 us)
Async XLA Ops:
  8.9 23.1 %collective-permute-start = (bf16[48,2688]{1,0:T(8,128)(2,1)S(1)}, bf16[48,2688]{1,0:T(8,128)(2,1)S(1)}, u32[]{:S(2)}, u32[]{:S(2)}) collective-permute-start(bf16[48,2688]{1,0:T(8,128)(2,1)S(1)} %fusion.20), channel_id=1, source_target_pairs={{0,8},{8,0},{16,24},{24,16},{1,9},{9,1},{17,25},{25,17},{2,10},{10... | collective-permute-start | bytes 774152 | tf_op jit(solution)/shard_map/ppermute | solution.py:821
  12.0 21.1 %collective-permute-start.1 = (bf16[48,2688]{1,0:T(8,128)(2,1)S(1)}, bf16[48,2688]{1,0:T(8,128)(2,1)S(1)}, u32[]{:S(2)}, u32[]{:S(2)}) collective-permute-start(bf16[48,2688]{1,0:T(8,128)(2,1)S(1)} %fusion.20), channel_id=1, source_target_pairs={{0,16},{8,24},{16,0},{24,8},{1,17},{9,25},{17,1},{25,9},{2,18},{10... | collective-permute-start | bytes 774152 | tf_op jit(solution)/shard_map/ppermute | solution.py:821
  19.9 146.0 %all-gather.3.cloned.1.call-start = ((), (), s32[]{:S(2)}) async-start(), calls=%async_computation.15 | async-start | bytes 5898240 | tf_op jit(solution)/shard_map/all_gather | solution.py:868
  41.4 37.7 %all-to-all-start.1 = ((bf16[4,48,1536]{2,1,0:T(8,128)(2,1)}), bf16[4,48,1536]{2,1,0:T(8,128)(2,1)}, u32[]{:S(2)}, u32[]{:S(2)}) async-start(bf16[4,48,1536]{2,1,0:T(8,128)(2,1)} %broadcast_in_dim.70), calls=%async_computation.1 | async-start | bytes 1179648 | tf_op jit(solution)/shard_map/all_to_all | solution.py:912
  53.7 25.4 %collective-permute-start.6 = (bf16[2,48,2688]{2,1,0:T(8,128)(2,1)}, bf16[2,48,2688]{2,1,0:T(8,128)(2,1)S(1)}, u32[]{:S(2)}, u32[]{:S(2)}) collective-permute-start(bf16[2,48,2688]{2,1,0:T(8,128)(2,1)} %pad_maximum_fusion.3), channel_id=1, source_target_pairs={{0,4},{1,5},{2,6},{3,7},{4,0},{5,1},{6,2},{7,3},{8,12},{9,13},{10,... | collective-permute-start | bytes 1548296 | tf_op jit(solution)/shard_map/ppermute | solution.py:792
  55.3 23.8 %collective-permute-start.7 = (bf16[2,48,2688]{2,1,0:T(8,128)(2,1)S(1)}, bf16[2,48,2688]{2,1,0:T(8,128)(2,1)S(1)}, u32[]{:S(2)}, u32[]{:S(2)}) collective-permute-start(bf16[2,48,2688]{2,1,0:T(8,128)(2,1)S(1)} %collective-permute-done.3.refs_4_), channel_id=1, source_target_pairs={{0,4},{1,5},{2,6},{3,7},{4,0},{5,1},{6,2},{7,3},{8,12},{9,13},{10,... | collective-permute-start | bytes 1548296 | tf_op jit(solution)/shard_map/ppermute | solution.py:792
  55.8 23.3 %collective-permute-start.8 = (bf16[2,48,2688]{2,1,0:T(8,128)(2,1)}, bf16[2,48,2688]{2,1,0:T(8,128)(2,1)}, u32[]{:S(2)}, u32[]{:S(2)}) collective-permute-start(bf16[2,48,2688]{2,1,0:T(8,128)(2,1)} %pad_maximum_fusion.4), channel_id=1, source_target_pairs={{0,2},{1,3},{2,0},{3,1},{4,6},{5,7},{6,4},{7,5},{8,10},{9,11},{10,... | collective-permute-start | bytes 1548296 | tf_op jit(solution)/shard_map/ppermute | solution.py:792
  56.3 23.1 %collective-permute-start.9 = (bf16[2,48,2688]{2,1,0:T(8,128)(2,1)S(1)}, bf16[2,48,2688]{2,1,0:T(8,128)(2,1)}, u32[]{:S(2)}, u32[]{:S(2)}) collective-permute-start(bf16[2,48,2688]{2,1,0:T(8,128)(2,1)S(1)} %collective-permute-done.4.refs_7_), channel_id=1, source_target_pairs={{0,2},{1,3},{2,0},{3,1},{4,6},{5,7},{6,4},{7,5},{8,10},{9,11},{10,... | collective-permute-start | bytes 1548296 | tf_op jit(solution)/shard_map/ppermute | solution.py:792
  82.3 31.9 %all-to-all-start.2 = ((bf16[4,4,48,1536]{3,2,1,0:T(8,128)(2,1)}), bf16[4,4,48,1536]{3,2,1,0:T(8,128)(2,1)S(1)}, u32[]{:S(2)}, u32[]{:S(2)}) async-start(bf16[4,4,48,1536]{3,2,1,0:T(8,128)(2,1)} %broadcast_in_dim.80), calls=%async_computation.2 | async-start | bytes 4718592 | tf_op jit(solution)/shard_map/all_to_all | solution.py:796
  114.2 23.0 %collective-permute-start.19 = (bf16[4,4,48,1536]{3,2,1,0:T(8,128)(2,1)S(1)}, bf16[4,4,48,1536]{3,2,1,0:T(8,128)(2,1)}, u32[]{:S(2)}, u32[]{:S(2)}) collective-permute-start(bf16[4,4,48,1536]{3,2,1,0:T(8,128)(2,1)S(1)} %all-to-all-done.2), channel_id=1, source_target_pairs={{0,1},{1,0},{2,3},{3,2},{4,5},{5,4},{6,7},{7,6},{8,9},{9,8},{10,11... | collective-permute-start | bytes 7077896 | tf_op jit(solution)/shard_map/ppermute | solution.py:789
  114.2 51.8 %all-to-all-start.3 = ((bf16[4,256,1536]{2,1,0:T(8,128)(2,1)}), bf16[4,256,1536]{2,1,0:T(8,128)(2,1)}, u32[]{:S(2)}, u32[]{:S(2)}) async-start(bf16[4,256,1536]{2,1,0:T(8,128)(2,1)} %repeat.2), calls=%async_computation.3 | async-start | bytes 6291456 | tf_op jit(solution)/shard_map/all_to_all | solution.py:796
  119.0 25.8 %collective-permute-start.16 = (bf16[256,1024]{1,0:T(8,128)(2,1)}, bf16[256,1024]{1,0:T(8,128)(2,1)}, u32[]{:S(2)}, u32[]{:S(2)}) collective-permute-start(bf16[256,1024]{1,0:T(8,128)(2,1)} %get-tuple-element.279.refs_3_.refs_7_), channel_id=1, source_target_pairs={{0,24},{1,25},{2,26},{3,27},{4,28},{5,29},{6,30},{7,31}} | collective-permute-start | bytes 1572872 | tf_op jit(solution)/shard_map/ppermute | solution.py:826
  125.2 29.6 %collective-permute-start.17 = (bf16[256,1024]{1,0:T(8,128)(2,1)}, bf16[256,1024]{1,0:T(8,128)(2,1)}, u32[]{:S(2)}, u32[]{:S(2)}) collective-permute-start(bf16[256,1024]{1,0:T(8,128)(2,1)} %get-tuple-element.279.refs_3_.refs_7_), channel_id=1, source_target_pairs={{0,16},{8,24},{1,17},{9,25},{2,18},{10,26},{3,19},{11,27},{4,20},{... | collective-permute-start | bytes 1572872 | tf_op jit(solution)/shard_map/ppermute | solution.py:826
  127.3 38.6 %collective-permute-start.18 = (bf16[256,1024]{1,0:T(8,128)(2,1)}, bf16[256,1024]{1,0:T(8,128)(2,1)}, u32[]{:S(2)}, u32[]{:S(2)}) collective-permute-start(bf16[256,1024]{1,0:T(8,128)(2,1)} %get-tuple-element.279.refs_3_.refs_7_), channel_id=1, source_target_pairs={{0,8},{8,16},{16,24},{1,9},{9,17},{17,25},{2,10},{10,18},{18,26},{... | collective-permute-start | bytes 1572872 | tf_op jit(solution)/shard_map/ppermute | solution.py:826
  165.9 53.2 %collective-permute-start.21 = (bf16[4,256,1536]{2,1,0:T(8,128)(2,1)}, bf16[4,256,1536]{2,1,0:T(8,128)(2,1)}, u32[]{:S(2)}, u32[]{:S(2)}) collective-permute-start(bf16[4,256,1536]{2,1,0:T(8,128)(2,1)} %all-to-all-done.3.refs_9_), channel_id=1, source_target_pairs={{0,1},{1,0},{2,3},{3,2},{4,5},{5,4},{6,7},{7,6},{8,9},{9,8},{10,11... | collective-permute-start | bytes 9437192 | tf_op jit(solution)/shard_map/ppermute | solution.py:789
  165.9 66.2 %all-to-all-start.4 = ((bf16[4,256,1536]{2,1,0:T(8,128)(2,1)}), bf16[4,256,1536]{2,1,0:T(8,128)(2,1)}, u32[]{:S(2)}, u32[]{:S(2)}) async-start(bf16[4,256,1536]{2,1,0:T(8,128)(2,1)} %repeat.3), calls=%async_computation.4 | async-start | bytes 6291456 | tf_op jit(solution)/shard_map/all_to_all | solution.py:796
  170.6 207.6 %all-gather.5.cloned.1.call-start = ((), (), s32[]{:S(2)}) async-start(), calls=%async_computation.16 | async-start | bytes 5898240 | tf_op jit(solution)/shard_map/all_gather | solution.py:868
  170.7 48.4 %collective-permute-start.20 = (bf16[256,1024]{1,0:T(8,128)(2,1)}, bf16[256,1024]{1,0:T(8,128)(2,1)S(1)}, u32[]{:S(2)}, u32[]{:S(2)}) collective-permute-start(bf16[256,1024]{1,0:T(8,128)(2,1)} %get-tuple-element.294.refs_3_.refs_7_), channel_id=1, source_target_pairs={{0,16},{8,24},{1,17},{9,25},{2,18},{10,26},{3,19},{11,27},{4,20},{... | collective-permute-start | bytes 1572872 | tf_op jit(solution)/shard_map/ppermute | solution.py:826
  225.2 27.5 %collective-permute-start.24 = (bf16[256,1536]{1,0:T(8,128)(2,1)}, bf16[256,1536]{1,0:T(8,128)(2,1)}, u32[]{:S(2)}, u32[]{:S(2)}) collective-permute-start(bf16[256,1536]{1,0:T(8,128)(2,1)} %get-tuple-element.301.refs_4_), channel_id=1, source_target_pairs={{0,2},{1,3},{2,0},{3,1},{4,6},{5,7},{6,4},{7,5},{8,10},{9,11},{10,... | collective-permute-start | bytes 2359304 | tf_op jit(solution)/shard_map/ppermute | solution.py:792
  227.1 36.4 %collective-permute-start.25 = (bf16[256,1536]{1,0:T(8,128)(2,1)}, bf16[256,1536]{1,0:T(8,128)(2,1)}, u32[]{:S(2)}, u32[]{:S(2)}) collective-permute-start(bf16[256,1536]{1,0:T(8,128)(2,1)} %get-tuple-element.301.refs_4_), channel_id=1, source_target_pairs={{0,4},{1,5},{2,6},{3,7},{4,0},{5,1},{6,2},{7,3},{8,12},{9,13},{10,... | collective-permute-start | bytes 2359304 | tf_op jit(solution)/shard_map/ppermute | solution.py:792
  228.7 34.8 %collective-permute-start.26 = (bf16[256,1536]{1,0:T(8,128)(2,1)}, bf16[256,1536]{1,0:T(8,128)(2,1)}, u32[]{:S(2)}, u32[]{:S(2)}) collective-permute-start(bf16[256,1536]{1,0:T(8,128)(2,1)} %get-tuple-element.301.refs_4_), channel_id=1, source_target_pairs={{0,6},{1,7},{2,4},{3,5},{4,2},{5,3},{6,0},{7,1},{8,14},{9,15},{10,... | collective-permute-start | bytes 2359304 | tf_op jit(solution)/shard_map/ppermute | solution.py:792
  230.0 22.7 %collective-permute-start.23 = (bf16[256,1024]{1,0:T(8,128)(2,1)}, bf16[256,1024]{1,0:T(8,128)(2,1)}, u32[]{:S(2)}, u32[]{:S(2)}) collective-permute-start(bf16[256,1024]{1,0:T(8,128)(2,1)} %get-tuple-element.294.refs_3_.refs_7_), channel_id=1, source_target_pairs={{0,24},{1,25},{2,26},{3,27},{4,28},{5,29},{6,30},{7,31}} | collective-permute-start | bytes 1572872 | tf_op jit(solution)/shard_map/ppermute | solution.py:826
  263.5 263.1 %reduce-scatter.5.cloned.1.call-start = ((), (), s32[]{:S(2)}) async-start(), calls=%async_computation.17 | async-start | bytes 2949120 | tf_op jit(solution)/shard_map/reduce_scatter | solution.py:1012
  263.6 25.2 %collective-permute-start.31 = (bf16[4,256,1536]{2,1,0:T(8,128)(2,1)}, bf16[4,256,1536]{2,1,0:T(8,128)(2,1)}, u32[]{:S(2)}, u32[]{:S(2)}) collective-permute-start(bf16[4,256,1536]{2,1,0:T(8,128)(2,1)} %all-to-all-done.4.refs_9_), channel_id=1, source_target_pairs={{0,1},{1,0},{2,3},{3,2},{4,5},{5,4},{6,7},{7,6},{8,9},{9,8},{10,11... | collective-permute-start | bytes 9437192 | tf_op jit(solution)/shard_map/ppermute | solution.py:789
  288.8 42.8 %collective-permute-start.32 = (bf16[256,1536]{1,0:T(8,128)(2,1)}, bf16[256,1536]{1,0:T(8,128)(2,1)S(1)}, u32[]{:S(2)}, u32[]{:S(2)}) collective-permute-start(bf16[256,1536]{1,0:T(8,128)(2,1)} %get-tuple-element.331.refs_4_), channel_id=1, source_target_pairs={{0,2},{1,3},{2,0},{3,1},{4,6},{5,7},{6,4},{7,5},{8,10},{9,11},{10,... | collective-permute-start | bytes 2359304 | tf_op jit(solution)/shard_map/ppermute | solution.py:792
  290.1 41.4 %collective-permute-start.33 = (bf16[256,1536]{1,0:T(8,128)(2,1)}, bf16[256,1536]{1,0:T(8,128)(2,1)}, u32[]{:S(2)}, u32[]{:S(2)}) collective-permute-start(bf16[256,1536]{1,0:T(8,128)(2,1)} %get-tuple-element.331.refs_4_), channel_id=1, source_target_pairs={{0,4},{1,5},{2,6},{3,7},{4,0},{5,1},{6,2},{7,3},{8,12},{9,13},{10,... | collective-permute-start | bytes 2359304 | tf_op jit(solution)/shard_map/ppermute | solution.py:792
  290.8 40.8 %collective-permute-start.34 = (bf16[256,1536]{1,0:T(8,128)(2,1)}, bf16[256,1536]{1,0:T(8,128)(2,1)}, u32[]{:S(2)}, u32[]{:S(2)}) collective-permute-start(bf16[256,1536]{1,0:T(8,128)(2,1)} %get-tuple-element.331.refs_4_), channel_id=1, source_target_pairs={{0,6},{1,7},{2,4},{3,5},{4,2},{5,3},{6,0},{7,1},{8,14},{9,15},{10,... | collective-permute-start | bytes 2359304 | tf_op jit(solution)/shard_map/ppermute | solution.py:792
  292.2 39.4 %collective-permute-start.35 = (bf16[256,1536]{1,0:T(8,128)(2,1)}, bf16[256,1536]{1,0:T(8,128)(2,1)}, u32[]{:S(2)}, u32[]{:S(2)}) collective-permute-start(bf16[256,1536]{1,0:T(8,128)(2,1)} %get-tuple-element.331.refs_4_), channel_id=1, source_target_pairs={{0,1},{1,0},{2,3},{3,2},{4,5},{5,4},{6,7},{7,6},{8,9},{9,8},{10,11... | collective-permute-start | bytes 2359304 | tf_op jit(solution)/shard_map/ppermute | solution.py:789
  378.3 148.4 %reduce-scatter.7.cloned.1.call-start = ((), (), s32[]{:S(2)}) async-start(), calls=%async_computation.18 | async-start | bytes 2949120 | tf_op jit(solution)/shard_map/reduce_scatter | solution.py:1012
  430.0 46.0 %collective-permute-start.40 = (bf16[1024,1536]{1,0:T(8,128)(2,1)}, bf16[1024,1536]{1,0:T(8,128)(2,1)}, u32[]{:S(2)}, u32[]{:S(2)}) collective-permute-start(bf16[1024,1536]{1,0:T(8,128)(2,1)} %get-tuple-element.372), channel_id=1, source_target_pairs={{0,1},{1,0},{2,3},{3,2},{4,5},{5,4},{6,7},{7,6},{8,9},{9,8},{10,11... | collective-permute-start | bytes 9437192 | tf_op jit(solution)/shard_map/ppermute | solution.py:789
  430.2 45.8 %all-to-all-start.5 = ((bf16[4,256,1536]{2,1,0:T(8,128)(2,1)}), bf16[4,256,1536]{2,1,0:T(8,128)(2,1)}, u32[]{:S(2)}, u32[]{:S(2)}) async-start(bf16[4,256,1536]{2,1,0:T(8,128)(2,1)} %sums.7), calls=%async_computation.5 | async-start | bytes 6291456 | tf_op jit(solution)/shard_map/all_to_all | solution.py:796
  434.9 91.8 %reduce-scatter.9.cloned.1.call-start = ((), (), s32[]{:S(2)}) async-start(), calls=%async_computation.19 | async-start | bytes 2949120 | tf_op jit(solution)/shard_map/reduce_scatter | solution.py:1012
  485.8 47.3 %collective-permute-start.42 = (bf16[1024,1536]{1,0:T(8,128)(2,1)}, bf16[1024,1536]{1,0:T(8,128)(2,1)}, u32[]{:S(2)}, u32[]{:S(2)}) collective-permute-start(bf16[1024,1536]{1,0:T(8,128)(2,1)} %get-tuple-element.396), channel_id=1, source_target_pairs={{0,1},{1,0},{2,3},{3,2},{4,5},{5,4},{6,7},{7,6},{8,9},{9,8},{10,11... | collective-permute-start | bytes 9437192 | tf_op jit(solution)/shard_map/ppermute | solution.py:789
  491.2 41.9 %all-to-all-start.6 = ((bf16[4,256,1536]{2,1,0:T(8,128)(2,1)}), bf16[4,256,1536]{2,1,0:T(8,128)(2,1)}, u32[]{:S(2)}, u32[]{:S(2)}) async-start(bf16[4,256,1536]{2,1,0:T(8,128)(2,1)} %sums.8), calls=%async_computation.6 | async-start | bytes 6291456 | tf_op jit(solution)/shard_map/all_to_all | solution.py:796
  534.6 45.6 %all-to-all-start.7 = ((bf16[4,256,1536]{2,1,0:T(8,128)(2,1)}), bf16[4,256,1536]{2,1,0:T(8,128)(2,1)}, u32[]{:S(2)}, u32[]{:S(2)}) async-start(bf16[4,256,1536]{2,1,0:T(8,128)(2,1)} %copy-done.9), calls=%async_computation.10 | async-start | bytes 6291456 | tf_op jit(solution)/shard_map/all_to_all | solution.py:796
  550.9 29.3 %collective-permute-start.45 = (bf16[4,4,48,1536]{3,2,1,0:T(8,128)(2,1)}, bf16[4,4,48,1536]{3,2,1,0:T(8,128)(2,1)}, u32[]{:S(2)}, u32[]{:S(2)}) collective-permute-start(bf16[4,4,48,1536]{3,2,1,0:T(8,128)(2,1)} %get-tuple-element.420), channel_id=1, source_target_pairs={{0,1},{1,0},{2,3},{3,2},{4,5},{5,4},{6,7},{7,6},{8,9},{9,8},{10,11... | collective-permute-start | bytes 7077896 | tf_op jit(solution)/shard_map/ppermute | solution.py:789
  550.9 29.2 %collective-permute-start.44 = (bf16[2,256,512]{2,1,0:T(8,128)(2,1)}, bf16[2,256,512]{2,1,0:T(8,128)(2,1)}, u32[]{:S(2)}, u32[]{:S(2)}) collective-permute-start(bf16[2,256,512]{2,1,0:T(8,128)(2,1)} %get-tuple-element.415), channel_id=1, source_target_pairs={{16,0},{24,8},{17,1},{25,9},{18,2},{26,10},{19,3},{27,11},{20,4},{... | collective-permute-start | bytes 1572872 | tf_op jit(solution)/shard_map/ppermute | solution.py:826
  580.2 22.9 %collective-permute-start.48 = (bf16[2,256,512]{2,1,0:T(8,128)(2,1)}, bf16[2,256,512]{2,1,0:T(8,128)(2,1)}, u32[]{:S(2)}, u32[]{:S(2)}) collective-permute-start(bf16[2,256,512]{2,1,0:T(8,128)(2,1)} %get-tuple-element.427), channel_id=1, source_target_pairs={{8,0},{16,8},{24,16},{9,1},{17,9},{25,17},{10,2},{18,10},{26,18},{... | collective-permute-start | bytes 1572872 | tf_op jit(solution)/shard_map/ppermute | solution.py:826
  581.7 30.2 %collective-permute-start.49 = (bf16[2,256,512]{2,1,0:T(8,128)(2,1)}, bf16[2,256,512]{2,1,0:T(8,128)(2,1)}, u32[]{:S(2)}, u32[]{:S(2)}) collective-permute-start(bf16[2,256,512]{2,1,0:T(8,128)(2,1)} %get-tuple-element.428), channel_id=1, source_target_pairs={{24,0},{25,1},{26,2},{27,3},{28,4},{29,5},{30,6},{31,7}} | collective-permute-start | bytes 1572872 | tf_op jit(solution)/shard_map/ppermute | solution.py:826
  612.0 45.4 %all-to-all-start.8 = ((bf16[4,4,48,1536]{3,2,1,0:T(8,128)(2,1)}), bf16[4,4,48,1536]{3,2,1,0:T(8,128)(2,1)}, u32[]{:S(2)}, u32[]{:S(2)}) async-start(bf16[4,4,48,1536]{3,2,1,0:T(8,128)(2,1)} %copy-done.11), calls=%async_computation.11 | async-start | bytes 4718592 | tf_op jit(solution)/shard_map/all_to_all | solution.py:796
  616.5 103.2 %reduce-scatter.11.cloned.1.call-start = ((), (), s32[]{:S(2)}) async-start(), calls=%async_computation.20 | async-start | bytes 2949120 | tf_op jit(solution)/shard_map/reduce_scatter | solution.py:1012
  617.9 39.5 %collective-permute-start.46 = (bf16[2,256,512]{2,1,0:T(8,128)(2,1)}, bf16[2,256,512]{2,1,0:T(8,128)(2,1)}, u32[]{:S(2)}, u32[]{:S(2)}) collective-permute-start(bf16[2,256,512]{2,1,0:T(8,128)(2,1)} %get-tuple-element.425), channel_id=1, source_target_pairs={{16,0},{24,8},{17,1},{25,9},{18,2},{26,10},{19,3},{27,11},{20,4},{... | collective-permute-start | bytes 1572872 | tf_op jit(solution)/shard_map/ppermute | solution.py:826
  667.4 33.1 %all-to-all-start.9 = ((bf16[4,4,48,1536]{3,2,1,0:T(8,128)(2,1)}), bf16[4,4,48,1536]{3,2,1,0:T(8,128)(2,1)S(1)}, u32[]{:S(2)}, u32[]{:S(2)}) async-start(bf16[4,4,48,1536]{3,2,1,0:T(8,128)(2,1)} %copy-done.10), calls=%async_computation.12 | async-start | bytes 4718592 | tf_op jit(solution)/shard_map/all_to_all | solution.py:796
  677.1 34.4 %collective-permute-start.52 = (bf16[4,48,1152]{2,1,0:T(8,128)(2,1)}, bf16[4,48,1152]{2,1,0:T(8,128)(2,1)S(1)}, u32[]{:S(2)}, u32[]{:S(2)}) collective-permute-start(bf16[4,48,1152]{2,1,0:T(8,128)(2,1)} %get-tuple-element.530), channel_id=1, source_target_pairs={{0,2},{1,3},{2,0},{3,1},{4,6},{5,7},{6,4},{7,5},{8,10},{9,11},{10,... | collective-permute-start | bytes 1327112 | tf_op jit(solution)/shard_map/ppermute | solution.py:792
  679.1 32.4 %collective-permute-start.53 = (bf16[4,48,1152]{2,1,0:T(8,128)(2,1)}, bf16[4,48,1152]{2,1,0:T(8,128)(2,1)}, u32[]{:S(2)}, u32[]{:S(2)}) collective-permute-start(bf16[4,48,1152]{2,1,0:T(8,128)(2,1)} %get-tuple-element.529), channel_id=1, source_target_pairs={{0,4},{1,5},{2,6},{3,7},{4,0},{5,1},{6,2},{7,3},{8,12},{9,13},{10,... | collective-permute-start | bytes 1327112 | tf_op jit(solution)/shard_map/ppermute | solution.py:792
  680.5 39.1 %collective-permute-start.54 = (bf16[4,48,1152]{2,1,0:T(8,128)(2,1)}, bf16[4,48,1152]{2,1,0:T(8,128)(2,1)}, u32[]{:S(2)}, u32[]{:S(2)}) collective-permute-start(bf16[4,48,1152]{2,1,0:T(8,128)(2,1)} %get-tuple-element.528), channel_id=1, source_target_pairs={{0,6},{1,7},{2,4},{3,5},{4,2},{5,3},{6,0},{7,1},{8,14},{9,15},{10,... | collective-permute-start | bytes 1327112 | tf_op jit(solution)/shard_map/ppermute | solution.py:792
  719.7 40.7 %all-to-all-start.10 = ((bf16[4,256,1536]{2,1,0:T(8,128)(2,1)}), bf16[4,256,1536]{2,1,0:T(8,128)(2,1)}, u32[]{:S(2)}, u32[]{:S(2)}) async-start(bf16[4,256,1536]{2,1,0:T(8,128)(2,1)} %sums.10), calls=%async_computation.14 | async-start | bytes 6291456 | tf_op jit(solution)/shard_map/all_to_all | solution.py:796
  730.7 21.2 %collective-permute-start.59 = (bf16[48,2688]{1,0:T(8,128)(2,1)S(1)}, bf16[48,2688]{1,0:T(8,128)(2,1)S(1)}, u32[]{:S(2)}, u32[]{:S(2)}) collective-permute-start(bf16[48,2688]{1,0:T(8,128)(2,1)S(1)} %get-tuple-element.467), channel_id=1, source_target_pairs={{0,16},{8,24},{16,0},{24,8},{1,17},{9,25},{17,1},{25,9},{2,18},{10... | collective-permute-start | bytes 774152 | tf_op jit(solution)/shard_map/ppermute | solution.py:821
  (123 other events, 1594.4 us)
Sparse Core Ops, SparseCore 0:
  34.2 105.2 all-gather.2
  263.6 86.8 all-gather.4
  378.4 45.4 reduce-scatter.4
  430.3 45.5 reduce-scatter.6
  478.1 47.5 reduce-scatter.8
  657.5 55.8 reduce-scatter.10

commit v5 on v4

--- a/solution.py
+++ b/solution.py
@@ -927,9 +927,7 @@
     blocks = [line, line_swap] + [x for _, _, x in moved] + swapped
     places = jnp.stack(places)
 
-    (h_in, kv, gains, weight), out_spread = join(
-        project(x_in, blocks, places, 2 * kv_width), out_spread
-    )
+    h_in, kv, gains, weight = project(x_in, blocks, places, 2 * kv_width)
     w_q = weight[:, :query_width]
     queries = [mm(h, w_q).astype(BF16) for h in h_in]
 

time: 785 us -> 794 us (1.011)
  blocking collectives: 0 us -> 31.2 us
  waiting for transfers between devices: 180 us -> 165 us
    all_to_all x0 -> x1, blocking collectives: none -> 31.2 us  [exchange(): lax.all_to_all(x, 'expert', split_axis=0, concat_axis=0, axis_index_group...]
    all_to_all x9 -> x8, waiting for transfers between devices: 22.1 us -> 15.1 us  [exchange(): lax.all_to_all(x, 'expert', split_axis=0, concat_axis=0, axis_index_group...]
    all_to_all x9 -> x8, starting transfers between devices: 40.6 us -> 37 us  [exchange(): lax.all_to_all(x, 'expert', split_axis=0, concat_axis=0, axis_index_group...]
  transfers between devices with their start and end apart: 78 -> 77, of which waited for: 26 -> 25; matrix products, arithmetic and copies ran while one was open for 6% -> 6% of each run, Pallas kernels for 45% -> 44%
where the time goes in v5:
time: 794 us; the launch traced here: 786 us
  Pallas kernels  349 us (44%)
  waiting for transfers between devices  165 us (21%)
  starting transfers between devices  133 us (17%)
  local copies, waits for them, and re-layouts  53.7 us (7%)
  blocking collectives  31.2 us (4%)
  other arithmetic  31 us (4%)
  between operations  15.8 us (2%)
    pallas_call x4, Pallas kernels, expert_pass(): pl.pallas_call(functools.partial(expert_kernel, block, chips, shards, pre...  162 us
    ppermute x12, waiting for transfers between devices, dp_along(): return lax.ppermute(x, 'dp', pairs)  74.9 us
    ppermute x12, starting transfers between devices, dp_along(): return lax.ppermute(x, 'dp', pairs)  51.4 us
    pallas_call x2, Pallas kernels, attend_back(): pl.pallas_call(functools.partial(attend_back_kernel, chunks), grid=(PAIRS...  50.9 us
    pallas_call x11, Pallas kernels, small_call(): pl.pallas_call(kernel, in_specs=in_specs or [NEAR] * len(inputs), out_spe...  44.1 us
    all_to_all x8, starting transfers between devices, exchange(): lax.all_to_all(x, 'expert', split_axis=0, concat_axis=0, axis_index_group...  37 us
    unnamed x190, local copies, waits for them, and re-layouts  35.6 us
    pallas_call x2, Pallas kernels, attend(): pl.pallas_call(functools.partial(attend_kernel, chunks), grid=(PAIRS,), i...  33.5 us
  transfers between devices with their start and end apart: 77, of which 25 were waited for; matrix products, arithmetic and copies ran while one was open for 6% of the time, Pallas kernels for 44%

profile of v5, /device:TPU:0, one launch (start us, length us, event | category | flops | bytes accessed | tf_op | source)
XLA Modules:
  0.0 786.0 jit_solution(2130765002282272315)
XLA Ops:
  41.4 6.9 all-to-all-start.1
  67.4 11.6 %all-to-all-done.1 = bf16[4,48,1536]{2,1,0:T(8,128)(2,1)} async-done(((bf16[4,48,1536]{2,1,0:T(8,128)(2,1)}), bf16[4,48,1536]{2,1,0:T(8,128)(2,1)}, u32[]{:S(2)}, u32[]{:S(2)}) %all-to-all-start.1) | async-done | bytes 589856 | tf_op jit(solution)/shard_map/all_to_all | solution.py:912
  81.4 31.2 %all_to_all.55 = bf16[4,4,48,1536]{3,2,1,0:T(8,128)(2,1)S(1)} all-to-all(bf16[4,4,48,1536]{3,2,1,0:T(8,128)(2,1)S(1)} %broadcast_in_dim.80), channel_id=1, replica_groups={{0,2,4,6},{1,3,5,7},{8,10,12,14},{9,11,13,15},{16,18,20,22},{17,19,21,2..., dimensions={0} | all-to-all | bytes 4718592 | tf_op jit(solution)/shard_map/all_to_all | solution.py:796
  112.7 4.7 all-to-all-start.3
  124.3 13.7 %project.1 = (bf16[256,1536]{1,0:T(8,128)(2,1)}, bf16[256,1536]{1,0:T(8,128)(2,1)}, bf16[256,1024]{1,0:T(8,128)(2,1)}, bf16[256,1024]{1,0:T(8,128)(2,1)}, f32[8,...) custom-call(s32[32]{0:T(128)S(1)} %stack.277.place_ref, bf16[256,1536]{1,0:T(8,128)(2,1)} %get-tuple-element.522.refs_0_.x_ref, ...), custom_call_target="tpu_custom_call" | custom-call | flops 1024 | bytes 1024 | tf_op jit(solution)/shard_map/project/pallas_call | solution.py:566
  138.1 6.8 collective-permute-start.16
  149.5 5.0 fusion.4.q_ref
  157.3 5.4 assemble.1.w_ref
  168.0 10.5 %collective-permute-done.18.refs_2_.refs_6_ = bf16[256,1024]{1,0:T(8,128)(2,1)} collective-permute-done((bf16[256,1024]{1,0:T(8,128)(2,1)}, bf16[256,1024]{1,0:T(8,128)(2,1)}, u32[]{:S(2)}, u32[]{:S(2)}) %collective-permute-start.18) | collective-permute-done | bytes 524320 | tf_op jit(solution)/shard_map/ppermute | solution.py:826
  178.5 4.7 all-to-all-start.4
  183.3 28.4 %collective-permute-start.20 = (bf16[256,1024]{1,0:T(8,128)(2,1)}, bf16[256,1024]{1,0:T(8,128)(2,1)S(1)}, u32[]{:S(2)}, u32[]{:S(2)}) collective-permute-start(bf16[256,1024]{1,0:T(8,128)(2,1)} %get-tuple-element.280.refs_3_.refs_7_), channel_id=1, source_target_pairs={{0,16},{8,24},{1,17},{9,25},{2,18},{10,26},{3,19},{11,27},{4,20},{... | collective-permute-start | bytes 1572872 | tf_op jit(solution)/shard_map/ppermute | solution.py:826
  211.7 16.8 %path_attention.2 = (bf16[256,1536]{1,0:T(8,128)(2,1)}, f32[4,8,256]{2,1,0:T(8,128)}) custom-call(bf16[256,1536]{1,0:T(8,128)(2,1)} %fusion.4.q_ref, bf16[256,1024]{1,0:T(8,128)(2,1)} %collective-permute-done.16.refs_0_.refs_4_, bf16[256,1024]{1,0:T(8,128)(2,1)} %collective-permute-done.17.refs_1_.refs_5_, ...), custom_call_target="tpu_custom_call" | custom-call | flops 25165824 | bytes 1048576 | tf_op jit(solution)/shard_map/path_attention/pallas_call | solution.py:106
  229.8 4.8 middle.2
  241.5 10.5 %collective-permute-done.22.refs_2_.refs_6_ = bf16[256,1024]{1,0:T(8,128)(2,1)S(1)} collective-permute-done((bf16[256,1024]{1,0:T(8,128)(2,1)}, bf16[256,1024]{1,0:T(8,128)(2,1)S(1)}, u32[]{:S(2)}, u32[]{:S(2)}) %collective-permute-start.22) | collective-permute-done | bytes 524320 | tf_op jit(solution)/shard_map/ppermute | solution.py:826
  252.0 9.9 %collective-permute-done.23.refs_0_.refs_4_ = bf16[256,1024]{1,0:T(8,128)(2,1)} collective-permute-done((bf16[256,1024]{1,0:T(8,128)(2,1)}, bf16[256,1024]{1,0:T(8,128)(2,1)}, u32[]{:S(2)}, u32[]{:S(2)}) %collective-permute-start.23) | collective-permute-done | bytes 524320 | tf_op jit(solution)/shard_map/ppermute | solution.py:826
  261.9 10.9 %collective-permute-done.25.refs_6_ = bf16[256,1536]{1,0:T(8,128)(2,1)} collective-permute-done((bf16[256,1536]{1,0:T(8,128)(2,1)}, bf16[256,1536]{1,0:T(8,128)(2,1)}, u32[]{:S(2)}, u32[]{:S(2)}) %collective-permute-start.25) | collective-permute-done | bytes 786464 | tf_op jit(solution)/shard_map/ppermute | solution.py:792
  274.1 16.7 %path_attention.3 = (bf16[256,1536]{1,0:T(8,128)(2,1)}, f32[4,8,256]{2,1,0:T(8,128)}) custom-call(bf16[256,1536]{1,0:T(8,128)(2,1)} %fusion.7.q_ref, bf16[256,1024]{1,0:T(8,128)(2,1)} %collective-permute-done.23.refs_0_.refs_4_, bf16[256,1024]{1,0:T(8,128)(2,1)} %copy-done.71, bf16[256,1024]{1,0:T(8,128)(2,1)} %copy-done.72, ...), custom_call_target="tpu_custom_call" | custom-call | flops 25165824 | bytes 1048576 | tf_op jit(solution)/shard_map/path_attention/pallas_call | solution.py:106
  292.0 4.9 middle.3
  301.6 39.2 %expert_pass.4 = (bf16[1024,1536]{1,0:T(8,128)(2,1)}, bf16[1024,1536]{1,0:T(8,128)(2,1)}, bf16[1024,1536]{1,0:T(8,128)(2,1)}, bf16[1024,1536]{1,0:T(8,128)(2,1)}...) custom-call(bf16[256,1536]{1,0:T(8,128)(2,1)} %collective-permute-done.27.refs_0_, ...), custom_call_target="tpu_custom_call" | custom-call | flops 1572864 | bytes 1572864 | tf_op jit(solution)/shard_map/expert_pass/pallas_call | solution.py:443
  346.6 41.0 %expert_pass.5 = (bf16[1024,1536]{1,0:T(8,128)(2,1)}, bf16[1024,1536]{1,0:T(8,128)(2,1)}, bf16[1024,1536]{1,0:T(8,128)(2,1)}, bf16[1024,1536]{1,0:T(8,128)(2,1)}...) custom-call(bf16[256,1536]{1,0:T(8,128)(2,1)} %collective-permute-done.35.refs_0_, bf16[256,1536]{1,0:T(8,128)(2,1)} %copy-done.75, ...), custom_call_target="tpu_custom_call" | custom-call | flops 1572864 | bytes 1572864 | tf_op jit(solution)/shard_map/expert_pass/pallas_call | solution.py:443
  387.8 40.7 %expert_pass.6 = (bf16[1024,1536]{1,0:T(8,128)(2,1)}, bf16[1024,1536]{1,0:T(8,128)(2,1)}, bf16[1024,1536]{1,0:T(8,128)(2,1)}, bf16[1024,1536]{1,0:T(8,128)(2,1)}...) custom-call(bf16[256,1536]{1,0:T(8,128)(2,1)} %collective-permute-do, ...), custom_call_target="tpu_custom_call", output_to_operand_aliasing={{0}: (13, {}), {1}: (14, {}), {2}: (15, {}), {3}: (16, {})} | custom-call | flops 1572864 | bytes 1572864 | tf_op jit(solution)/shard_map/expert_pass/pallas_call | solution.py:443
  428.7 5.7 collective-permute-done.39
  439.5 4.7 all-to-all-start.5
  444.3 41.1 %expert_pass.7 = (bf16[1024,1536]{1,0:T(8,128)(2,1)}, bf16[1024,1536]{1,0:T(8,128)(2,1)}, bf16[1024,1536]{1,0:T(8,128)(2,1)}, bf16[1024,1536]{1,0:T(8,128)(2,1)}...) custom-call(bf16[256,1536]{1,0:T(8,128)(2,1)} %collective-permute-do, ...), custom_call_target="tpu_custom_call", output_to_operand_aliasing={{0}: (13, {}), {1}: (14, {}), {2}: (15, {}), {3}: (16, {})} | custom-call | flops 1572864 | bytes 1572864 | tf_op jit(solution)/shard_map/expert_pass/pallas_call | solution.py:443
  486.5 5.7 middle_back.2
  495.6 5.0 sums.8
  500.6 4.9 all-to-all-start.6
  505.5 25.4 %path_attention_back.2 = (bf16[256,1536]{1,0:T(8,128)(2,1)}, bf16[2,256,512]{2,1,0:T(8,128)(2,1)}, bf16[2,256,512]{2,1,0:T(8,128)(2,1)}, bf16[2,256,512]{2,1,0:T(8,128)(2,1)}, bf16[2,256,512]{2,1,0:T(8,128)(2,1)}) custom-call(bf16[256,1536]{1,0:T(8,128)(2,1)} %fusion.4.q_ref, bf16[256,1536]{1,0:T(8,128)(2,1)} %copy-done.51, ...), custom_call_target="tpu_custom_call" | custom-call | flops 62914560 | bytes 1048576 | tf_op jit(solution)/shard_map/path_attention_back/pallas_call | solution.py:179
  536.1 6.5 all-to-all-done.6.got_ref
  543.9 4.6 all-to-all-start.7
  548.6 5.7 middle_back.3
  554.4 4.3 weight_grad.3
  563.8 25.6 %path_attention_back.3 = (bf16[256,1536]{1,0:T(8,128)(2,1)}, bf16[2,256,512]{2,1,0:T(8,128)(2,1)}, bf16[2,256,512]{2,1,0:T(8,128)(2,1)}, bf16[2,256,512]{2,1,0:T(8,128)(2,1)}, bf16[2,256,512]{2,1,0:T(8,128)(2,1)}) custom-call(bf16[256,1536]{1,0:T(8,128)(2,1)} %fusion.7.q_ref, bf16[256,1536]{1,0:T(8,128)(2,1)} %copy-done.50, ...), custom_call_target="tpu_custom_call" | custom-call | flops 62914560 | bytes 1048576 | tf_op jit(solution)/shard_map/path_attention_back/pallas_call | solution.py:179
  596.8 4.2 weight_grad.4
  602.5 5.2 sums.10
  612.3 8.9 %collective-permute-done.49 = bf16[2,256,512]{2,1,0:T(8,128)(2,1)} collective-permute-done((bf16[2,256,512]{2,1,0:T(8,128)(2,1)}, bf16[2,256,512]{2,1,0:T(8,128)(2,1)}, u32[]{:S(2)}, u32[]{:S(2)}) %collective-permute-start.49) | collective-permute-done | bytes 524320 | tf_op jit(solution)/shard_map/ppermute | solution.py:826
  621.2 4.5 all-to-all-start.8
  634.6 9.9 %collective-permute-done.47 = bf16[2,256,512]{2,1,0:T(8,128)(2,1)} collective-permute-done((bf16[2,256,512]{2,1,0:T(8,128)(2,1)}, bf16[2,256,512]{2,1,0:T(8,128)(2,1)}, u32[]{:S(2)}, u32[]{:S(2)}) %collective-permute-start.47) | collective-permute-done | bytes 524320 | tf_op jit(solution)/shard_map/ppermute | solution.py:826
  644.6 22.0 %collective-permute-done.46 = bf16[2,256,512]{2,1,0:T(8,128)(2,1)} collective-permute-done((bf16[2,256,512]{2,1,0:T(8,128)(2,1)}, bf16[2,256,512]{2,1,0:T(8,128)(2,1)}, u32[]{:S(2)}, u32[]{:S(2)}) %collective-permute-start.46) | collective-permute-done | bytes 524320 | tf_op jit(solution)/shard_map/ppermute | solution.py:826
  670.6 4.6 weight_grad.5
  692.8 16.2 %collective-permute-done.55 = bf16[48,1536]{1,0:T(8,128)(2,1)S(1)} collective-permute-done((bf16[48,1536]{1,0:T(8,128)(2,1)S(1)}, bf16[48,1536]{1,0:T(8,128)(2,1)S(1)}, u32[]{:S(2)}, u32[]{:S(2)}) %collective-permute-start.55) | collective-permute-done | bytes 147488 | tf_op jit(solution)/shard_map/ppermute | solution.py:821
  710.3 10.4 %collective-permute-done.57 = bf16[48,1536]{1,0:T(8,128)(2,1)} collective-permute-done((bf16[48,1536]{1,0:T(8,128)(2,1)S(1)}, bf16[48,1536]{1,0:T(8,128)(2,1)}, u32[]{:S(2)}, u32[]{:S(2)}) %collective-permute-start.57) | collective-permute-done | bytes 147488 | tf_op jit(solution)/shard_map/ppermute | solution.py:821
  720.7 8.2 %collective-permute-done.54.refs_4_ = bf16[4,48,1152]{2,1,0:T(8,128)(2,1)} collective-permute-done((bf16[4,48,1152]{2,1,0:T(8,128)(2,1)}, bf16[4,48,1152]{2,1,0:T(8,128)(2,1)}, u32[]{:S(2)}, u32[]{:S(2)}) %collective-permute-start.54) | collective-permute-done | bytes 442400 | tf_op jit(solution)/shard_map/ppermute | solution.py:792
  728.9 4.8 all-to-all-start.10
  740.0 4.3 collective-permute-start.60
  744.4 6.0 input_back.2
  750.4 6.0 input_back.3
  761.1 8.6 %all-to-all-done.10 = bf16[4,256,1536]{2,1,0:T(8,128)(2,1)} async-done(((bf16[4,256,1536]{2,1,0:T(8,128)(2,1)}), bf16[4,256,1536]{2,1,0:T(8,128)(2,1)}, u32[]{:S(2)}, u32[]{:S(2)}) %all-to-all-start.10) | async-done | bytes 3145760 | tf_op jit(solution)/shard_map/all_to_all | solution.py:796
  (405 shorter events, 182.6 us)
Async XLA Ops:
  8.9 23.1 %collective-permute-start = (bf16[48,2688]{1,0:T(8,128)(2,1)S(1)}, bf16[48,2688]{1,0:T(8,128)(2,1)S(1)}, u32[]{:S(2)}, u32[]{:S(2)}) collective-permute-start(bf16[48,2688]{1,0:T(8,128)(2,1)S(1)} %fusion.20), channel_id=1, source_target_pairs={{0,8},{8,0},{16,24},{24,16},{1,9},{9,1},{17,25},{25,17},{2,10},{10... | collective-permute-start | bytes 774152 | tf_op jit(solution)/shard_map/ppermute | solution.py:821
  12.0 21.1 %collective-permute-start.1 = (bf16[48,2688]{1,0:T(8,128)(2,1)S(1)}, bf16[48,2688]{1,0:T(8,128)(2,1)S(1)}, u32[]{:S(2)}, u32[]{:S(2)}) collective-permute-start(bf16[48,2688]{1,0:T(8,128)(2,1)S(1)} %fusion.20), channel_id=1, source_target_pairs={{0,16},{8,24},{16,0},{24,8},{1,17},{9,25},{17,1},{25,9},{2,18},{10... | collective-permute-start | bytes 774152 | tf_op jit(solution)/shard_map/ppermute | solution.py:821
  19.9 158.6 %all-gather.3.cloned.1.call-start = ((), (), s32[]{:S(2)}) async-start(), calls=%async_computation.15 | async-start | bytes 5898240 | tf_op jit(solution)/shard_map/all_gather | solution.py:868
  41.4 37.7 %all-to-all-start.1 = ((bf16[4,48,1536]{2,1,0:T(8,128)(2,1)}), bf16[4,48,1536]{2,1,0:T(8,128)(2,1)}, u32[]{:S(2)}, u32[]{:S(2)}) async-start(bf16[4,48,1536]{2,1,0:T(8,128)(2,1)} %broadcast_in_dim.70), calls=%async_computation.1 | async-start | bytes 1179648 | tf_op jit(solution)/shard_map/all_to_all | solution.py:912
  53.7 25.4 %collective-permute-start.6 = (bf16[2,48,2688]{2,1,0:T(8,128)(2,1)}, bf16[2,48,2688]{2,1,0:T(8,128)(2,1)S(1)}, u32[]{:S(2)}, u32[]{:S(2)}) collective-permute-start(bf16[2,48,2688]{2,1,0:T(8,128)(2,1)} %pad_maximum_fusion.3), channel_id=1, source_target_pairs={{0,4},{1,5},{2,6},{3,7},{4,0},{5,1},{6,2},{7,3},{8,12},{9,13},{10,... | collective-permute-start | bytes 1548296 | tf_op jit(solution)/shard_map/ppermute | solution.py:792
  55.2 23.8 %collective-permute-start.7 = (bf16[2,48,2688]{2,1,0:T(8,128)(2,1)S(1)}, bf16[2,48,2688]{2,1,0:T(8,128)(2,1)S(1)}, u32[]{:S(2)}, u32[]{:S(2)}) collective-permute-start(bf16[2,48,2688]{2,1,0:T(8,128)(2,1)S(1)} %collective-permute-done.3.refs_4_), channel_id=1, source_target_pairs={{0,4},{1,5},{2,6},{3,7},{4,0},{5,1},{6,2},{7,3},{8,12},{9,13},{10,... | collective-permute-start | bytes 1548296 | tf_op jit(solution)/shard_map/ppermute | solution.py:792
  55.8 23.3 %collective-permute-start.8 = (bf16[2,48,2688]{2,1,0:T(8,128)(2,1)}, bf16[2,48,2688]{2,1,0:T(8,128)(2,1)}, u32[]{:S(2)}, u32[]{:S(2)}) collective-permute-start(bf16[2,48,2688]{2,1,0:T(8,128)(2,1)} %pad_maximum_fusion.4), channel_id=1, source_target_pairs={{0,2},{1,3},{2,0},{3,1},{4,6},{5,7},{6,4},{7,5},{8,10},{9,11},{10,... | collective-permute-start | bytes 1548296 | tf_op jit(solution)/shard_map/ppermute | solution.py:792
  56.3 23.1 %collective-permute-start.9 = (bf16[2,48,2688]{2,1,0:T(8,128)(2,1)S(1)}, bf16[2,48,2688]{2,1,0:T(8,128)(2,1)}, u32[]{:S(2)}, u32[]{:S(2)}) collective-permute-start(bf16[2,48,2688]{2,1,0:T(8,128)(2,1)S(1)} %collective-permute-done.4.refs_7_), channel_id=1, source_target_pairs={{0,2},{1,3},{2,0},{3,1},{4,6},{5,7},{6,4},{7,5},{8,10},{9,11},{10,... | collective-permute-start | bytes 1548296 | tf_op jit(solution)/shard_map/ppermute | solution.py:792
  112.6 44.6 %collective-permute-start.19 = (bf16[4,4,48,1536]{3,2,1,0:T(8,128)(2,1)S(1)}, bf16[4,4,48,1536]{3,2,1,0:T(8,128)(2,1)}, u32[]{:S(2)}, u32[]{:S(2)}) collective-permute-start(bf16[4,4,48,1536]{3,2,1,0:T(8,128)(2,1)S(1)} %all_to_all.55), channel_id=1, source_target_pairs={{0,1},{1,0},{2,3},{3,2},{4,5},{5,4},{6,7},{7,6},{8,9},{9,8},{10,11... | collective-permute-start | bytes 7077896 | tf_op jit(solution)/shard_map/ppermute | solution.py:789
  112.7 65.8 %all-to-all-start.3 = ((bf16[4,256,1536]{2,1,0:T(8,128)(2,1)}), bf16[4,256,1536]{2,1,0:T(8,128)(2,1)}, u32[]{:S(2)}, u32[]{:S(2)}) async-start(bf16[4,256,1536]{2,1,0:T(8,128)(2,1)} %repeat.2), calls=%async_computation.3 | async-start | bytes 6291456 | tf_op jit(solution)/shard_map/all_to_all | solution.py:796
  138.1 26.7 %collective-permute-start.16 = (bf16[256,1024]{1,0:T(8,128)(2,1)}, bf16[256,1024]{1,0:T(8,128)(2,1)}, u32[]{:S(2)}, u32[]{:S(2)}) collective-permute-start(bf16[256,1024]{1,0:T(8,128)(2,1)} %get-tuple-element.265.refs_3_.refs_7_), channel_id=1, source_target_pairs={{0,24},{1,25},{2,26},{3,27},{4,28},{5,29},{6,30},{7,31}} | collective-permute-start | bytes 1572872 | tf_op jit(solution)/shard_map/ppermute | solution.py:826
  144.9 23.1 %collective-permute-start.17 = (bf16[256,1024]{1,0:T(8,128)(2,1)}, bf16[256,1024]{1,0:T(8,128)(2,1)}, u32[]{:S(2)}, u32[]{:S(2)}) collective-permute-start(bf16[256,1024]{1,0:T(8,128)(2,1)} %get-tuple-element.265.refs_3_.refs_7_), channel_id=1, source_target_pairs={{0,16},{8,24},{1,17},{9,25},{2,18},{10,26},{3,19},{11,27},{4,20},{... | collective-permute-start | bytes 1572872 | tf_op jit(solution)/shard_map/ppermute | solution.py:826
  147.0 31.5 %collective-permute-start.18 = (bf16[256,1024]{1,0:T(8,128)(2,1)}, bf16[256,1024]{1,0:T(8,128)(2,1)}, u32[]{:S(2)}, u32[]{:S(2)}) collective-permute-start(bf16[256,1024]{1,0:T(8,128)(2,1)} %get-tuple-element.265.refs_3_.refs_7_), channel_id=1, source_target_pairs={{0,8},{8,16},{16,24},{1,9},{9,17},{17,25},{2,10},{10,18},{18,26},{... | collective-permute-start | bytes 1572872 | tf_op jit(solution)/shard_map/ppermute | solution.py:826
  178.5 50.0 %collective-permute-start.21 = (bf16[4,256,1536]{2,1,0:T(8,128)(2,1)}, bf16[4,256,1536]{2,1,0:T(8,128)(2,1)}, u32[]{:S(2)}, u32[]{:S(2)}) collective-permute-start(bf16[4,256,1536]{2,1,0:T(8,128)(2,1)} %all-to-all-done.3.refs_9_), channel_id=1, source_target_pairs={{0,1},{1,0},{2,3},{3,2},{4,5},{5,4},{6,7},{7,6},{8,9},{9,8},{10,11... | collective-permute-start | bytes 9437192 | tf_op jit(solution)/shard_map/ppermute | solution.py:789
  178.5 63.0 %all-to-all-start.4 = ((bf16[4,256,1536]{2,1,0:T(8,128)(2,1)}), bf16[4,256,1536]{2,1,0:T(8,128)(2,1)}, u32[]{:S(2)}, u32[]{:S(2)}) async-start(bf16[4,256,1536]{2,1,0:T(8,128)(2,1)} %repeat.3), calls=%async_computation.4 | async-start | bytes 6291456 | tf_op jit(solution)/shard_map/all_to_all | solution.py:796
  183.2 204.5 %all-gather.5.cloned.1.call-start = ((), (), s32[]{:S(2)}) async-start(), calls=%async_computation.16 | async-start | bytes 5898240 | tf_op jit(solution)/shard_map/all_gather | solution.py:868
  183.3 45.2 %collective-permute-start.20 = (bf16[256,1024]{1,0:T(8,128)(2,1)}, bf16[256,1024]{1,0:T(8,128)(2,1)S(1)}, u32[]{:S(2)}, u32[]{:S(2)}) collective-permute-start(bf16[256,1024]{1,0:T(8,128)(2,1)} %get-tuple-element.280.refs_3_.refs_7_), channel_id=1, source_target_pairs={{0,16},{8,24},{1,17},{9,25},{2,18},{10,26},{3,19},{11,27},{4,20},{... | collective-permute-start | bytes 1572872 | tf_op jit(solution)/shard_map/ppermute | solution.py:826
  234.6 27.3 %collective-permute-start.24 = (bf16[256,1536]{1,0:T(8,128)(2,1)}, bf16[256,1536]{1,0:T(8,128)(2,1)}, u32[]{:S(2)}, u32[]{:S(2)}) collective-permute-start(bf16[256,1536]{1,0:T(8,128)(2,1)} %get-tuple-element.287.refs_4_), channel_id=1, source_target_pairs={{0,2},{1,3},{2,0},{3,1},{4,6},{5,7},{6,4},{7,5},{8,10},{9,11},{10,... | collective-permute-start | bytes 2359304 | tf_op jit(solution)/shard_map/ppermute | solution.py:792
  236.5 36.3 %collective-permute-start.25 = (bf16[256,1536]{1,0:T(8,128)(2,1)}, bf16[256,1536]{1,0:T(8,128)(2,1)}, u32[]{:S(2)}, u32[]{:S(2)}) collective-permute-start(bf16[256,1536]{1,0:T(8,128)(2,1)} %get-tuple-element.287.refs_4_), channel_id=1, source_target_pairs={{0,4},{1,5},{2,6},{3,7},{4,0},{5,1},{6,2},{7,3},{8,12},{9,13},{10,... | collective-permute-start | bytes 2359304 | tf_op jit(solution)/shard_map/ppermute | solution.py:792
  238.0 34.9 %collective-permute-start.26 = (bf16[256,1536]{1,0:T(8,128)(2,1)}, bf16[256,1536]{1,0:T(8,128)(2,1)}, u32[]{:S(2)}, u32[]{:S(2)}) collective-permute-start(bf16[256,1536]{1,0:T(8,128)(2,1)} %get-tuple-element.287.refs_4_), channel_id=1, source_target_pairs={{0,6},{1,7},{2,4},{3,5},{4,2},{5,3},{6,0},{7,1},{8,14},{9,15},{10,... | collective-permute-start | bytes 2359304 | tf_op jit(solution)/shard_map/ppermute | solution.py:792
  239.4 22.5 %collective-permute-start.23 = (bf16[256,1024]{1,0:T(8,128)(2,1)}, bf16[256,1024]{1,0:T(8,128)(2,1)}, u32[]{:S(2)}, u32[]{:S(2)}) collective-permute-start(bf16[256,1024]{1,0:T(8,128)(2,1)} %get-tuple-element.280.refs_3_.refs_7_), channel_id=1, source_target_pairs={{0,24},{1,25},{2,26},{3,27},{4,28},{5,29},{6,30},{7,31}} | collective-permute-start | bytes 1572872 | tf_op jit(solution)/shard_map/ppermute | solution.py:826
  272.9 263.2 %reduce-scatter.5.cloned.1.call-start = ((), (), s32[]{:S(2)}) async-start(), calls=%async_computation.17 | async-start | bytes 2949120 | tf_op jit(solution)/shard_map/reduce_scatter | solution.py:1010
  272.9 25.2 %collective-permute-start.31 = (bf16[4,256,1536]{2,1,0:T(8,128)(2,1)}, bf16[4,256,1536]{2,1,0:T(8,128)(2,1)}, u32[]{:S(2)}, u32[]{:S(2)}) collective-permute-start(bf16[4,256,1536]{2,1,0:T(8,128)(2,1)} %all-to-all-done.4.refs_9_), channel_id=1, source_target_pairs={{0,1},{1,0},{2,3},{3,2},{4,5},{5,4},{6,7},{7,6},{8,9},{9,8},{10,11... | collective-permute-start | bytes 9437192 | tf_op jit(solution)/shard_map/ppermute | solution.py:789
  298.1 42.8 %collective-permute-start.32 = (bf16[256,1536]{1,0:T(8,128)(2,1)}, bf16[256,1536]{1,0:T(8,128)(2,1)S(1)}, u32[]{:S(2)}, u32[]{:S(2)}) collective-permute-start(bf16[256,1536]{1,0:T(8,128)(2,1)} %get-tuple-element.317.refs_4_), channel_id=1, source_target_pairs={{0,2},{1,3},{2,0},{3,1},{4,6},{5,7},{6,4},{7,5},{8,10},{9,11},{10,... | collective-permute-start | bytes 2359304 | tf_op jit(solution)/shard_map/ppermute | solution.py:792
  299.3 41.6 %collective-permute-start.33 = (bf16[256,1536]{1,0:T(8,128)(2,1)}, bf16[256,1536]{1,0:T(8,128)(2,1)}, u32[]{:S(2)}, u32[]{:S(2)}) collective-permute-start(bf16[256,1536]{1,0:T(8,128)(2,1)} %get-tuple-element.317.refs_4_), channel_id=1, source_target_pairs={{0,4},{1,5},{2,6},{3,7},{4,0},{5,1},{6,2},{7,3},{8,12},{9,13},{10,... | collective-permute-start | bytes 2359304 | tf_op jit(solution)/shard_map/ppermute | solution.py:792
  300.1 40.8 %collective-permute-start.34 = (bf16[256,1536]{1,0:T(8,128)(2,1)}, bf16[256,1536]{1,0:T(8,128)(2,1)}, u32[]{:S(2)}, u32[]{:S(2)}) collective-permute-start(bf16[256,1536]{1,0:T(8,128)(2,1)} %get-tuple-element.317.refs_4_), channel_id=1, source_target_pairs={{0,6},{1,7},{2,4},{3,5},{4,2},{5,3},{6,0},{7,1},{8,14},{9,15},{10,... | collective-permute-start | bytes 2359304 | tf_op jit(solution)/shard_map/ppermute | solution.py:792
  301.6 39.3 %collective-permute-start.35 = (bf16[256,1536]{1,0:T(8,128)(2,1)}, bf16[256,1536]{1,0:T(8,128)(2,1)}, u32[]{:S(2)}, u32[]{:S(2)}) collective-permute-start(bf16[256,1536]{1,0:T(8,128)(2,1)} %get-tuple-element.317.refs_4_), channel_id=1, source_target_pairs={{0,1},{1,0},{2,3},{3,2},{4,5},{5,4},{6,7},{7,6},{8,9},{9,8},{10,11... | collective-permute-start | bytes 2359304 | tf_op jit(solution)/shard_map/ppermute | solution.py:789
  387.7 148.3 %reduce-scatter.7.cloned.1.call-start = ((), (), s32[]{:S(2)}) async-start(), calls=%async_computation.18 | async-start | bytes 2949120 | tf_op jit(solution)/shard_map/reduce_scatter | solution.py:1010
  439.4 46.0 %collective-permute-start.40 = (bf16[1024,1536]{1,0:T(8,128)(2,1)}, bf16[1024,1536]{1,0:T(8,128)(2,1)}, u32[]{:S(2)}, u32[]{:S(2)}) collective-permute-start(bf16[1024,1536]{1,0:T(8,128)(2,1)} %get-tuple-element.358), channel_id=1, source_target_pairs={{0,1},{1,0},{2,3},{3,2},{4,5},{5,4},{6,7},{7,6},{8,9},{9,8},{10,11... | collective-permute-start | bytes 9437192 | tf_op jit(solution)/shard_map/ppermute | solution.py:789
  439.5 45.8 %all-to-all-start.5 = ((bf16[4,256,1536]{2,1,0:T(8,128)(2,1)}), bf16[4,256,1536]{2,1,0:T(8,128)(2,1)}, u32[]{:S(2)}, u32[]{:S(2)}) async-start(bf16[4,256,1536]{2,1,0:T(8,128)(2,1)} %sums.7), calls=%async_computation.5 | async-start | bytes 6291456 | tf_op jit(solution)/shard_map/all_to_all | solution.py:796
  444.2 91.8 %reduce-scatter.9.cloned.1.call-start = ((), (), s32[]{:S(2)}) async-start(), calls=%async_computation.19 | async-start | bytes 2949120 | tf_op jit(solution)/shard_map/reduce_scatter | solution.py:1010
  495.2 47.3 %collective-permute-start.42 = (bf16[1024,1536]{1,0:T(8,128)(2,1)}, bf16[1024,1536]{1,0:T(8,128)(2,1)}, u32[]{:S(2)}, u32[]{:S(2)}) collective-permute-start(bf16[1024,1536]{1,0:T(8,128)(2,1)} %get-tuple-element.382), channel_id=1, source_target_pairs={{0,1},{1,0},{2,3},{3,2},{4,5},{5,4},{6,7},{7,6},{8,9},{9,8},{10,11... | collective-permute-start | bytes 9437192 | tf_op jit(solution)/shard_map/ppermute | solution.py:789
  500.6 41.9 %all-to-all-start.6 = ((bf16[4,256,1536]{2,1,0:T(8,128)(2,1)}), bf16[4,256,1536]{2,1,0:T(8,128)(2,1)}, u32[]{:S(2)}, u32[]{:S(2)}) async-start(bf16[4,256,1536]{2,1,0:T(8,128)(2,1)} %sums.8), calls=%async_computation.6 | async-start | bytes 6291456 | tf_op jit(solution)/shard_map/all_to_all | solution.py:796
  543.9 45.4 %all-to-all-start.7 = ((bf16[4,256,1536]{2,1,0:T(8,128)(2,1)}), bf16[4,256,1536]{2,1,0:T(8,128)(2,1)}, u32[]{:S(2)}, u32[]{:S(2)}) async-start(bf16[4,256,1536]{2,1,0:T(8,128)(2,1)} %copy-done.9), calls=%async_computation.10 | async-start | bytes 6291456 | tf_op jit(solution)/shard_map/all_to_all | solution.py:796
  560.1 29.2 %collective-permute-start.45 = (bf16[4,4,48,1536]{3,2,1,0:T(8,128)(2,1)}, bf16[4,4,48,1536]{3,2,1,0:T(8,128)(2,1)}, u32[]{:S(2)}, u32[]{:S(2)}) collective-permute-start(bf16[4,4,48,1536]{3,2,1,0:T(8,128)(2,1)} %get-tuple-element.406), channel_id=1, source_target_pairs={{0,1},{1,0},{2,3},{3,2},{4,5},{5,4},{6,7},{7,6},{8,9},{9,8},{10,11... | collective-permute-start | bytes 7077896 | tf_op jit(solution)/shard_map/ppermute | solution.py:789
  560.1 29.2 %collective-permute-start.44 = (bf16[2,256,512]{2,1,0:T(8,128)(2,1)}, bf16[2,256,512]{2,1,0:T(8,128)(2,1)}, u32[]{:S(2)}, u32[]{:S(2)}) collective-permute-start(bf16[2,256,512]{2,1,0:T(8,128)(2,1)} %get-tuple-element.401), channel_id=1, source_target_pairs={{16,0},{24,8},{17,1},{25,9},{18,2},{26,10},{19,3},{27,11},{20,4},{... | collective-permute-start | bytes 1572872 | tf_op jit(solution)/shard_map/ppermute | solution.py:826
  589.4 22.9 %collective-permute-start.48 = (bf16[2,256,512]{2,1,0:T(8,128)(2,1)}, bf16[2,256,512]{2,1,0:T(8,128)(2,1)}, u32[]{:S(2)}, u32[]{:S(2)}) collective-permute-start(bf16[2,256,512]{2,1,0:T(8,128)(2,1)} %get-tuple-element.413), channel_id=1, source_target_pairs={{8,0},{16,8},{24,16},{9,1},{17,9},{25,17},{10,2},{18,10},{26,18},{... | collective-permute-start | bytes 1572872 | tf_op jit(solution)/shard_map/ppermute | solution.py:826
  590.9 30.2 %collective-permute-start.49 = (bf16[2,256,512]{2,1,0:T(8,128)(2,1)}, bf16[2,256,512]{2,1,0:T(8,128)(2,1)}, u32[]{:S(2)}, u32[]{:S(2)}) collective-permute-start(bf16[2,256,512]{2,1,0:T(8,128)(2,1)} %get-tuple-element.414), channel_id=1, source_target_pairs={{24,0},{25,1},{26,2},{27,3},{28,4},{29,5},{30,6},{31,7}} | collective-permute-start | bytes 1572872 | tf_op jit(solution)/shard_map/ppermute | solution.py:826
  621.2 45.4 %all-to-all-start.8 = ((bf16[4,4,48,1536]{3,2,1,0:T(8,128)(2,1)}), bf16[4,4,48,1536]{3,2,1,0:T(8,128)(2,1)}, u32[]{:S(2)}, u32[]{:S(2)}) async-start(bf16[4,4,48,1536]{3,2,1,0:T(8,128)(2,1)} %copy-done.11), calls=%async_computation.11 | async-start | bytes 4718592 | tf_op jit(solution)/shard_map/all_to_all | solution.py:796
  625.7 103.2 %reduce-scatter.11.cloned.1.call-start = ((), (), s32[]{:S(2)}) async-start(), calls=%async_computation.20 | async-start | bytes 2949120 | tf_op jit(solution)/shard_map/reduce_scatter | solution.py:1010
  627.0 39.5 %collective-permute-start.46 = (bf16[2,256,512]{2,1,0:T(8,128)(2,1)}, bf16[2,256,512]{2,1,0:T(8,128)(2,1)}, u32[]{:S(2)}, u32[]{:S(2)}) collective-permute-start(bf16[2,256,512]{2,1,0:T(8,128)(2,1)} %get-tuple-element.411), channel_id=1, source_target_pairs={{16,0},{24,8},{17,1},{25,9},{18,2},{26,10},{19,3},{27,11},{20,4},{... | collective-permute-start | bytes 1572872 | tf_op jit(solution)/shard_map/ppermute | solution.py:826
  676.5 33.2 %all-to-all-start.9 = ((bf16[4,4,48,1536]{3,2,1,0:T(8,128)(2,1)}), bf16[4,4,48,1536]{3,2,1,0:T(8,128)(2,1)S(1)}, u32[]{:S(2)}, u32[]{:S(2)}) async-start(bf16[4,4,48,1536]{3,2,1,0:T(8,128)(2,1)} %copy-done.10), calls=%async_computation.12 | async-start | bytes 4718592 | tf_op jit(solution)/shard_map/all_to_all | solution.py:796
  686.3 34.4 %collective-permute-start.52 = (bf16[4,48,1152]{2,1,0:T(8,128)(2,1)}, bf16[4,48,1152]{2,1,0:T(8,128)(2,1)S(1)}, u32[]{:S(2)}, u32[]{:S(2)}) collective-permute-start(bf16[4,48,1152]{2,1,0:T(8,128)(2,1)} %get-tuple-element.516), channel_id=1, source_target_pairs={{0,2},{1,3},{2,0},{3,1},{4,6},{5,7},{6,4},{7,5},{8,10},{9,11},{10,... | collective-permute-start | bytes 1327112 | tf_op jit(solution)/shard_map/ppermute | solution.py:792
  688.3 32.4 %collective-permute-start.53 = (bf16[4,48,1152]{2,1,0:T(8,128)(2,1)}, bf16[4,48,1152]{2,1,0:T(8,128)(2,1)}, u32[]{:S(2)}, u32[]{:S(2)}) collective-permute-start(bf16[4,48,1152]{2,1,0:T(8,128)(2,1)} %get-tuple-element.515), channel_id=1, source_target_pairs={{0,4},{1,5},{2,6},{3,7},{4,0},{5,1},{6,2},{7,3},{8,12},{9,13},{10,... | collective-permute-start | bytes 1327112 | tf_op jit(solution)/shard_map/ppermute | solution.py:792
  689.8 39.2 %collective-permute-start.54 = (bf16[4,48,1152]{2,1,0:T(8,128)(2,1)}, bf16[4,48,1152]{2,1,0:T(8,128)(2,1)}, u32[]{:S(2)}, u32[]{:S(2)}) collective-permute-start(bf16[4,48,1152]{2,1,0:T(8,128)(2,1)} %get-tuple-element.514), channel_id=1, source_target_pairs={{0,6},{1,7},{2,4},{3,5},{4,2},{5,3},{6,0},{7,1},{8,14},{9,15},{10,... | collective-permute-start | bytes 1327112 | tf_op jit(solution)/shard_map/ppermute | solution.py:792
  728.9 40.8 %all-to-all-start.10 = ((bf16[4,256,1536]{2,1,0:T(8,128)(2,1)}), bf16[4,256,1536]{2,1,0:T(8,128)(2,1)}, u32[]{:S(2)}, u32[]{:S(2)}) async-start(bf16[4,256,1536]{2,1,0:T(8,128)(2,1)} %sums.10), calls=%async_computation.14 | async-start | bytes 6291456 | tf_op jit(solution)/shard_map/all_to_all | solution.py:796
  739.9 21.2 %collective-permute-start.59 = (bf16[48,2688]{1,0:T(8,128)(2,1)S(1)}, bf16[48,2688]{1,0:T(8,128)(2,1)S(1)}, u32[]{:S(2)}, u32[]{:S(2)}) collective-permute-start(bf16[48,2688]{1,0:T(8,128)(2,1)S(1)} %get-tuple-element.453), channel_id=1, source_target_pairs={{0,16},{8,24},{16,0},{24,8},{1,17},{9,25},{17,1},{25,9},{2,18},{10... | collective-permute-start | bytes 774152 | tf_op jit(solution)/shard_map/ppermute | solution.py:821
  740.0 21.1 %collective-permute-start.60 = (bf16[48,2688]{1,0:T(8,128)(2,1)S(1)}, bf16[48,2688]{1,0:T(8,128)(2,1)S(1)}, u32[]{:S(2)}, u32[]{:S(2)}) collective-permute-start(bf16[48,2688]{1,0:T(8,128)(2,1)S(1)} %get-tuple-element.454), channel_id=1, source_target_pairs={{0,24},{8,16},{16,8},{24,0},{1,25},{9,17},{17,9},{25,1},{2,26},{10... | collective-permute-start | bytes 774152 | tf_op jit(solution)/shard_map/ppermute | solution.py:821
  (122 other events, 1526.7 us)
Sparse Core Ops, SparseCore 0:
  34.2 105.2 all-gather.2
  273.0 86.6 all-gather.4
  387.8 45.2 reduce-scatter.4
  439.7 45.2 reduce-scatter.6
  487.1 47.5 reduce-scatter.8
  666.7 55.9 reduce-scatter.10
